TPU v7x, 512 devices: a whole 4x4x16 slice. The times are simulated.
512 devices in a mesh: dp: 64 (over z, x), expert: 8 (over y, core).
Axes of the slice: x: 4, y: 4, z: 16, core: 2. Of those that a mesh axis runs over, the one named last changes fastest.
Arguments:
- gradient: float32 [64, 768, 1024], P('expert', 'dp'), may hold values from -400 to 400
- momentum: float32 [64, 768, 1024], P('expert', 'dp'), may hold values from -100 to 100
Outputs:
- momentum_next: float32 [64, 768, 1024], P('expert', 'dp')
- update: bfloat16 [64, 768, 1024], P('expert', 'dp')
All inputs are finite; a program needn't handle non-finite values.
Results may differ from a plain program's by a relative error of at most 0.0063.
Values may be sent and summed in bfloat16 or wider, within the bound.
No kernel may reach another device: no remote copies, remote signals or barrier semaphores. Data moves between devices by JAX's collectives and lax.ppermute only.
A program may use at most 64 MiB of HBM per device.

v0:
```python
import math

import jax
import jax.numpy as jnp
from jax import lax
from jax.sharding import PartitionSpec as P

D = 1024
FF = 768
MATS = 8


MOMENTUM_RATE = 0.95
RMS_CAP = 0.5
NORM_EPS = 1e-07
COEF_A = 3.4445
COEF_B = -4.775
COEF_C = 2.0315


def clip_factor(total_square, groups):
    return jnp.minimum(1.0, RMS_CAP * math.sqrt(groups * MATS * FF * D) / jnp.sqrt(total_square))


def polynomial_of(iterate):
    gram_matrix = jnp.dot(iterate, iterate.T, preferred_element_type=jnp.float32).astype(
        jnp.bfloat16
    )
    squared = jnp.dot(gram_matrix, gram_matrix, preferred_element_type=jnp.float32)
    return (COEF_B * gram_matrix.astype(jnp.float32) + COEF_C * squared).astype(jnp.bfloat16)


def orthogonal_block(initial, column_start, block_width):
    iterate = initial
    polynomial = polynomial_of(iterate)
    combined = COEF_A * iterate.astype(jnp.float32) + jnp.dot(
        polynomial, iterate, preferred_element_type=jnp.float32
    )
    iterate = combined.astype(jnp.bfloat16)
    polynomial = polynomial_of(iterate)
    scale = 0.2 * math.sqrt(max(FF, D))
    combined = COEF_A * iterate.astype(jnp.float32) + jnp.dot(
        polynomial, iterate, preferred_element_type=jnp.float32
    )
    scaled = (scale * combined).astype(jnp.bfloat16)
    return lax.dynamic_slice_in_dim(scaled, column_start, block_width, 1)


def local(gradient, momentum):
    dp_count = lax.axis_size("dp")
    copies = dp_count // MATS
    shard_rows = gradient.shape[1]
    block_width = D // copies
    local_square = jnp.sum(gradient * gradient)
    total_square = lax.psum(local_square, ("dp", "expert"))
    factor = clip_factor(total_square, lax.axis_size("expert"))
    momentum_next = MOMENTUM_RATE * momentum + factor * gradient
    blended = factor * gradient + MOMENTUM_RATE * momentum_next
    norm_square = lax.psum(jnp.sum(blended * blended, axis=(1, 2)), "dp")
    initial = (blended / (jnp.sqrt(norm_square) + NORM_EPS)[:, None, None]).astype(jnp.bfloat16)
    outgoing = jnp.tile(initial, (copies, 1, 1))
    incoming = lax.all_to_all(outgoing, "dp", split_axis=0, concat_axis=0, tiled=True)
    whole = incoming.reshape(dp_count * shard_rows, D)
    column_start = lax.axis_index("dp") // MATS * block_width
    finished = orthogonal_block(whole, column_start, block_width)
    returning = finished.reshape(dp_count, shard_rows, block_width)
    arrived = lax.all_to_all(returning, "dp", split_axis=0, concat_axis=0, tiled=True)
    update = (
        arrived.reshape(copies, MATS, shard_rows, block_width)
        .transpose(1, 2, 0, 3)
        .reshape(MATS, shard_rows, D)
    )
    return (momentum_next, update)


def solution(mesh):
    in_specs = (P("expert", "dp", None), P("expert", "dp", None))
    out_specs = (P("expert", "dp", None), P("expert", "dp", None))
    return jax.shard_map(local, mesh=mesh, in_specs=in_specs, out_specs=out_specs, check_vma=False)
```

profile of v0, /device:TPU:6, one launch (start us, length us, event | category | flops | bytes accessed | tf_op | source)
XLA Modules:
  0.0 378.1 jit_solution(9604875106964299296)
XLA Ops:
  0.6 0.0 copy-start
  0.6 1.8 multiply_reduce_fusion.1
  2.4 108.3 %psum.14 = f32[]{:T(128)} all-reduce(f32[]{:T(128)} %multiply_reduce_fusion.1), channel_id=1, replica_groups=mesh['dp'=64,'expert'=8] {'dp','expert'}, use_global_device_ids=true, to_apply=%region_1.0 | all-reduce | flops 1 | bytes 8 | tf_op jit(solution)/shard_map/psum | solution.py:55
  111.4 1.3 multiply_reduce_fusion
  112.7 0.0 copy-start.2
  112.7 136.5 %psum.15 = f32[8]{0:T(128)S(1)} all-reduce(f32[8]{0:T(128)S(1)} %get-tuple-element.2), channel_id=1, replica_groups=mesh['dp'=64,'expert'=8] {'dp'}, use_global_device_ids=true, to_apply=%region_3.0 | all-reduce | flops 8 | bytes 64 | tf_op jit(solution)/shard_map/psum | solution.py:59
  249.3 0.0 copy-done
  249.3 0.1 divide_convert_fusion
  249.4 0.1 copy.5
  249.5 1.6 tile.4
  251.1 0.0 copy-done.2
  251.1 18.2 %all-to-all-start = ((bf16[64,12,1024]{2,1,0:T(8,128)(2,1)}), bf16[64,12,1024]{2,1,0:T(8,128)(2,1)S(1)}, u32[]{:S(2)}, u32[]{:S(2)}) async-start(bf16[64,12,1024]{2,1,0:T(8,128)(2,1)} %bitcast.17), calls=%async_computation | async-start | bytes 4194304 | tf_op jit(solution)/shard_map/all_to_all | solution.py:62
  269.3 67.2 %all-to-all-done = bf16[64,12,1024]{2,1,0:T(8,128)(2,1)S(1)} async-done(((bf16[64,12,1024]{2,1,0:T(8,128)(2,1)}), bf16[64,12,1024]{2,1,0:T(8,128)(2,1)S(1)}, u32[]{:S(2)}, u32[]{:S(2)}) %all-to-all-start) | async-done | bytes 1572896 | tf_op jit(solution)/shard_map/all_to_all | solution.py:62
  336.6 1.3 reshape.21
  337.9 0.0 copy-start.1
  337.9 4.5 %convolution_convert_fusion.1 = bf16[768,768]{1,0:T(8,128)(2,1)} fusion(bf16[768,1024]{1,0:T(8,128)(2,1)} %reshape.21), kind=kOutput, calls=%fused_computation.4 | convolution fusion | flops 1208549376 | bytes 2752512 | tf_op jit(solution)/shard_map/dot_general | solution.py:26
  342.4 0.0 copy-done.1
  342.4 4.5 %add_convert_fusion = bf16[768,1024]{1,0:T(8,128)(2,1)S(1)} fusion(bf16[768,1024]{1,0:T(8,128)(2,1)S(1)} %copy-done.1, bf16[768,768]{1,0:T(8,128)(2,1)} %convolution_convert_fusion.1), kind=kOutput, calls=%fused_computation | convolution fusion | flops 2120024064 | bytes 4325376 | tf_op jit(solution)/shard_map/dot_general | solution.py:36
  346.9 1.4 convolution_convert_fusion
  348.3 4.0 %fusion = f32[768,1024]{1,0:T(8,128)} fusion(bf16[768,1024]{1,0:T(8,128)(2,1)S(1)} %add_convert_fusion, bf16[768,768]{1,0:T(8,128)(2,1)S(1)} %convolution_convert_fusion), kind=kOutput, calls=%fused_computation.5 | convolution fusion | flops 2116878336 | bytes 5898240 | tf_op jit(solution)/shard_map/dot_general | solution.py:42
  352.3 1.1 fusion.2
  353.5 23.9 %all_to_all.10 = bf16[64,12,128]{2,1,0:T(8,128)(2,1)S(1)} all-to-all(bf16[64,12,128]{2,1,0:T(8,128)(2,1)S(1)} %reshape.22), channel_id=1, replica_groups=mesh['dp'=64,'expert'=8] {'dp'}, dimensions={0} | all-to-all | bytes 393216 | tf_op jit(solution)/shard_map/all_to_all | solution.py:67
  377.3 0.7 copy.8
  (2 shorter events, 0.1 us)
Async XLA Ops:
  0.6 248.6 %copy-start = (f32[8,12,1024]{2,0,1:T(8,128)S(1)}, f32[8,12,1024]{2,0,1:T(8,128)}, u32[]{:S(2)}) copy-start(f32[8,12,1024]{2,0,1:T(8,128)} %param.2) | copy-start | bytes 1179652
  112.7 138.4 %copy-start.2 = (f32[8,12,1024]{2,0,1:T(8,128)}, f32[8,12,1024]{2,0,1:T(8,128)S(1)}, u32[]{:S(2)}) copy-start(f32[8,12,1024]{2,0,1:T(8,128)S(1)} %get-tuple-element.3) | copy-start | bytes 1179652
  251.1 85.4 %all-to-all-start = ((bf16[64,12,1024]{2,1,0:T(8,128)(2,1)}), bf16[64,12,1024]{2,1,0:T(8,128)(2,1)S(1)}, u32[]{:S(2)}, u32[]{:S(2)}) async-start(bf16[64,12,1024]{2,1,0:T(8,128)(2,1)} %bitcast.17), calls=%async_computation | async-start | bytes 4194304 | tf_op jit(solution)/shard_map/all_to_all | solution.py:62
  337.9 4.5 %copy-start.1 = (bf16[768,1024]{1,0:T(8,128)(2,1)S(1)}, bf16[768,1024]{1,0:T(8,128)(2,1)}, u32[]{:S(2)}) copy-start(bf16[768,1024]{1,0:T(8,128)(2,1)} %reshape.21) | copy-start | bytes 4718596
where the time goes:
time: 379 us; the launch traced here: 378 us
  blocking collectives  269 us (71%)
  waiting for transfers between devices  67.2 us (18%)
  starting transfers between devices  18.2 us (5%)
  matrix products  14.4 us (4%)
  other arithmetic  4.29 us (1%)
  local copies, waits for them, and re-layouts  3.85 us (1%)
    psum x1, blocking collectives, local(): norm_square = lax.psum(jnp.sum(blended * blended, axis=(1, 2)), 'dp')  137 us
    psum x1, blocking collectives, local(): total_square = lax.psum(local_square, ('dp', 'expert'))  108 us
    all_to_all x1, waiting for transfers between devices, local(): lax.all_to_all(outgoing, 'dp', split_axis=0, concat_axis=0, tiled=True)  67.2 us
    all_to_all x1, blocking collectives, local(): lax.all_to_all(returning, 'dp', split_axis=0, concat_axis=0, tiled=True)  23.9 us
    all_to_all x1, starting transfers between devices, local(): lax.all_to_all(outgoing, 'dp', split_axis=0, concat_axis=0, tiled=True)  18.2 us
    dot_general x2, matrix products, orthogonal_block(): jnp.dot(polynomial, iterate, preferred_element_type=jnp.float32)  8.56 us
  transfers between devices with their start and end apart: 1, of which 1 were waited for; matrix products, arithmetic and copies ran while one was open for 0% of the time, Pallas kernels for 0%

commit v1 on v0

v1 whole, which is shorter than its diff:
```python
import math

import jax
import jax.numpy as jnp
from jax import lax
from jax.experimental import pallas as pl
from jax.experimental.pallas import tpu as pltpu
from jax.sharding import Mesh, PartitionSpec as P

D = 1024
FF = 768
MATS = 8
HALF = D // 2
TILE = 256
PLANES = ((0, 2, 4, 6, 9, 11, 13, 15), (1, 3, 5, 7, 8, 10, 12, 14))
SHIFTS = (2, 3, 1)


MOMENTUM_RATE = 0.95
RMS_CAP = 0.5
NORM_EPS = 1e-07
COEF_A = 3.4445
COEF_B = -4.775
COEF_C = 2.0315


def dot_f32(left, right):
    return jnp.dot(left, right, preferred_element_type=jnp.float32)


def dot_transposed(left, right):
    return lax.dot_general(left, right, (((1,), (1,)), ((), ())), preferred_element_type=jnp.float32)


def call(kernel, out_shape, *args, scratch=(), cost=None, space=pltpu.VMEM, limit=32768):
    return pl.pallas_call(
        kernel,
        out_shape=out_shape,
        in_specs=[pl.BlockSpec(memory_space=space)] * len(args),
        out_specs=jax.tree.map(lambda _: pl.BlockSpec(memory_space=pltpu.VMEM), out_shape),
        scratch_shapes=scratch,
        compiler_params=pltpu.CompilerParams(vmem_limit_bytes=limit * 1024),
        cost_estimate=cost,
    )(*args)


def start_kernel(gradient, momentum, sums, kept, decayed, arrivals):
    copies = [
        pltpu.make_async_copy(gradient, kept, arrivals.at[0]),
        pltpu.make_async_copy(momentum, decayed, arrivals.at[1]),
    ]
    for copy in copies:
        copy.start()
    copies[0].wait()
    value = kept[...]
    sums[...] = jnp.broadcast_to(jnp.sum(value * value), sums.shape)
    copies[1].wait()
    decayed[...] = MOMENTUM_RATE * decayed[...]


def add_kernel(parts, out):
    out[...] = jnp.broadcast_to(jnp.sum(parts[...], axis=0, keepdims=True), out.shape)


def blend_kernel(total, gradient, decayed, momentum_next, outgoing):
    total_square = jnp.sum(total[...], axis=0)[:, :1]
    factor = jnp.minimum(1.0, RMS_CAP * math.sqrt(MATS * MATS * FF * D) / jnp.sqrt(total_square))
    scaled = factor[None] * gradient[...]
    following = decayed[...] + scaled
    momentum_next[...] = following
    blended = jnp.swapaxes(scaled + MOMENTUM_RATE * following, 0, 1)
    left, right = blended[:, :, :HALF], blended[:, :, HALF:]
    packed = jnp.concatenate([left[:, :8], right[:, :8], left[:, 8:], right[:, 8:]], axis=1)
    outgoing[...] = packed.astype(jnp.bfloat16)


def unpacked(value):
    left, right = [], []
    for number in range(0, MATS, 2):
        first, second = value[number], value[number + 1]
        left += [first[:8], second[:8], first[16:20], second[16:20]]
        right += [first[8:16], second[8:16], first[20:], second[20:]]
    return jnp.concatenate(left, axis=0), jnp.concatenate(right, axis=0)


def packed_blocks(left, right):
    blocks = []
    for start in range(0, left.shape[0], 24):
        for place in range(2):
            head, tail = start + 8 * place, start + 16 + 4 * place
            blocks.append(
                jnp.concatenate(
                    [left[head : head + 8], right[head : head + 8], left[tail : tail + 4], right[tail : tail + 4]],
                    axis=0,
                )
            )
    return blocks


def orthogonal_kernel(*refs):
    pieces, (out, whole, product, gram, poly, second) = refs[:MATS], refs[MATS:]
    rows = FF // MATS
    tiles = [slice(start, start + TILE) for start in range(0, FF, TILE)]
    for number, piece in enumerate(pieces):
        left, right = unpacked(piece[...].astype(jnp.float32))
        place = slice(number * rows, (number + 1) * rows)
        whole[place, :HALF] = left.astype(jnp.bfloat16)
        whole[place, HALF:] = right.astype(jnp.bfloat16)
    on_diagonal = lax.broadcasted_iota(jnp.int32, (TILE, TILE), 0) == lax.broadcasted_iota(
        jnp.int32, (TILE, TILE), 1
    )
    norm_square = jnp.float32(0.0)
    for tile in tiles:
        product[tile, :] = dot_transposed(whole[tile, :], whole[...])
        norm_square += jnp.sum(jnp.where(on_diagonal, product[tile, tile], 0.0))
    inverse = 1.0 / (jnp.sqrt(jnp.full((1, 1), norm_square, jnp.float32)) + NORM_EPS)
    for tile in tiles:
        gram[tile, :] = (product[tile, :] * (inverse * inverse)).astype(jnp.bfloat16)
    for tile in tiles:
        squared = dot_f32(gram[tile, :], gram[...])
        poly[tile, :] = (COEF_B * gram[tile, :].astype(jnp.float32) + COEF_C * squared).astype(
            jnp.bfloat16
        )
    for tile in tiles:
        combined = COEF_A * whole[tile, :].astype(jnp.float32) + dot_f32(poly[tile, :], whole[...])
        second[tile, :] = (inverse * combined).astype(jnp.bfloat16)
    for tile in tiles:
        gram[tile, :] = dot_transposed(second[tile, :], second[...]).astype(jnp.bfloat16)
    own = gram[:rows, :]
    own_poly = (COEF_B * own.astype(jnp.float32) + COEF_C * dot_f32(own, gram[...])).astype(
        jnp.bfloat16
    )
    combined = COEF_A * second[:rows, :].astype(jnp.float32) + dot_f32(own_poly, second[...])
    scaled = 0.2 * math.sqrt(max(FF, D)) * combined
    for number, block in enumerate(packed_blocks(scaled[:, :HALF], scaled[:, HALF:])):
        out[number] = block.astype(jnp.bfloat16)


def spread_kernel(arrived, out):
    value = arrived[...].astype(jnp.float32)
    left = jnp.concatenate([value[:, :8], value[:, 16:20]], axis=1)
    right = jnp.concatenate([value[:, 8:16], value[:, 20:]], axis=1)
    out[:, :, :HALF] = jnp.swapaxes(left, 0, 1).astype(jnp.bfloat16)
    out[:, :, HALF:] = jnp.swapaxes(right, 0, 1).astype(jnp.bfloat16)


def orthogonal_rows(pieces):
    return call(
        orthogonal_kernel,
        jax.ShapeDtypeStruct(pieces[0].shape, jnp.bfloat16),
        *pieces,
        scratch=[
            pltpu.VMEM((FF, D), jnp.bfloat16),
            pltpu.VMEM((FF, FF), jnp.float32),
            pltpu.VMEM((FF, FF), jnp.bfloat16),
            pltpu.VMEM((FF, FF), jnp.bfloat16),
            pltpu.VMEM((FF, D), jnp.bfloat16),
        ],
        cost=pl.CostEstimate(
            flops=2 * FF * (3 * FF * D + FF * FF), bytes_accessed=2 * FF * D, transcendentals=0
        ),
    )


def exchanged(value, axes, groups=None):
    return lax.all_to_all(value, axes, split_axis=0, concat_axis=0, tiled=True, axis_index_groups=groups)


def gathered(piece):
    def across(value):
        return lax.ppermute(value, "z", [(plane, plane ^ 1) for plane in range(16)])

    pieces = [piece]
    for shift in SHIFTS:
        near = lax.ppermute(piece, "x", [(place, (place + shift) % 4) for place in range(4)])
        pieces += [near, across(near)]
    return pieces + [across(piece)]


def local(gradient, momentum):
    shape = (gradient.shape[1], MATS, D)
    gradient, momentum = jnp.swapaxes(gradient, 0, 1), jnp.swapaxes(momentum, 0, 1)
    whole = jax.ShapeDtypeStruct(shape, jnp.float32)
    squares, kept, decayed = call(
        start_kernel,
        (jax.ShapeDtypeStruct((32, 1, 128), jnp.float32), whole, whole),
        gradient,
        momentum,
        scratch=[pltpu.SemaphoreType.DMA((2,))],
        space=pl.ANY,
        limit=54272,
    )
    squares = exchanged(squares, ("x", "y", "core"))
    squares = call(add_kernel, jax.ShapeDtypeStruct((16, 1, 128), jnp.float32), squares)
    squares = exchanged(squares, "z")
    momentum_next, outgoing = call(
        blend_kernel,
        (
            whole,
            jax.ShapeDtypeStruct((MATS, 24, HALF), jnp.bfloat16),
        ),
        squares,
        kept,
        decayed,
    )
    piece = exchanged(outgoing, "z", PLANES)
    returning = orthogonal_rows(gathered(piece))
    arrived = exchanged(returning, "z", PLANES)
    update = call(spread_kernel, jax.ShapeDtypeStruct(shape, jnp.bfloat16), arrived)
    return (jnp.swapaxes(momentum_next, 0, 1), jnp.swapaxes(update, 0, 1))


def solution(mesh):
    split = Mesh(mesh.devices.reshape(16, 4, 4, 2), ("z", "x", "y", "core"))
    spec = P(("y", "core"), ("z", "x"), None)
    return jax.shard_map(local, mesh=split, in_specs=(spec, spec), out_specs=(spec, spec), check_vma=False)
```

time: 379 us -> 119 us (0.31)
  blocking collectives: 269 us -> 79.4 us
  waiting for transfers between devices: 67.2 us -> 6.37 us
  matrix products: 14.4 us -> 0 us
  Pallas kernels: 0 us -> 8.85 us
  other arithmetic: 4.29 us -> 0 us
  local copies, waits for them, and re-layouts: 3.85 us -> 0 us
    psum x2 -> x0, blocking collectives: 245 us -> none  [the longest x1 137 us: local(): norm_square = lax.psum(jnp.sum(blended * blended, axis=(1, 2)), 'dp')]
    all_to_all x1 -> x0, waiting for transfers between devices: 67.2 us -> none  [local(): lax.all_to_all(outgoing, 'dp', split_axis=0, concat_axis=0, tiled=True)]
    all_to_all x1 -> x4, blocking collectives: 23.9 us -> 79.4 us  [exchanged(): lax.all_to_all(value, axes, split_axis=0, concat_axis=0, tiled=True, axis...]
    ppermute x0 -> x7, starting transfers between devices: none -> 21.5 us  [the longest x4 11.7 us: across(): return lax.ppermute(value, 'z', [(plane, plane ^ 1) for plane in range(16)])]
    all_to_all x1 -> x0, starting transfers between devices: 18.2 us -> none  [local(): lax.all_to_all(outgoing, 'dp', split_axis=0, concat_axis=0, tiled=True)]
    dot_general x4 -> x0, matrix products: 14.4 us -> none  [the longest x2 8.56 us: orthogonal_block(): jnp.dot(polynomial, iterate, preferred_element_type=jnp.float32)]
    pallas_call x0 -> x5, Pallas kernels: none -> 8.85 us  [call(): pl.pallas_call(kernel, out_shape=out_shape, in_specs=[pl.BlockSpec(memory...]
    ppermute x0 -> x7, waiting for transfers between devices: none -> 6.37 us  [the longest x4 6.29 us: across(): return lax.ppermute(value, 'z', [(plane, plane ^ 1) for plane in range(16)])]
  transfers between devices with their start and end apart: 1 -> 7, of which waited for: 1 -> 4; matrix products, arithmetic and copies ran while one was open for 0% -> 0% of each run, Pallas kernels for 0% -> 0%
where the time goes in v1:
time: 119 us; the launch traced here: 117 us
  blocking collectives  79.4 us (67%)
  starting transfers between devices  21.5 us (18%)
  Pallas kernels  8.85 us (7%)
  waiting for transfers between devices  6.37 us (5%)
    all_to_all x4, blocking collectives, exchanged(): lax.all_to_all(value, axes, split_axis=0, concat_axis=0, tiled=True, axis...  79.4 us
    ppermute x4, starting transfers between devices, across(): return lax.ppermute(value, 'z', [(plane, plane ^ 1) for plane in range(16)])  11.7 us
    ppermute x3, starting transfers between devices, gathered(): lax.ppermute(piece, 'x', [(place, (place + shift) % 4) for place in range...  9.87 us
    pallas_call x5, Pallas kernels, call(): pl.pallas_call(kernel, out_shape=out_shape, in_specs=[pl.BlockSpec(memory...  8.85 us
    ppermute x4, waiting for transfers between devices, across(): return lax.ppermute(value, 'z', [(plane, plane ^ 1) for plane in range(16)])  6.29 us
  transfers between devices with their start and end apart: 7, of which 4 were waited for; matrix products, arithmetic and copies ran while one was open for 0% of the time, Pallas kernels for 0%

profile of v1, /device:TPU:6, one launch (start us, length us, event | category | flops | bytes accessed | tf_op | source)
XLA Modules:
  0.0 116.9 jit_solution(12181928739515879084)
XLA Ops:
  0.6 1.3 %shard_map.41 = (f32[32,1,128]{2,1,0:T(1,128)S(1)}, f32[12,8,1024]{2,1,0:T(8,128)S(1)}, f32[12,8,1024]{2,1,0:T(8,128)S(1)}) custom-call(f32[12,8,1024]{2,1,0:T(8,128)} %bitcast.4, f32[12,8,1024]{2,1,0:T(8,128)} %bitcast.5), custom_call_target="tpu_custom_call" | custom-call | tf_op jit(solution)/shard_map/pallas_call | solution.py:36
  1.9 14.1 %all_to_all.20.parts = f32[32,1,128]{2,1,0:T(1,128)S(1)} all-to-all(f32[32,1,128]{2,1,0:T(1,128)S(1)} %get-tuple-element.7), channel_id=1, replica_groups=mesh['z'=16,'x'=4,'y'=4,'core'=2] {'x','y','core'}, dimensions={0} | all-to-all | bytes 32768 | tf_op jit(solution)/shard_map/all_to_all | solution.py:166
  16.0 26.3 %all_to_all.21.total = f32[16,1,128]{2,1,0:T(1,128)S(1)} all-to-all(f32[16,1,128]{2,1,0:T(1,128)S(1)} %shard_map.42), channel_id=1, replica_groups=mesh['z'=16,'x'=4,'y'=4,'core'=2] {'z'}, dimensions={0} | all-to-all | bytes 16384 | tf_op jit(solution)/shard_map/all_to_all | solution.py:166
  42.3 0.9 shard_map.43
  43.1 19.6 %all_to_all.22.refs_0_ = bf16[8,24,512]{2,1,0:T(8,128)(2,1)S(1)} all-to-all(bf16[8,24,512]{2,1,0:T(8,128)(2,1)S(1)} %get-tuple-element.11), channel_id=1, replica_groups={{0,64,128,192,288,352,416,480},{32,96,160,224,256,320,384,448},{1,65,12..., dimensions={0} | all-to-all | bytes 393216 | tf_op jit(solution)/shard_map/all_to_all | solution.py:166
  62.7 4.0 %collective-permute-start.4 = (bf16[8,24,512]{2,1,0:T(8,128)(2,1)S(1)}, bf16[8,24,512]{2,1,0:T(8,128)(2,1)S(1)}, u32[]{:S(2)}, u32[]{:S(2)}) collective-permute-start(bf16[8,24,512]{2,1,0:T(8,128)(2,1)S(1)} %all_to_all.22.refs_0_), channel_id=1, source_target_pairs={{0,8},{8,16},{16,24},{24,0},{1,9},{9,17},{17,25},{25,1},{2,10},{10... | collective-permute-start | bytes 589832 | tf_op jit(solution)/shard_map/ppermute | solution.py:175
  66.7 1.9 %collective-permute-start.2 = (bf16[8,24,512]{2,1,0:T(8,128)(2,1)S(1)}, bf16[8,24,512]{2,1,0:T(8,128)(2,1)S(1)}, u32[]{:S(2)}, u32[]{:S(2)}) collective-permute-start(bf16[8,24,512]{2,1,0:T(8,128)(2,1)S(1)} %all_to_all.22.refs_0_), channel_id=1, source_target_pairs={{0,24},{8,0},{16,8},{24,16},{1,25},{9,1},{17,9},{25,17},{2,26},{10... | collective-permute-start | bytes 589832 | tf_op jit(solution)/shard_map/ppermute | solution.py:175
  68.7 4.0 %collective-permute-start = (bf16[8,24,512]{2,1,0:T(8,128)(2,1)S(1)}, bf16[8,24,512]{2,1,0:T(8,128)(2,1)S(1)}, u32[]{:S(2)}, u32[]{:S(2)}) collective-permute-start(bf16[8,24,512]{2,1,0:T(8,128)(2,1)S(1)} %all_to_all.22.refs_0_), channel_id=1, source_target_pairs={{0,16},{8,24},{16,0},{24,8},{1,17},{9,25},{17,1},{25,9},{2,18},{10... | collective-permute-start | bytes 589832 | tf_op jit(solution)/shard_map/ppermute | solution.py:175
  72.6 1.9 %collective-permute-start.6 = (bf16[8,24,512]{2,1,0:T(8,128)(2,1)S(1)}, bf16[8,24,512]{2,1,0:T(8,128)(2,1)S(1)}, u32[]{:S(2)}, u32[]{:S(2)}) collective-permute-start(bf16[8,24,512]{2,1,0:T(8,128)(2,1)S(1)} %all_to_all.22.refs_0_), channel_id=1, source_target_pairs={{0,32},{32,0},{64,96},{96,64},{128,160},{160,128},{192,224},{224,1... | collective-permute-start | bytes 589832 | tf_op jit(solution)/shard_map/ppermute | solution.py:171
  74.6 0.0 collective-permute-done.4.refs_5_
  74.6 3.9 %collective-permute-start.5 = (bf16[8,24,512]{2,1,0:T(8,128)(2,1)S(1)}, bf16[8,24,512]{2,1,0:T(8,128)(2,1)S(1)}, u32[]{:S(2)}, u32[]{:S(2)}) collective-permute-start(bf16[8,24,512]{2,1,0:T(8,128)(2,1)S(1)} %collective-permute-done.4.refs_5_), channel_id=1, source_target_pairs={{0,32},{32,0},{64,96},{96,64},{128,160},{160,128},{192,224},{224,1... | collective-permute-start | bytes 589832 | tf_op jit(solution)/shard_map/ppermute | solution.py:171
  78.5 0.1 collective-permute-done.2.refs_3_
  78.6 1.9 %collective-permute-start.3 = (bf16[8,24,512]{2,1,0:T(8,128)(2,1)S(1)}, bf16[8,24,512]{2,1,0:T(8,128)(2,1)S(1)}, u32[]{:S(2)}, u32[]{:S(2)}) collective-permute-start(bf16[8,24,512]{2,1,0:T(8,128)(2,1)S(1)} %collective-permute-done.2.refs_3_), channel_id=1, source_target_pairs={{0,32},{32,0},{64,96},{96,64},{128,160},{160,128},{192,224},{224,1... | collective-permute-start | bytes 589832 | tf_op jit(solution)/shard_map/ppermute | solution.py:171
  80.5 0.0 collective-permute-done.refs_1_
  80.5 3.9 %collective-permute-start.1 = (bf16[8,24,512]{2,1,0:T(8,128)(2,1)S(1)}, bf16[8,24,512]{2,1,0:T(8,128)(2,1)S(1)}, u32[]{:S(2)}, u32[]{:S(2)}) collective-permute-start(bf16[8,24,512]{2,1,0:T(8,128)(2,1)S(1)} %collective-permute-done.refs_1_), channel_id=1, source_target_pairs={{0,32},{32,0},{64,96},{96,64},{128,160},{160,128},{192,224},{224,1... | collective-permute-start | bytes 589832 | tf_op jit(solution)/shard_map/ppermute | solution.py:171
  84.4 0.0 collective-permute-done.6.refs_7_
  84.4 1.3 %collective-permute-done.5.refs_6_ = bf16[8,24,512]{2,1,0:T(8,128)(2,1)S(1)} collective-permute-done((bf16[8,24,512]{2,1,0:T(8,128)(2,1)S(1)}, bf16[8,24,512]{2,1,0:T(8,128)(2,1)S(1)}, u32[]{:S(2)}, u32[]{:S(2)}) %collective-permute-start.5) | collective-permute-done | bytes 196640 | tf_op jit(solution)/shard_map/ppermute | solution.py:171
  85.8 2.9 %collective-permute-done.3.refs_4_ = bf16[8,24,512]{2,1,0:T(8,128)(2,1)S(1)} collective-permute-done((bf16[8,24,512]{2,1,0:T(8,128)(2,1)S(1)}, bf16[8,24,512]{2,1,0:T(8,128)(2,1)S(1)}, u32[]{:S(2)}, u32[]{:S(2)}) %collective-permute-start.3) | collective-permute-done | bytes 196640 | tf_op jit(solution)/shard_map/ppermute | solution.py:171
  88.6 2.1 %collective-permute-done.1.refs_2_ = bf16[8,24,512]{2,1,0:T(8,128)(2,1)S(1)} collective-permute-done((bf16[8,24,512]{2,1,0:T(8,128)(2,1)S(1)}, bf16[8,24,512]{2,1,0:T(8,128)(2,1)S(1)}, u32[]{:S(2)}, u32[]{:S(2)}) %collective-permute-start.1) | collective-permute-done | bytes 196640 | tf_op jit(solution)/shard_map/ppermute | solution.py:171
  90.7 5.9 %shard_map.44 = bf16[8,24,512]{2,1,0:T(8,128)(2,1)S(1)} custom-call(bf16[8,24,512]{2,1,0:T(8,128)(2,1)S(1)} %all_to_all.22.refs_0_, bf16[8,24,512]{2,1,0:T(8,128)(2,1)S(1)} %collective-permute-done.refs_1_, bf16[8,24,512]{2,1,0:T(8,128)(2,1)S(1)} %collective-permute-done.1.refs_2_, bf16[8,24,512]{2,1,0:T(8,128)(2,1)S(1)} %collective-permute-done.2.refs_3_, ...), custom_call_target="tpu_custom_call" | custom-call | flops 4529848320 | bytes 1572864 | tf_op jit(solution)/shard_map/pallas_call | solution.py:36
  96.6 19.5 %all_to_all.23.arrived = bf16[8,24,512]{2,1,0:T(8,128)(2,1)S(1)} all-to-all(bf16[8,24,512]{2,1,0:T(8,128)(2,1)S(1)} %shard_map.44), channel_id=1, replica_groups={{0,64,128,192,288,352,416,480},{32,96,160,224,256,320,384,448},{1,65,12..., dimensions={0} | all-to-all | bytes 393216 | tf_op jit(solution)/shard_map/all_to_all | solution.py:166
  116.1 0.8 shard_map.45
  (1 shorter events, 0.0 us)
Async XLA Ops:
  62.7 11.8 %collective-permute-start.4 = (bf16[8,24,512]{2,1,0:T(8,128)(2,1)S(1)}, bf16[8,24,512]{2,1,0:T(8,128)(2,1)S(1)}, u32[]{:S(2)}, u32[]{:S(2)}) collective-permute-start(bf16[8,24,512]{2,1,0:T(8,128)(2,1)S(1)} %all_to_all.22.refs_0_), channel_id=1, source_target_pairs={{0,8},{8,16},{16,24},{24,0},{1,9},{9,17},{17,25},{25,1},{2,10},{10... | collective-permute-start | bytes 589832 | tf_op jit(solution)/shard_map/ppermute | solution.py:175
  66.7 11.8 %collective-permute-start.2 = (bf16[8,24,512]{2,1,0:T(8,128)(2,1)S(1)}, bf16[8,24,512]{2,1,0:T(8,128)(2,1)S(1)}, u32[]{:S(2)}, u32[]{:S(2)}) collective-permute-start(bf16[8,24,512]{2,1,0:T(8,128)(2,1)S(1)} %all_to_all.22.refs_0_), channel_id=1, source_target_pairs={{0,24},{8,0},{16,8},{24,16},{1,25},{9,1},{17,9},{25,17},{2,26},{10... | collective-permute-start | bytes 589832 | tf_op jit(solution)/shard_map/ppermute | solution.py:175
  68.7 11.8 %collective-permute-start = (bf16[8,24,512]{2,1,0:T(8,128)(2,1)S(1)}, bf16[8,24,512]{2,1,0:T(8,128)(2,1)S(1)}, u32[]{:S(2)}, u32[]{:S(2)}) collective-permute-start(bf16[8,24,512]{2,1,0:T(8,128)(2,1)S(1)} %all_to_all.22.refs_0_), channel_id=1, source_target_pairs={{0,16},{8,24},{16,0},{24,8},{1,17},{9,25},{17,1},{25,9},{2,18},{10... | collective-permute-start | bytes 589832 | tf_op jit(solution)/shard_map/ppermute | solution.py:175
  72.6 11.8 %collective-permute-start.6 = (bf16[8,24,512]{2,1,0:T(8,128)(2,1)S(1)}, bf16[8,24,512]{2,1,0:T(8,128)(2,1)S(1)}, u32[]{:S(2)}, u32[]{:S(2)}) collective-permute-start(bf16[8,24,512]{2,1,0:T(8,128)(2,1)S(1)} %all_to_all.22.refs_0_), channel_id=1, source_target_pairs={{0,32},{32,0},{64,96},{96,64},{128,160},{160,128},{192,224},{224,1... | collective-permute-start | bytes 589832 | tf_op jit(solution)/shard_map/ppermute | solution.py:171
  74.6 11.2 %collective-permute-start.5 = (bf16[8,24,512]{2,1,0:T(8,128)(2,1)S(1)}, bf16[8,24,512]{2,1,0:T(8,128)(2,1)S(1)}, u32[]{:S(2)}, u32[]{:S(2)}) collective-permute-start(bf16[8,24,512]{2,1,0:T(8,128)(2,1)S(1)} %collective-permute-done.4.refs_5_), channel_id=1, source_target_pairs={{0,32},{32,0},{64,96},{96,64},{128,160},{160,128},{192,224},{224,1... | collective-permute-start | bytes 589832 | tf_op jit(solution)/shard_map/ppermute | solution.py:171
  78.6 10.1 %collective-permute-start.3 = (bf16[8,24,512]{2,1,0:T(8,128)(2,1)S(1)}, bf16[8,24,512]{2,1,0:T(8,128)(2,1)S(1)}, u32[]{:S(2)}, u32[]{:S(2)}) collective-permute-start(bf16[8,24,512]{2,1,0:T(8,128)(2,1)S(1)} %collective-permute-done.2.refs_3_), channel_id=1, source_target_pairs={{0,32},{32,0},{64,96},{96,64},{128,160},{160,128},{192,224},{224,1... | collective-permute-start | bytes 589832 | tf_op jit(solution)/shard_map/ppermute | solution.py:171
  80.5 10.2 %collective-permute-start.1 = (bf16[8,24,512]{2,1,0:T(8,128)(2,1)S(1)}, bf16[8,24,512]{2,1,0:T(8,128)(2,1)S(1)}, u32[]{:S(2)}, u32[]{:S(2)}) collective-permute-start(bf16[8,24,512]{2,1,0:T(8,128)(2,1)S(1)} %collective-permute-done.refs_1_), channel_id=1, source_target_pairs={{0,32},{32,0},{64,96},{96,64},{128,160},{160,128},{192,224},{224,1... | collective-permute-start | bytes 589832 | tf_op jit(solution)/shard_map/ppermute | solution.py:171

commit v2 on v1

--- a/solution.py
+++ b/solution.py
@@ -13,7 +13,6 @@
 HALF = D // 2
 TILE = 256
 PLANES = ((0, 2, 4, 6, 9, 11, 13, 15), (1, 3, 5, 7, 8, 10, 12, 14))
-SHIFTS = (2, 3, 1)
 
 
 MOMENTUM_RATE = 0.95
@@ -170,11 +169,11 @@
     def across(value):
         return lax.ppermute(value, "z", [(plane, plane ^ 1) for plane in range(16)])
 
-    pieces = [piece]
-    for shift in SHIFTS:
-        near = lax.ppermute(piece, "x", [(place, (place + shift) % 4) for place in range(4)])
-        pieces += [near, across(near)]
-    return pieces + [across(piece)]
+    def along(value, shift):
+        return lax.ppermute(value, "x", [(place, (place + shift) % 4) for place in range(4)])
+
+    next_x, back_x, plane, far_x = along(piece, 1), along(piece, 3), across(piece), along(piece, 2)
+    return [piece, next_x, back_x, across(back_x), plane, along(plane, 1), far_x, across(far_x)]
 
 
 def local(gradient, momentum):

time: 119 us -> 115 us (0.966)
  blocking collectives: 79.4 us -> 77 us
    ppermute x4 -> x3, starting transfers between devices: 11.7 us -> 7.76 us  [across(): return lax.ppermute(value, 'z', [(plane, plane ^ 1) for plane in range(16)])]
    ppermute x4 -> x3, waiting for transfers between devices: 6.29 us -> 3.03 us  [across(): return lax.ppermute(value, 'z', [(plane, plane ^ 1) for plane in range(16)])]
    ppermute x3 -> x4, starting transfers between devices: 9.87 us -> 13 us  [along(): lax.ppermute(value, 'x', [(place, (place + shift) % 4) for place in range...]
    ppermute x3 -> x4, waiting for transfers between devices: 0.08 us -> 2.6 us  [along(): lax.ppermute(value, 'x', [(place, (place + shift) % 4) for place in range...]
    all_to_all x4, blocking collectives: 79.4 us -> 77 us  [exchanged(): lax.all_to_all(value, axes, split_axis=0, concat_axis=0, tiled=True, axis...]
  transfers between devices with their start and end apart: 7 -> 7, of which waited for: 4 -> 3; matrix products, arithmetic and copies ran while one was open for 0% -> 0% of each run, Pallas kernels for 0% -> 0%
where the time goes in v2:
time: 115 us; the launch traced here: 113 us
  blocking collectives  77 us (67%)
  starting transfers between devices  20.8 us (18%)
  Pallas kernels  8.84 us (8%)
  waiting for transfers between devices  5.63 us (5%)
    all_to_all x4, blocking collectives, exchanged(): lax.all_to_all(value, axes, split_axis=0, concat_axis=0, tiled=True, axis...  77 us
    ppermute x4, starting transfers between devices, along(): lax.ppermute(value, 'x', [(place, (place + shift) % 4) for place in range...  13 us
    pallas_call x5, Pallas kernels, call(): pl.pallas_call(kernel, out_shape=out_shape, in_specs=[pl.BlockSpec(memory...  8.84 us
    ppermute x3, starting transfers between devices, across(): return lax.ppermute(value, 'z', [(plane, plane ^ 1) for plane in range(16)])  7.76 us
    ppermute x3, waiting for transfers between devices, across(): return lax.ppermute(value, 'z', [(plane, plane ^ 1) for plane in range(16)])  3.03 us
    ppermute x4, waiting for transfers between devices, along(): lax.ppermute(value, 'x', [(place, (place + shift) % 4) for place in range...  2.6 us
  transfers between devices with their start and end apart: 7, of which 3 were waited for; matrix products, arithmetic and copies ran while one was open for 0% of the time, Pallas kernels for 0%

profile of v2, /device:TPU:6, one launch (start us, length us, event | category | flops | bytes accessed | tf_op | source)
XLA Modules:
  0.0 113.0 jit_solution(5951761459043479370)
XLA Ops:
  0.6 1.3 %shard_map.41 = (f32[32,1,128]{2,1,0:T(1,128)S(1)}, f32[12,8,1024]{2,1,0:T(8,128)S(1)}, f32[12,8,1024]{2,1,0:T(8,128)S(1)}) custom-call(f32[12,8,1024]{2,1,0:T(8,128)} %bitcast.4, f32[12,8,1024]{2,1,0:T(8,128)} %bitcast.5), custom_call_target="tpu_custom_call" | custom-call | tf_op jit(solution)/shard_map/pallas_call | solution.py:35
  1.9 14.1 %all_to_all.20.parts = f32[32,1,128]{2,1,0:T(1,128)S(1)} all-to-all(f32[32,1,128]{2,1,0:T(1,128)S(1)} %get-tuple-element.7), channel_id=1, replica_groups=mesh['z'=16,'x'=4,'y'=4,'core'=2] {'x','y','core'}, dimensions={0} | all-to-all | bytes 32768 | tf_op jit(solution)/shard_map/all_to_all | solution.py:165
  16.0 26.3 %all_to_all.21.total = f32[16,1,128]{2,1,0:T(1,128)S(1)} all-to-all(f32[16,1,128]{2,1,0:T(1,128)S(1)} %shard_map.42), channel_id=1, replica_groups=mesh['z'=16,'x'=4,'y'=4,'core'=2] {'z'}, dimensions={0} | all-to-all | bytes 16384 | tf_op jit(solution)/shard_map/all_to_all | solution.py:165
  42.3 0.9 shard_map.43
  43.1 19.6 %all_to_all.22.refs_0_ = bf16[8,24,512]{2,1,0:T(8,128)(2,1)S(1)} all-to-all(bf16[8,24,512]{2,1,0:T(8,128)(2,1)S(1)} %get-tuple-element.11), channel_id=1, replica_groups={{0,64,128,192,288,352,416,480},{32,96,160,224,256,320,384,448},{1,65,12..., dimensions={0} | all-to-all | bytes 393216 | tf_op jit(solution)/shard_map/all_to_all | solution.py:165
  62.7 4.0 %collective-permute-start.5 = (bf16[8,24,512]{2,1,0:T(8,128)(2,1)S(1)}, bf16[8,24,512]{2,1,0:T(8,128)(2,1)S(1)}, u32[]{:S(2)}, u32[]{:S(2)}) collective-permute-start(bf16[8,24,512]{2,1,0:T(8,128)(2,1)S(1)} %all_to_all.22.refs_0_), channel_id=1, source_target_pairs={{0,16},{8,24},{16,0},{24,8},{1,17},{9,25},{17,1},{25,9},{2,18},{10... | collective-permute-start | bytes 589832 | tf_op jit(solution)/shard_map/ppermute | solution.py:173
  66.8 1.9 %collective-permute-start.3 = (bf16[8,24,512]{2,1,0:T(8,128)(2,1)S(1)}, bf16[8,24,512]{2,1,0:T(8,128)(2,1)S(1)}, u32[]{:S(2)}, u32[]{:S(2)}) collective-permute-start(bf16[8,24,512]{2,1,0:T(8,128)(2,1)S(1)} %all_to_all.22.refs_0_), channel_id=1, source_target_pairs={{0,32},{32,0},{64,96},{96,64},{128,160},{160,128},{192,224},{224,1... | collective-permute-start | bytes 589832 | tf_op jit(solution)/shard_map/ppermute | solution.py:170
  68.7 2.7 %collective-permute-start.1 = (bf16[8,24,512]{2,1,0:T(8,128)(2,1)S(1)}, bf16[8,24,512]{2,1,0:T(8,128)(2,1)S(1)}, u32[]{:S(2)}, u32[]{:S(2)}) collective-permute-start(bf16[8,24,512]{2,1,0:T(8,128)(2,1)S(1)} %all_to_all.22.refs_0_), channel_id=1, source_target_pairs={{0,24},{8,0},{16,8},{24,16},{1,25},{9,1},{17,9},{25,17},{2,26},{10... | collective-permute-start | bytes 589832 | tf_op jit(solution)/shard_map/ppermute | solution.py:173
  71.4 4.3 %collective-permute-start = (bf16[8,24,512]{2,1,0:T(8,128)(2,1)S(1)}, bf16[8,24,512]{2,1,0:T(8,128)(2,1)S(1)}, u32[]{:S(2)}, u32[]{:S(2)}) collective-permute-start(bf16[8,24,512]{2,1,0:T(8,128)(2,1)S(1)} %all_to_all.22.refs_0_), channel_id=1, source_target_pairs={{0,8},{8,16},{16,24},{24,0},{1,9},{9,17},{17,25},{25,1},{2,10},{10... | collective-permute-start | bytes 589832 | tf_op jit(solution)/shard_map/ppermute | solution.py:173
  75.8 0.0 collective-permute-done.5.refs_6_
  75.8 3.9 %collective-permute-start.6 = (bf16[8,24,512]{2,1,0:T(8,128)(2,1)S(1)}, bf16[8,24,512]{2,1,0:T(8,128)(2,1)S(1)}, u32[]{:S(2)}, u32[]{:S(2)}) collective-permute-start(bf16[8,24,512]{2,1,0:T(8,128)(2,1)S(1)} %collective-permute-done.5.refs_6_), channel_id=1, source_target_pairs={{0,32},{32,0},{64,96},{96,64},{128,160},{160,128},{192,224},{224,1... | collective-permute-start | bytes 589832 | tf_op jit(solution)/shard_map/ppermute | solution.py:170
  79.7 0.0 collective-permute-done.3.refs_4_
  79.7 1.9 %collective-permute-start.4 = (bf16[8,24,512]{2,1,0:T(8,128)(2,1)S(1)}, bf16[8,24,512]{2,1,0:T(8,128)(2,1)S(1)}, u32[]{:S(2)}, u32[]{:S(2)}) collective-permute-start(bf16[8,24,512]{2,1,0:T(8,128)(2,1)S(1)} %collective-permute-done.3.refs_4_), channel_id=1, source_target_pairs={{0,8},{8,16},{16,24},{24,0},{1,9},{9,17},{17,25},{25,1},{2,10},{10... | collective-permute-start | bytes 589832 | tf_op jit(solution)/shard_map/ppermute | solution.py:173
  81.7 0.0 collective-permute-done.1.refs_2_
  81.7 1.9 %collective-permute-start.2 = (bf16[8,24,512]{2,1,0:T(8,128)(2,1)S(1)}, bf16[8,24,512]{2,1,0:T(8,128)(2,1)S(1)}, u32[]{:S(2)}, u32[]{:S(2)}) collective-permute-start(bf16[8,24,512]{2,1,0:T(8,128)(2,1)S(1)} %collective-permute-done.1.refs_2_), channel_id=1, source_target_pairs={{0,32},{32,0},{64,96},{96,64},{128,160},{160,128},{192,224},{224,1... | collective-permute-start | bytes 589832 | tf_op jit(solution)/shard_map/ppermute | solution.py:170
  83.6 0.0 collective-permute-done.refs_1_
  83.6 1.1 collective-permute-done.6.refs_7_
  84.7 2.6 %collective-permute-done.4.refs_5_ = bf16[8,24,512]{2,1,0:T(8,128)(2,1)S(1)} collective-permute-done((bf16[8,24,512]{2,1,0:T(8,128)(2,1)S(1)}, bf16[8,24,512]{2,1,0:T(8,128)(2,1)S(1)}, u32[]{:S(2)}, u32[]{:S(2)}) %collective-permute-start.4) | collective-permute-done | bytes 196640 | tf_op jit(solution)/shard_map/ppermute | solution.py:173
  87.3 1.9 %collective-permute-done.2.refs_3_ = bf16[8,24,512]{2,1,0:T(8,128)(2,1)S(1)} collective-permute-done((bf16[8,24,512]{2,1,0:T(8,128)(2,1)S(1)}, bf16[8,24,512]{2,1,0:T(8,128)(2,1)S(1)}, u32[]{:S(2)}, u32[]{:S(2)}) %collective-permute-start.2) | collective-permute-done | bytes 196640 | tf_op jit(solution)/shard_map/ppermute | solution.py:170
  89.2 5.9 %shard_map.44 = bf16[8,24,512]{2,1,0:T(8,128)(2,1)S(1)} custom-call(bf16[8,24,512]{2,1,0:T(8,128)(2,1)S(1)} %all_to_all.22.refs_0_, bf16[8,24,512]{2,1,0:T(8,128)(2,1)S(1)} %collective-permute-done.refs_1_, bf16[8,24,512]{2,1,0:T(8,128)(2,1)S(1)} %collective-permute-done.1.refs_2_, bf16[8,24,512]{2,1,0:T(8,128)(2,1)S(1)} %collective-permute-done.2.refs_3_, ...), custom_call_target="tpu_custom_call" | custom-call | flops 4529848320 | bytes 1572864 | tf_op jit(solution)/shard_map/pallas_call | solution.py:35
  95.1 17.1 %all_to_all.23.arrived = bf16[8,24,512]{2,1,0:T(8,128)(2,1)S(1)} all-to-all(bf16[8,24,512]{2,1,0:T(8,128)(2,1)S(1)} %shard_map.44), channel_id=1, replica_groups={{0,64,128,192,288,352,416,480},{32,96,160,224,256,320,384,448},{1,65,12..., dimensions={0} | all-to-all | bytes 393216 | tf_op jit(solution)/shard_map/all_to_all | solution.py:165
  112.2 0.8 shard_map.45
  (1 shorter events, 0.0 us)
Async XLA Ops:
  62.7 13.0 %collective-permute-start.5 = (bf16[8,24,512]{2,1,0:T(8,128)(2,1)S(1)}, bf16[8,24,512]{2,1,0:T(8,128)(2,1)S(1)}, u32[]{:S(2)}, u32[]{:S(2)}) collective-permute-start(bf16[8,24,512]{2,1,0:T(8,128)(2,1)S(1)} %all_to_all.22.refs_0_), channel_id=1, source_target_pairs={{0,16},{8,24},{16,0},{24,8},{1,17},{9,25},{17,1},{25,9},{2,18},{10... | collective-permute-start | bytes 589832 | tf_op jit(solution)/shard_map/ppermute | solution.py:173
  66.8 12.9 %collective-permute-start.3 = (bf16[8,24,512]{2,1,0:T(8,128)(2,1)S(1)}, bf16[8,24,512]{2,1,0:T(8,128)(2,1)S(1)}, u32[]{:S(2)}, u32[]{:S(2)}) collective-permute-start(bf16[8,24,512]{2,1,0:T(8,128)(2,1)S(1)} %all_to_all.22.refs_0_), channel_id=1, source_target_pairs={{0,32},{32,0},{64,96},{96,64},{128,160},{160,128},{192,224},{224,1... | collective-permute-start | bytes 589832 | tf_op jit(solution)/shard_map/ppermute | solution.py:170
  68.7 13.0 %collective-permute-start.1 = (bf16[8,24,512]{2,1,0:T(8,128)(2,1)S(1)}, bf16[8,24,512]{2,1,0:T(8,128)(2,1)S(1)}, u32[]{:S(2)}, u32[]{:S(2)}) collective-permute-start(bf16[8,24,512]{2,1,0:T(8,128)(2,1)S(1)} %all_to_all.22.refs_0_), channel_id=1, source_target_pairs={{0,24},{8,0},{16,8},{24,16},{1,25},{9,1},{17,9},{25,17},{2,26},{10... | collective-permute-start | bytes 589832 | tf_op jit(solution)/shard_map/ppermute | solution.py:173
  71.4 12.2 %collective-permute-start = (bf16[8,24,512]{2,1,0:T(8,128)(2,1)S(1)}, bf16[8,24,512]{2,1,0:T(8,128)(2,1)S(1)}, u32[]{:S(2)}, u32[]{:S(2)}) collective-permute-start(bf16[8,24,512]{2,1,0:T(8,128)(2,1)S(1)} %all_to_all.22.refs_0_), channel_id=1, source_target_pairs={{0,8},{8,16},{16,24},{24,0},{1,9},{9,17},{17,25},{25,1},{2,10},{10... | collective-permute-start | bytes 589832 | tf_op jit(solution)/shard_map/ppermute | solution.py:173
  75.8 8.9 %collective-permute-start.6 = (bf16[8,24,512]{2,1,0:T(8,128)(2,1)S(1)}, bf16[8,24,512]{2,1,0:T(8,128)(2,1)S(1)}, u32[]{:S(2)}, u32[]{:S(2)}) collective-permute-start(bf16[8,24,512]{2,1,0:T(8,128)(2,1)S(1)} %collective-permute-done.5.refs_6_), channel_id=1, source_target_pairs={{0,32},{32,0},{64,96},{96,64},{128,160},{160,128},{192,224},{224,1... | collective-permute-start | bytes 589832 | tf_op jit(solution)/shard_map/ppermute | solution.py:170
  79.7 7.6 %collective-permute-start.4 = (bf16[8,24,512]{2,1,0:T(8,128)(2,1)S(1)}, bf16[8,24,512]{2,1,0:T(8,128)(2,1)S(1)}, u32[]{:S(2)}, u32[]{:S(2)}) collective-permute-start(bf16[8,24,512]{2,1,0:T(8,128)(2,1)S(1)} %collective-permute-done.3.refs_4_), channel_id=1, source_target_pairs={{0,8},{8,16},{16,24},{24,0},{1,9},{9,17},{17,25},{25,1},{2,10},{10... | collective-permute-start | bytes 589832 | tf_op jit(solution)/shard_map/ppermute | solution.py:173
  81.7 7.6 %collective-permute-start.2 = (bf16[8,24,512]{2,1,0:T(8,128)(2,1)S(1)}, bf16[8,24,512]{2,1,0:T(8,128)(2,1)S(1)}, u32[]{:S(2)}, u32[]{:S(2)}) collective-permute-start(bf16[8,24,512]{2,1,0:T(8,128)(2,1)S(1)} %collective-permute-done.1.refs_2_), channel_id=1, source_target_pairs={{0,32},{32,0},{64,96},{96,64},{128,160},{160,128},{192,224},{224,1... | collective-permute-start | bytes 589832 | tf_op jit(solution)/shard_map/ppermute | solution.py:170

commit v3 on v2

--- a/solution.py
+++ b/solution.py
@@ -166,14 +166,22 @@
 
 
 def gathered(piece):
-    def across(value):
-        return lax.ppermute(value, "z", [(plane, plane ^ 1) for plane in range(16)])
-
-    def along(value, shift):
-        return lax.ppermute(value, "x", [(place, (place + shift) % 4) for place in range(4)])
-
-    next_x, back_x, plane, far_x = along(piece, 1), along(piece, 3), across(piece), along(piece, 2)
-    return [piece, next_x, back_x, across(back_x), plane, along(plane, 1), far_x, across(far_x)]
+    def swapped(value, axis, flip):
+        size = lax.axis_size(axis)
+        return lax.ppermute(value, axis, [(place, place ^ flip) for place in range(size)])
+
+    side, other_side, far = swapped(piece, "x", 1), swapped(piece, "x", 3), swapped(piece, "x", 2)
+    plane = swapped(piece, "z", 1)
+    return [
+        piece,
+        side,
+        other_side,
+        far,
+        swapped(far, "z", 1),
+        plane,
+        swapped(plane, "x", 3),
+        swapped(plane, "x", 1),
+    ]
 
 
 def local(gradient, momentum):

time: 115 us -> 114 us (level); the launches traced: 113 us -> 114 us
  waiting for transfers between devices: 5.63 us -> 3.61 us
  starting transfers between devices: 20.8 us -> 22.8 us
    ppermute x7, waiting for transfers between devices: 5.63 us -> 3.61 us  [swapped(): lax.ppermute(value, axis, [(place, place ^ flip) for place in range(size)])]
    ppermute x7, starting transfers between devices: 20.8 us -> 22.8 us  [swapped(): lax.ppermute(value, axis, [(place, place ^ flip) for place in range(size)])]
  transfers between devices with their start and end apart: 7 -> 7, of which waited for: 3 -> 2; matrix products, arithmetic and copies ran while one was open for 0% -> 0% of each run, Pallas kernels for 0% -> 0%
where the time goes in v3:
time: 114 us
  blocking collectives  78 us (68%)
  starting transfers between devices  22.8 us (20%)
  Pallas kernels  8.85 us (8%)
  waiting for transfers between devices  3.61 us (3%)
    all_to_all x4, blocking collectives, exchanged(): lax.all_to_all(value, axes, split_axis=0, concat_axis=0, tiled=True, axis...  78 us
    ppermute x7, starting transfers between devices, swapped(): lax.ppermute(value, axis, [(place, place ^ flip) for place in range(size)])  22.8 us
    pallas_call x5, Pallas kernels, call(): pl.pallas_call(kernel, out_shape=out_shape, in_specs=[pl.BlockSpec(memory...  8.85 us
    ppermute x7, waiting for transfers between devices, swapped(): lax.ppermute(value, axis, [(place, place ^ flip) for place in range(size)])  3.61 us
  transfers between devices with their start and end apart: 7, of which 2 were waited for; matrix products, arithmetic and copies ran while one was open for 0% of the time, Pallas kernels for 0%

profile of v3, /device:TPU:6, one launch (start us, length us, event | category | flops | bytes accessed | tf_op | source)
XLA Modules:
  0.0 114.0 jit_solution(2152567702763452367)
XLA Ops:
  0.6 1.3 %shard_map.41 = (f32[32,1,128]{2,1,0:T(1,128)S(1)}, f32[12,8,1024]{2,1,0:T(8,128)S(1)}, f32[12,8,1024]{2,1,0:T(8,128)S(1)}) custom-call(f32[12,8,1024]{2,1,0:T(8,128)} %bitcast.4, f32[12,8,1024]{2,1,0:T(8,128)} %bitcast.5), custom_call_target="tpu_custom_call" | custom-call | tf_op jit(solution)/shard_map/pallas_call | solution.py:35
  1.9 14.1 %all_to_all.20.parts = f32[32,1,128]{2,1,0:T(1,128)S(1)} all-to-all(f32[32,1,128]{2,1,0:T(1,128)S(1)} %get-tuple-element.7), channel_id=1, replica_groups=mesh['z'=16,'x'=4,'y'=4,'core'=2] {'x','y','core'}, dimensions={0} | all-to-all | bytes 32768 | tf_op jit(solution)/shard_map/all_to_all | solution.py:165
  16.0 26.3 %all_to_all.21.total = f32[16,1,128]{2,1,0:T(1,128)S(1)} all-to-all(f32[16,1,128]{2,1,0:T(1,128)S(1)} %shard_map.42), channel_id=1, replica_groups=mesh['z'=16,'x'=4,'y'=4,'core'=2] {'z'}, dimensions={0} | all-to-all | bytes 16384 | tf_op jit(solution)/shard_map/all_to_all | solution.py:165
  42.3 0.9 shard_map.43
  43.1 19.6 %all_to_all.22.refs_0_ = bf16[8,24,512]{2,1,0:T(8,128)(2,1)S(1)} all-to-all(bf16[8,24,512]{2,1,0:T(8,128)(2,1)S(1)} %get-tuple-element.11), channel_id=1, replica_groups={{0,64,128,192,288,352,416,480},{32,96,160,224,256,320,384,448},{1,65,12..., dimensions={0} | all-to-all | bytes 393216 | tf_op jit(solution)/shard_map/all_to_all | solution.py:165
  62.7 1.9 %collective-permute-start.4 = (bf16[8,24,512]{2,1,0:T(8,128)(2,1)S(1)}, bf16[8,24,512]{2,1,0:T(8,128)(2,1)S(1)}, u32[]{:S(2)}, u32[]{:S(2)}) collective-permute-start(bf16[8,24,512]{2,1,0:T(8,128)(2,1)S(1)} %all_to_all.22.refs_0_), channel_id=1, source_target_pairs={{0,32},{32,0},{64,96},{96,64},{128,160},{160,128},{192,224},{224,1... | collective-permute-start | bytes 589832 | tf_op jit(solution)/shard_map/ppermute | solution.py:171
  64.7 4.0 %collective-permute-start.2 = (bf16[8,24,512]{2,1,0:T(8,128)(2,1)S(1)}, bf16[8,24,512]{2,1,0:T(8,128)(2,1)S(1)}, u32[]{:S(2)}, u32[]{:S(2)}) collective-permute-start(bf16[8,24,512]{2,1,0:T(8,128)(2,1)S(1)} %all_to_all.22.refs_0_), channel_id=1, source_target_pairs={{0,16},{8,24},{16,0},{24,8},{1,17},{9,25},{17,1},{25,9},{2,18},{10... | collective-permute-start | bytes 589832 | tf_op jit(solution)/shard_map/ppermute | solution.py:171
  68.7 3.1 %collective-permute-start.1 = (bf16[8,24,512]{2,1,0:T(8,128)(2,1)S(1)}, bf16[8,24,512]{2,1,0:T(8,128)(2,1)S(1)}, u32[]{:S(2)}, u32[]{:S(2)}) collective-permute-start(bf16[8,24,512]{2,1,0:T(8,128)(2,1)S(1)} %all_to_all.22.refs_0_), channel_id=1, source_target_pairs={{0,24},{8,16},{16,8},{24,0},{1,25},{9,17},{17,9},{25,1},{2,26},{10... | collective-permute-start | bytes 589832 | tf_op jit(solution)/shard_map/ppermute | solution.py:171
  71.8 2.1 %collective-permute-start = (bf16[8,24,512]{2,1,0:T(8,128)(2,1)S(1)}, bf16[8,24,512]{2,1,0:T(8,128)(2,1)S(1)}, u32[]{:S(2)}, u32[]{:S(2)}) collective-permute-start(bf16[8,24,512]{2,1,0:T(8,128)(2,1)S(1)} %all_to_all.22.refs_0_), channel_id=1, source_target_pairs={{0,8},{8,0},{16,24},{24,16},{1,9},{9,1},{17,25},{25,17},{2,10},{10... | collective-permute-start | bytes 589832 | tf_op jit(solution)/shard_map/ppermute | solution.py:171
  73.9 0.0 collective-permute-done.4.refs_5_
  73.9 3.8 %collective-permute-start.6 = (bf16[8,24,512]{2,1,0:T(8,128)(2,1)S(1)}, bf16[8,24,512]{2,1,0:T(8,128)(2,1)S(1)}, u32[]{:S(2)}, u32[]{:S(2)}) collective-permute-start(bf16[8,24,512]{2,1,0:T(8,128)(2,1)S(1)} %collective-permute-done.4.refs_5_), channel_id=1, source_target_pairs={{0,8},{8,0},{16,24},{24,16},{1,9},{9,1},{17,25},{25,17},{2,10},{10... | collective-permute-start | bytes 589832 | tf_op jit(solution)/shard_map/ppermute | solution.py:171
  77.7 4.0 %collective-permute-start.5 = (bf16[8,24,512]{2,1,0:T(8,128)(2,1)S(1)}, bf16[8,24,512]{2,1,0:T(8,128)(2,1)S(1)}, u32[]{:S(2)}, u32[]{:S(2)}) collective-permute-start(bf16[8,24,512]{2,1,0:T(8,128)(2,1)S(1)} %collective-permute-done.4.refs_5_), channel_id=1, source_target_pairs={{0,24},{8,16},{16,8},{24,0},{1,25},{9,17},{17,9},{25,1},{2,26},{10... | collective-permute-start | bytes 589832 | tf_op jit(solution)/shard_map/ppermute | solution.py:171
  81.6 0.0 collective-permute-done.2.refs_3_
  81.7 3.9 %collective-permute-start.3 = (bf16[8,24,512]{2,1,0:T(8,128)(2,1)S(1)}, bf16[8,24,512]{2,1,0:T(8,128)(2,1)S(1)}, u32[]{:S(2)}, u32[]{:S(2)}) collective-permute-start(bf16[8,24,512]{2,1,0:T(8,128)(2,1)S(1)} %collective-permute-done.2.refs_3_), channel_id=1, source_target_pairs={{0,32},{32,0},{64,96},{96,64},{128,160},{160,128},{192,224},{224,1... | collective-permute-start | bytes 589832 | tf_op jit(solution)/shard_map/ppermute | solution.py:171
  85.6 0.0 collective-permute-done.1.refs_2_
  85.6 0.0 collective-permute-done.refs_1_
  85.6 0.0 collective-permute-done.6.refs_7_
  85.6 0.8 collective-permute-done.5.refs_6_
  86.5 2.8 %collective-permute-done.3.refs_4_ = bf16[8,24,512]{2,1,0:T(8,128)(2,1)S(1)} collective-permute-done((bf16[8,24,512]{2,1,0:T(8,128)(2,1)S(1)}, bf16[8,24,512]{2,1,0:T(8,128)(2,1)S(1)}, u32[]{:S(2)}, u32[]{:S(2)}) %collective-permute-start.3) | collective-permute-done | bytes 196640 | tf_op jit(solution)/shard_map/ppermute | solution.py:171
  89.2 5.9 %shard_map.44 = bf16[8,24,512]{2,1,0:T(8,128)(2,1)S(1)} custom-call(bf16[8,24,512]{2,1,0:T(8,128)(2,1)S(1)} %all_to_all.22.refs_0_, bf16[8,24,512]{2,1,0:T(8,128)(2,1)S(1)} %collective-permute-done.refs_1_, bf16[8,24,512]{2,1,0:T(8,128)(2,1)S(1)} %collective-permute-done.1.refs_2_, bf16[8,24,512]{2,1,0:T(8,128)(2,1)S(1)} %collective-permute-done.2.refs_3_, ...), custom_call_target="tpu_custom_call" | custom-call | flops 4529848320 | bytes 1572864 | tf_op jit(solution)/shard_map/pallas_call | solution.py:35
  95.1 18.1 %all_to_all.23.arrived = bf16[8,24,512]{2,1,0:T(8,128)(2,1)S(1)} all-to-all(bf16[8,24,512]{2,1,0:T(8,128)(2,1)S(1)} %shard_map.44), channel_id=1, replica_groups={{0,64,128,192,288,352,416,480},{32,96,160,224,256,320,384,448},{1,65,12..., dimensions={0} | all-to-all | bytes 393216 | tf_op jit(solution)/shard_map/all_to_all | solution.py:165
  113.2 0.8 shard_map.45
  (1 shorter events, 0.0 us)
Async XLA Ops:
  62.7 11.2 %collective-permute-start.4 = (bf16[8,24,512]{2,1,0:T(8,128)(2,1)S(1)}, bf16[8,24,512]{2,1,0:T(8,128)(2,1)S(1)}, u32[]{:S(2)}, u32[]{:S(2)}) collective-permute-start(bf16[8,24,512]{2,1,0:T(8,128)(2,1)S(1)} %all_to_all.22.refs_0_), channel_id=1, source_target_pairs={{0,32},{32,0},{64,96},{96,64},{128,160},{160,128},{192,224},{224,1... | collective-permute-start | bytes 589832 | tf_op jit(solution)/shard_map/ppermute | solution.py:171
  64.7 17.0 %collective-permute-start.2 = (bf16[8,24,512]{2,1,0:T(8,128)(2,1)S(1)}, bf16[8,24,512]{2,1,0:T(8,128)(2,1)S(1)}, u32[]{:S(2)}, u32[]{:S(2)}) collective-permute-start(bf16[8,24,512]{2,1,0:T(8,128)(2,1)S(1)} %all_to_all.22.refs_0_), channel_id=1, source_target_pairs={{0,16},{8,24},{16,0},{24,8},{1,17},{9,25},{17,1},{25,9},{2,18},{10... | collective-permute-start | bytes 589832 | tf_op jit(solution)/shard_map/ppermute | solution.py:171
  68.7 16.9 %collective-permute-start.1 = (bf16[8,24,512]{2,1,0:T(8,128)(2,1)S(1)}, bf16[8,24,512]{2,1,0:T(8,128)(2,1)S(1)}, u32[]{:S(2)}, u32[]{:S(2)}) collective-permute-start(bf16[8,24,512]{2,1,0:T(8,128)(2,1)S(1)} %all_to_all.22.refs_0_), channel_id=1, source_target_pairs={{0,24},{8,16},{16,8},{24,0},{1,25},{9,17},{17,9},{25,1},{2,26},{10... | collective-permute-start | bytes 589832 | tf_op jit(solution)/shard_map/ppermute | solution.py:171
  71.8 13.8 %collective-permute-start = (bf16[8,24,512]{2,1,0:T(8,128)(2,1)S(1)}, bf16[8,24,512]{2,1,0:T(8,128)(2,1)S(1)}, u32[]{:S(2)}, u32[]{:S(2)}) collective-permute-start(bf16[8,24,512]{2,1,0:T(8,128)(2,1)S(1)} %all_to_all.22.refs_0_), channel_id=1, source_target_pairs={{0,8},{8,0},{16,24},{24,16},{1,9},{9,1},{17,25},{25,17},{2,10},{10... | collective-permute-start | bytes 589832 | tf_op jit(solution)/shard_map/ppermute | solution.py:171
  73.9 11.7 %collective-permute-start.6 = (bf16[8,24,512]{2,1,0:T(8,128)(2,1)S(1)}, bf16[8,24,512]{2,1,0:T(8,128)(2,1)S(1)}, u32[]{:S(2)}, u32[]{:S(2)}) collective-permute-start(bf16[8,24,512]{2,1,0:T(8,128)(2,1)S(1)} %collective-permute-done.4.refs_5_), channel_id=1, source_target_pairs={{0,8},{8,0},{16,24},{24,16},{1,9},{9,1},{17,25},{25,17},{2,10},{10... | collective-permute-start | bytes 589832 | tf_op jit(solution)/shard_map/ppermute | solution.py:171
  77.7 8.8 %collective-permute-start.5 = (bf16[8,24,512]{2,1,0:T(8,128)(2,1)S(1)}, bf16[8,24,512]{2,1,0:T(8,128)(2,1)S(1)}, u32[]{:S(2)}, u32[]{:S(2)}) collective-permute-start(bf16[8,24,512]{2,1,0:T(8,128)(2,1)S(1)} %collective-permute-done.4.refs_5_), channel_id=1, source_target_pairs={{0,24},{8,16},{16,8},{24,0},{1,25},{9,17},{17,9},{25,1},{2,26},{10... | collective-permute-start | bytes 589832 | tf_op jit(solution)/shard_map/ppermute | solution.py:171
  81.7 7.6 %collective-permute-start.3 = (bf16[8,24,512]{2,1,0:T(8,128)(2,1)S(1)}, bf16[8,24,512]{2,1,0:T(8,128)(2,1)S(1)}, u32[]{:S(2)}, u32[]{:S(2)}) collective-permute-start(bf16[8,24,512]{2,1,0:T(8,128)(2,1)S(1)} %collective-permute-done.2.refs_3_), channel_id=1, source_target_pairs={{0,32},{32,0},{64,96},{96,64},{128,160},{160,128},{192,224},{224,1... | collective-permute-start | bytes 589832 | tf_op jit(solution)/shard_map/ppermute | solution.py:171

commit v4 on v3

--- a/solution.py
+++ b/solution.py
@@ -61,13 +61,19 @@
     out[...] = jnp.broadcast_to(jnp.sum(parts[...], axis=0, keepdims=True), out.shape)
 
 
-def blend_kernel(total, gradient, decayed, momentum_next, outgoing):
+def factor_of(total):
     total_square = jnp.sum(total[...], axis=0)[:, :1]
     factor = jnp.minimum(1.0, RMS_CAP * math.sqrt(MATS * MATS * FF * D) / jnp.sqrt(total_square))
-    scaled = factor[None] * gradient[...]
-    following = decayed[...] + scaled
-    momentum_next[...] = following
-    blended = jnp.swapaxes(scaled + MOMENTUM_RATE * following, 0, 1)
+    return factor[None]
+
+
+def follow_kernel(total, gradient, decayed, momentum_next):
+    momentum_next[...] = decayed[...] + factor_of(total) * gradient[...]
+
+
+def blend_kernel(total, gradient, decayed, outgoing):
+    scaled = factor_of(total) * gradient[...]
+    blended = jnp.swapaxes(scaled + MOMENTUM_RATE * (decayed[...] + scaled), 0, 1)
     left, right = blended[:, :, :HALF], blended[:, :, HALF:]
     packed = jnp.concatenate([left[:, :8], right[:, :8], left[:, 8:], right[:, 8:]], axis=1)
     outgoing[...] = packed.astype(jnp.bfloat16)
@@ -97,24 +103,22 @@
 
 
 def orthogonal_kernel(*refs):
-    pieces, (out, whole, product, gram, poly, second) = refs[:MATS], refs[MATS:]
+    pieces, (out, whole, gram, poly, second) = refs[:MATS], refs[MATS:]
     rows = FF // MATS
     tiles = [slice(start, start + TILE) for start in range(0, FF, TILE)]
+    squares = jnp.zeros(pieces[0].shape[1:], jnp.float32)
     for number, piece in enumerate(pieces):
-        left, right = unpacked(piece[...].astype(jnp.float32))
+        value = piece[...].astype(jnp.float32)
+        squares += jnp.sum(value * value, axis=0)
+        left, right = unpacked(value)
         place = slice(number * rows, (number + 1) * rows)
         whole[place, :HALF] = left.astype(jnp.bfloat16)
         whole[place, HALF:] = right.astype(jnp.bfloat16)
-    on_diagonal = lax.broadcasted_iota(jnp.int32, (TILE, TILE), 0) == lax.broadcasted_iota(
-        jnp.int32, (TILE, TILE), 1
-    )
-    norm_square = jnp.float32(0.0)
-    for tile in tiles:
-        product[tile, :] = dot_transposed(whole[tile, :], whole[...])
-        norm_square += jnp.sum(jnp.where(on_diagonal, product[tile, tile], 0.0))
-    inverse = 1.0 / (jnp.sqrt(jnp.full((1, 1), norm_square, jnp.float32)) + NORM_EPS)
-    for tile in tiles:
-        gram[tile, :] = (product[tile, :] * (inverse * inverse)).astype(jnp.bfloat16)
+    norm_square = jnp.full((1, 1), jnp.sum(squares), jnp.float32)
+    inverse = 1.0 / (jnp.sqrt(norm_square) + NORM_EPS)
+    for tile in tiles:
+        product = dot_transposed(whole[tile, :], whole[...])
+        gram[tile, :] = (product * (inverse * inverse)).astype(jnp.bfloat16)
     for tile in tiles:
         squared = dot_f32(gram[tile, :], gram[...])
         poly[tile, :] = (COEF_B * gram[tile, :].astype(jnp.float32) + COEF_C * squared).astype(
@@ -150,7 +154,6 @@
         *pieces,
         scratch=[
             pltpu.VMEM((FF, D), jnp.bfloat16),
-            pltpu.VMEM((FF, FF), jnp.float32),
             pltpu.VMEM((FF, FF), jnp.bfloat16),
             pltpu.VMEM((FF, FF), jnp.bfloat16),
             pltpu.VMEM((FF, D), jnp.bfloat16),
@@ -200,18 +203,12 @@
     squares = exchanged(squares, ("x", "y", "core"))
     squares = call(add_kernel, jax.ShapeDtypeStruct((16, 1, 128), jnp.float32), squares)
     squares = exchanged(squares, "z")
-    momentum_next, outgoing = call(
-        blend_kernel,
-        (
-            whole,
-            jax.ShapeDtypeStruct((MATS, 24, HALF), jnp.bfloat16),
-        ),
-        squares,
-        kept,
-        decayed,
+    outgoing = call(
+        blend_kernel, jax.ShapeDtypeStruct((MATS, 24, HALF), jnp.bfloat16), squares, kept, decayed
     )
     piece = exchanged(outgoing, "z", PLANES)
     returning = orthogonal_rows(gathered(piece))
+    momentum_next = call(follow_kernel, whole, squares, kept, decayed)
     arrived = exchanged(returning, "z", PLANES)
     update = call(spread_kernel, jax.ShapeDtypeStruct(shape, jnp.bfloat16), arrived)
     return (jnp.swapaxes(momentum_next, 0, 1), jnp.swapaxes(update, 0, 1))

time: 114 us -> 115 us (level)
  the two profiles are of different devices: /device:TPU:6 before, /device:TPU:32 now
where the time goes in v4:
time: 115 us; the launch traced here: 114 us
  blocking collectives  59 us (51%)
  starting transfers between devices  25.9 us (23%)
  waiting for transfers between devices  19.2 us (17%)
  Pallas kernels  9.32 us (8%)
    all_to_all x3, blocking collectives, exchanged(): lax.all_to_all(value, axes, split_axis=0, concat_axis=0, tiled=True, axis...  59 us
    ppermute x7, starting transfers between devices, swapped(): lax.ppermute(value, axis, [(place, place ^ flip) for place in range(size)])  22.5 us
    all_to_all x1, waiting for transfers between devices, exchanged(): lax.all_to_all(value, axes, split_axis=0, concat_axis=0, tiled=True, axis...  13.6 us
    pallas_call x6, Pallas kernels, call(): pl.pallas_call(kernel, out_shape=out_shape, in_specs=[pl.BlockSpec(memory...  9.32 us
    ppermute x7, waiting for transfers between devices, swapped(): lax.ppermute(value, axis, [(place, place ^ flip) for place in range(size)])  5.62 us
    all_to_all x1, starting transfers between devices, exchanged(): lax.all_to_all(value, axes, split_axis=0, concat_axis=0, tiled=True, axis...  3.39 us
  transfers between devices with their start and end apart: 8, of which 3 were waited for; matrix products, arithmetic and copies ran while one was open for 0% of the time, Pallas kernels for 1%

profile of v4, /device:TPU:32, one launch (start us, length us, event | category | flops | bytes accessed | tf_op | source)
XLA Modules:
  0.0 114.2 jit_solution(2586490909827505867)
XLA Ops:
  0.6 1.3 %shard_map.41 = (f32[32,1,128]{2,1,0:T(1,128)S(1)}, f32[12,8,1024]{2,1,0:T(8,128)S(1)}, f32[12,8,1024]{2,1,0:T(8,128)S(1)}) custom-call(f32[12,8,1024]{2,1,0:T(8,128)} %bitcast.4, f32[12,8,1024]{2,1,0:T(8,128)} %bitcast.5), custom_call_target="tpu_custom_call" | custom-call | tf_op jit(solution)/shard_map/pallas_call | solution.py:35
  1.9 14.5 %all_to_all.20.parts = f32[32,1,128]{2,1,0:T(1,128)S(1)} all-to-all(f32[32,1,128]{2,1,0:T(1,128)S(1)} %get-tuple-element.5), channel_id=1, replica_groups=mesh['z'=16,'x'=4,'y'=4,'core'=2] {'x','y','core'}, dimensions={0} | all-to-all | bytes 32768 | tf_op jit(solution)/shard_map/all_to_all | solution.py:168
  16.4 26.1 %all_to_all.21.total = f32[16,1,128]{2,1,0:T(1,128)S(1)} all-to-all(f32[16,1,128]{2,1,0:T(1,128)S(1)} %shard_map.42), channel_id=1, replica_groups=mesh['z'=16,'x'=4,'y'=4,'core'=2] {'z'}, dimensions={0} | all-to-all | bytes 16384 | tf_op jit(solution)/shard_map/all_to_all | solution.py:168
  42.6 0.2 shard_map.44
  42.8 18.4 %all_to_all.22.refs_0_ = bf16[8,24,512]{2,1,0:T(8,128)(2,1)S(1)} all-to-all(bf16[8,24,512]{2,1,0:T(8,128)(2,1)S(1)} %shard_map.44), channel_id=1, replica_groups={{0,64,128,192,288,352,416,480},{32,96,160,224,256,320,384,448},{1,65,12..., dimensions={0} | all-to-all | bytes 393216 | tf_op jit(solution)/shard_map/all_to_all | solution.py:168
  61.2 4.5 %collective-permute-start.4 = (bf16[8,24,512]{2,1,0:T(8,128)(2,1)S(1)}, bf16[8,24,512]{2,1,0:T(8,128)(2,1)S(1)}, u32[]{:S(2)}, u32[]{:S(2)}) collective-permute-start(bf16[8,24,512]{2,1,0:T(8,128)(2,1)S(1)} %all_to_all.22.refs_0_), channel_id=1, source_target_pairs={{0,32},{32,0},{64,96},{96,64},{128,160},{160,128},{192,224},{224,1... | collective-permute-start | bytes 589832 | tf_op jit(solution)/shard_map/ppermute | solution.py:174
  65.7 3.2 %collective-permute-start.2 = (bf16[8,24,512]{2,1,0:T(8,128)(2,1)S(1)}, bf16[8,24,512]{2,1,0:T(8,128)(2,1)S(1)}, u32[]{:S(2)}, u32[]{:S(2)}) collective-permute-start(bf16[8,24,512]{2,1,0:T(8,128)(2,1)S(1)} %all_to_all.22.refs_0_), channel_id=1, source_target_pairs={{0,16},{8,24},{16,0},{24,8},{1,17},{9,25},{17,1},{25,9},{2,18},{10... | collective-permute-start | bytes 589832 | tf_op jit(solution)/shard_map/ppermute | solution.py:174
  68.9 4.0 %collective-permute-start.1 = (bf16[8,24,512]{2,1,0:T(8,128)(2,1)S(1)}, bf16[8,24,512]{2,1,0:T(8,128)(2,1)S(1)}, u32[]{:S(2)}, u32[]{:S(2)}) collective-permute-start(bf16[8,24,512]{2,1,0:T(8,128)(2,1)S(1)} %all_to_all.22.refs_0_), channel_id=1, source_target_pairs={{0,24},{8,16},{16,8},{24,0},{1,25},{9,17},{17,9},{25,1},{2,26},{10... | collective-permute-start | bytes 589832 | tf_op jit(solution)/shard_map/ppermute | solution.py:174
  72.9 2.1 %collective-permute-start = (bf16[8,24,512]{2,1,0:T(8,128)(2,1)S(1)}, bf16[8,24,512]{2,1,0:T(8,128)(2,1)S(1)}, u32[]{:S(2)}, u32[]{:S(2)}) collective-permute-start(bf16[8,24,512]{2,1,0:T(8,128)(2,1)S(1)} %all_to_all.22.refs_0_), channel_id=1, source_target_pairs={{0,8},{8,0},{16,24},{24,16},{1,9},{9,1},{17,25},{25,17},{2,10},{10... | collective-permute-start | bytes 589832 | tf_op jit(solution)/shard_map/ppermute | solution.py:174
  75.0 0.0 collective-permute-done.4.refs_5_
  75.0 3.7 %collective-permute-start.6 = (bf16[8,24,512]{2,1,0:T(8,128)(2,1)S(1)}, bf16[8,24,512]{2,1,0:T(8,128)(2,1)S(1)}, u32[]{:S(2)}, u32[]{:S(2)}) collective-permute-start(bf16[8,24,512]{2,1,0:T(8,128)(2,1)S(1)} %collective-permute-done.4.refs_5_), channel_id=1, source_target_pairs={{0,8},{8,0},{16,24},{24,16},{1,9},{9,1},{17,25},{25,17},{2,10},{10... | collective-permute-start | bytes 589832 | tf_op jit(solution)/shard_map/ppermute | solution.py:174
  78.7 3.1 %collective-permute-start.5 = (bf16[8,24,512]{2,1,0:T(8,128)(2,1)S(1)}, bf16[8,24,512]{2,1,0:T(8,128)(2,1)S(1)}, u32[]{:S(2)}, u32[]{:S(2)}) collective-permute-start(bf16[8,24,512]{2,1,0:T(8,128)(2,1)S(1)} %collective-permute-done.4.refs_5_), channel_id=1, source_target_pairs={{0,24},{8,16},{16,8},{24,0},{1,25},{9,17},{17,9},{25,1},{2,26},{10... | collective-permute-start | bytes 589832 | tf_op jit(solution)/shard_map/ppermute | solution.py:174
  81.8 0.0 collective-permute-done.2.refs_3_
  81.9 1.9 %collective-permute-start.3 = (bf16[8,24,512]{2,1,0:T(8,128)(2,1)S(1)}, bf16[8,24,512]{2,1,0:T(8,128)(2,1)S(1)}, u32[]{:S(2)}, u32[]{:S(2)}) collective-permute-start(bf16[8,24,512]{2,1,0:T(8,128)(2,1)S(1)} %collective-permute-done.2.refs_3_), channel_id=1, source_target_pairs={{0,32},{32,0},{64,96},{96,64},{128,160},{160,128},{192,224},{224,1... | collective-permute-start | bytes 589832 | tf_op jit(solution)/shard_map/ppermute | solution.py:174
  83.8 0.0 collective-permute-done.1.refs_2_
  83.8 0.0 collective-permute-done.refs_1_
  83.8 0.0 collective-permute-done.6.refs_7_
  83.8 3.7 %collective-permute-done.5.refs_6_ = bf16[8,24,512]{2,1,0:T(8,128)(2,1)S(1)} collective-permute-done((bf16[8,24,512]{2,1,0:T(8,128)(2,1)S(1)}, bf16[8,24,512]{2,1,0:T(8,128)(2,1)S(1)}, u32[]{:S(2)}, u32[]{:S(2)}) %collective-permute-start.5) | collective-permute-done | bytes 196640 | tf_op jit(solution)/shard_map/ppermute | solution.py:174
  87.5 1.9 %collective-permute-done.3.refs_4_ = bf16[8,24,512]{2,1,0:T(8,128)(2,1)S(1)} collective-permute-done((bf16[8,24,512]{2,1,0:T(8,128)(2,1)S(1)}, bf16[8,24,512]{2,1,0:T(8,128)(2,1)S(1)}, u32[]{:S(2)}, u32[]{:S(2)}) %collective-permute-start.3) | collective-permute-done | bytes 196640 | tf_op jit(solution)/shard_map/ppermute | solution.py:174
  89.4 6.1 %shard_map.45 = bf16[8,24,512]{2,1,0:T(8,128)(2,1)} custom-call(bf16[8,24,512]{2,1,0:T(8,128)(2,1)S(1)} %all_to_all.22.refs_0_, bf16[8,24,512]{2,1,0:T(8,128)(2,1)S(1)} %collective-permute-done.refs_1_, bf16[8,24,512]{2,1,0:T(8,128)(2,1)S(1)} %collective-permute-done.1.refs_2_, bf16[8,24,512]{2,1,0:T(8,128)(2,1)S(1)} %collective-permute-done.2.refs_3_, ...), custom_call_target="tpu_custom_call" | custom-call | flops 4529848320 | bytes 1572864 | tf_op jit(solution)/shard_map/pallas_call | solution.py:35
  95.5 3.4 %all-to-all-start.3 = ((bf16[8,24,512]{2,1,0:T(8,128)(2,1)}), bf16[8,24,512]{2,1,0:T(8,128)(2,1)S(1)}, u32[]{:S(2)}, u32[]{:S(2)}) async-start(bf16[8,24,512]{2,1,0:T(8,128)(2,1)} %shard_map.45), calls=%async_computation.3 | async-start | bytes 393216 | tf_op jit(solution)/shard_map/all_to_all | solution.py:168
  98.9 0.9 shard_map.43
  99.8 13.6 %all-to-all-done.3.arrived = bf16[8,24,512]{2,1,0:T(8,128)(2,1)S(1)} async-done(((bf16[8,24,512]{2,1,0:T(8,128)(2,1)}), bf16[8,24,512]{2,1,0:T(8,128)(2,1)S(1)}, u32[]{:S(2)}, u32[]{:S(2)}) %all-to-all-start.3) | async-done | bytes 196640 | tf_op jit(solution)/shard_map/all_to_all | solution.py:168
  113.4 0.8 shard_map.46
  (1 shorter events, 0.0 us)
Async XLA Ops:
  61.2 13.7 %collective-permute-start.4 = (bf16[8,24,512]{2,1,0:T(8,128)(2,1)S(1)}, bf16[8,24,512]{2,1,0:T(8,128)(2,1)S(1)}, u32[]{:S(2)}, u32[]{:S(2)}) collective-permute-start(bf16[8,24,512]{2,1,0:T(8,128)(2,1)S(1)} %all_to_all.22.refs_0_), channel_id=1, source_target_pairs={{0,32},{32,0},{64,96},{96,64},{128,160},{160,128},{192,224},{224,1... | collective-permute-start | bytes 589832 | tf_op jit(solution)/shard_map/ppermute | solution.py:174
  65.7 16.1 %collective-permute-start.2 = (bf16[8,24,512]{2,1,0:T(8,128)(2,1)S(1)}, bf16[8,24,512]{2,1,0:T(8,128)(2,1)S(1)}, u32[]{:S(2)}, u32[]{:S(2)}) collective-permute-start(bf16[8,24,512]{2,1,0:T(8,128)(2,1)S(1)} %all_to_all.22.refs_0_), channel_id=1, source_target_pairs={{0,16},{8,24},{16,0},{24,8},{1,17},{9,25},{17,1},{25,9},{2,18},{10... | collective-permute-start | bytes 589832 | tf_op jit(solution)/shard_map/ppermute | solution.py:174
  68.9 14.9 %collective-permute-start.1 = (bf16[8,24,512]{2,1,0:T(8,128)(2,1)S(1)}, bf16[8,24,512]{2,1,0:T(8,128)(2,1)S(1)}, u32[]{:S(2)}, u32[]{:S(2)}) collective-permute-start(bf16[8,24,512]{2,1,0:T(8,128)(2,1)S(1)} %all_to_all.22.refs_0_), channel_id=1, source_target_pairs={{0,24},{8,16},{16,8},{24,0},{1,25},{9,17},{17,9},{25,1},{2,26},{10... | collective-permute-start | bytes 589832 | tf_op jit(solution)/shard_map/ppermute | solution.py:174
  72.9 10.9 %collective-permute-start = (bf16[8,24,512]{2,1,0:T(8,128)(2,1)S(1)}, bf16[8,24,512]{2,1,0:T(8,128)(2,1)S(1)}, u32[]{:S(2)}, u32[]{:S(2)}) collective-permute-start(bf16[8,24,512]{2,1,0:T(8,128)(2,1)S(1)} %all_to_all.22.refs_0_), channel_id=1, source_target_pairs={{0,8},{8,0},{16,24},{24,16},{1,9},{9,1},{17,25},{25,17},{2,10},{10... | collective-permute-start | bytes 589832 | tf_op jit(solution)/shard_map/ppermute | solution.py:174
  75.0 8.8 %collective-permute-start.6 = (bf16[8,24,512]{2,1,0:T(8,128)(2,1)S(1)}, bf16[8,24,512]{2,1,0:T(8,128)(2,1)S(1)}, u32[]{:S(2)}, u32[]{:S(2)}) collective-permute-start(bf16[8,24,512]{2,1,0:T(8,128)(2,1)S(1)} %collective-permute-done.4.refs_5_), channel_id=1, source_target_pairs={{0,8},{8,0},{16,24},{24,16},{1,9},{9,1},{17,25},{25,17},{2,10},{10... | collective-permute-start | bytes 589832 | tf_op jit(solution)/shard_map/ppermute | solution.py:174
  78.7 8.8 %collective-permute-start.5 = (bf16[8,24,512]{2,1,0:T(8,128)(2,1)S(1)}, bf16[8,24,512]{2,1,0:T(8,128)(2,1)S(1)}, u32[]{:S(2)}, u32[]{:S(2)}) collective-permute-start(bf16[8,24,512]{2,1,0:T(8,128)(2,1)S(1)} %collective-permute-done.4.refs_5_), channel_id=1, source_target_pairs={{0,24},{8,16},{16,8},{24,0},{1,25},{9,17},{17,9},{25,1},{2,26},{10... | collective-permute-start | bytes 589832 | tf_op jit(solution)/shard_map/ppermute | solution.py:174
  81.9 7.6 %collective-permute-start.3 = (bf16[8,24,512]{2,1,0:T(8,128)(2,1)S(1)}, bf16[8,24,512]{2,1,0:T(8,128)(2,1)S(1)}, u32[]{:S(2)}, u32[]{:S(2)}) collective-permute-start(bf16[8,24,512]{2,1,0:T(8,128)(2,1)S(1)} %collective-permute-done.2.refs_3_), channel_id=1, source_target_pairs={{0,32},{32,0},{64,96},{96,64},{128,160},{160,128},{192,224},{224,1... | collective-permute-start | bytes 589832 | tf_op jit(solution)/shard_map/ppermute | solution.py:174
  95.5 17.9 %all-to-all-start.3 = ((bf16[8,24,512]{2,1,0:T(8,128)(2,1)}), bf16[8,24,512]{2,1,0:T(8,128)(2,1)S(1)}, u32[]{:S(2)}, u32[]{:S(2)}) async-start(bf16[8,24,512]{2,1,0:T(8,128)(2,1)} %shard_map.45), calls=%async_computation.3 | async-start | bytes 393216 | tf_op jit(solution)/shard_map/all_to_all | solution.py:168

commit v5 on v4

--- a/solution.py
+++ b/solution.py
@@ -1,3 +1,4 @@
+import itertools
 import math
 
 import jax
@@ -168,22 +169,29 @@
     return lax.all_to_all(value, axes, split_axis=0, concat_axis=0, tiled=True, axis_index_groups=groups)
 
 
+def swapped(value, flips):
+    pairs = []
+    for plane, place, core in itertools.product(range(16), range(4), range(2)):
+        over, along = flips[core]
+        target = ((plane ^ over) * 4 + (place ^ along)) * 2 + core
+        pairs.append(((plane * 4 + place) * 2 + core, target))
+    return lax.ppermute(value, ("z", "x", "core"), pairs)
+
+
 def gathered(piece):
-    def swapped(value, axis, flip):
-        size = lax.axis_size(axis)
-        return lax.ppermute(value, axis, [(place, place ^ flip) for place in range(size)])
-
-    side, other_side, far = swapped(piece, "x", 1), swapped(piece, "x", 3), swapped(piece, "x", 2)
-    plane = swapped(piece, "z", 1)
+    first = swapped(piece, ((1, 0), (0, 1)))
+    second = swapped(piece, ((0, 1), (1, 0)))
+    third = swapped(piece, ((0, 2), (0, 3)))
+    fourth = swapped(piece, ((0, 3), (0, 2)))
     return [
         piece,
-        side,
-        other_side,
-        far,
-        swapped(far, "z", 1),
-        plane,
-        swapped(plane, "x", 3),
-        swapped(plane, "x", 1),
+        fourth,
+        third,
+        swapped(third, ((1, 0), (1, 0))),
+        second,
+        swapped(second, ((1, 0), (0, 2))),
+        first,
+        swapped(first, ((0, 3), (1, 0))),
     ]
 
 

time: 115 us -> 116 us (level)
  the two profiles are of different devices: /device:TPU:32 before, /device:TPU:6 now
where the time goes in v5:
time: 116 us; the launch traced here: 115 us
  blocking collectives  59.9 us (52%)
  starting transfers between devices  25.6 us (22%)
  waiting for transfers between devices  19.9 us (17%)
  Pallas kernels  9.33 us (8%)
    all_to_all x3, blocking collectives, exchanged(): lax.all_to_all(value, axes, split_axis=0, concat_axis=0, tiled=True, axis...  59.9 us
    ppermute x7, starting transfers between devices, swapped(): return lax.ppermute(value, ('z', 'x', 'core'), pairs)  22.2 us
    all_to_all x1, waiting for transfers between devices, exchanged(): lax.all_to_all(value, axes, split_axis=0, concat_axis=0, tiled=True, axis...  14.3 us
    pallas_call x6, Pallas kernels, call(): pl.pallas_call(kernel, out_shape=out_shape, in_specs=[pl.BlockSpec(memory...  9.33 us
    ppermute x7, waiting for transfers between devices, swapped(): return lax.ppermute(value, ('z', 'x', 'core'), pairs)  5.63 us
    all_to_all x1, starting transfers between devices, exchanged(): lax.all_to_all(value, axes, split_axis=0, concat_axis=0, tiled=True, axis...  3.39 us
  transfers between devices with their start and end apart: 8, of which 3 were waited for; matrix products, arithmetic and copies ran while one was open for 0% of the time, Pallas kernels for 1%

profile of v5, /device:TPU:6, one launch (start us, length us, event | category | flops | bytes accessed | tf_op | source)
XLA Modules:
  0.0 115.5 jit_solution(1664771625425341670)
XLA Ops:
  0.6 1.3 %shard_map.41 = (f32[32,1,128]{2,1,0:T(1,128)S(1)}, f32[12,8,1024]{2,1,0:T(8,128)S(1)}, f32[12,8,1024]{2,1,0:T(8,128)S(1)}) custom-call(f32[12,8,1024]{2,1,0:T(8,128)} %bitcast.4, f32[12,8,1024]{2,1,0:T(8,128)} %bitcast.5), custom_call_target="tpu_custom_call" | custom-call | tf_op jit(solution)/shard_map/pallas_call | solution.py:36
  1.9 14.1 %all_to_all.20.parts = f32[32,1,128]{2,1,0:T(1,128)S(1)} all-to-all(f32[32,1,128]{2,1,0:T(1,128)S(1)} %get-tuple-element.5), channel_id=1, replica_groups=mesh['z'=16,'x'=4,'y'=4,'core'=2] {'x','y','core'}, dimensions={0} | all-to-all | bytes 32768 | tf_op jit(solution)/shard_map/all_to_all | solution.py:169
  16.0 26.3 %all_to_all.21.total = f32[16,1,128]{2,1,0:T(1,128)S(1)} all-to-all(f32[16,1,128]{2,1,0:T(1,128)S(1)} %shard_map.42), channel_id=1, replica_groups=mesh['z'=16,'x'=4,'y'=4,'core'=2] {'z'}, dimensions={0} | all-to-all | bytes 16384 | tf_op jit(solution)/shard_map/all_to_all | solution.py:169
  42.3 0.2 shard_map.44
  42.5 19.6 %all_to_all.22.refs_0_ = bf16[8,24,512]{2,1,0:T(8,128)(2,1)S(1)} all-to-all(bf16[8,24,512]{2,1,0:T(8,128)(2,1)S(1)} %shard_map.44), channel_id=1, replica_groups={{0,64,128,192,288,352,416,480},{32,96,160,224,256,320,384,448},{1,65,12..., dimensions={0} | all-to-all | bytes 393216 | tf_op jit(solution)/shard_map/all_to_all | solution.py:169
  62.1 1.9 %collective-permute-start.5 = (bf16[8,24,512]{2,1,0:T(8,128)(2,1)S(1)}, bf16[8,24,512]{2,1,0:T(8,128)(2,1)S(1)}, u32[]{:S(2)}, u32[]{:S(2)}) collective-permute-start(bf16[8,24,512]{2,1,0:T(8,128)(2,1)S(1)} %all_to_all.22.refs_0_), channel_id=1, source_target_pairs={{0,32},{1,9},{8,40},{9,1},{16,48},{17,25},{24,56},{25,17},{32,0},{... | collective-permute-start | bytes 589832 | tf_op jit(solution)/shard_map/ppermute | solution.py:178
  64.0 2.6 %collective-permute-start.3 = (bf16[8,24,512]{2,1,0:T(8,128)(2,1)S(1)}, bf16[8,24,512]{2,1,0:T(8,128)(2,1)S(1)}, u32[]{:S(2)}, u32[]{:S(2)}) collective-permute-start(bf16[8,24,512]{2,1,0:T(8,128)(2,1)S(1)} %all_to_all.22.refs_0_), channel_id=1, source_target_pairs={{0,8},{1,33},{8,0},{9,41},{16,24},{17,49},{24,16},{25,57},{32,40},... | collective-permute-start | bytes 589832 | tf_op jit(solution)/shard_map/ppermute | solution.py:178
  66.6 4.8 %collective-permute-start.1 = (bf16[8,24,512]{2,1,0:T(8,128)(2,1)S(1)}, bf16[8,24,512]{2,1,0:T(8,128)(2,1)S(1)}, u32[]{:S(2)}, u32[]{:S(2)}) collective-permute-start(bf16[8,24,512]{2,1,0:T(8,128)(2,1)S(1)} %all_to_all.22.refs_0_), channel_id=1, source_target_pairs={{0,16},{1,25},{8,24},{9,17},{16,0},{17,9},{24,8},{25,1},{32,48},{3... | collective-permute-start | bytes 589832 | tf_op jit(solution)/shard_map/ppermute | solution.py:178
  71.4 3.1 %collective-permute-start = (bf16[8,24,512]{2,1,0:T(8,128)(2,1)S(1)}, bf16[8,24,512]{2,1,0:T(8,128)(2,1)S(1)}, u32[]{:S(2)}, u32[]{:S(2)}) collective-permute-start(bf16[8,24,512]{2,1,0:T(8,128)(2,1)S(1)} %all_to_all.22.refs_0_), channel_id=1, source_target_pairs={{0,24},{1,17},{8,16},{9,25},{16,8},{17,1},{24,0},{25,9},{32,56},{3... | collective-permute-start | bytes 589832 | tf_op jit(solution)/shard_map/ppermute | solution.py:178
  74.5 0.0 collective-permute-done.5.refs_6_
  74.5 4.0 %collective-permute-start.6 = (bf16[8,24,512]{2,1,0:T(8,128)(2,1)S(1)}, bf16[8,24,512]{2,1,0:T(8,128)(2,1)S(1)}, u32[]{:S(2)}, u32[]{:S(2)}) collective-permute-start(bf16[8,24,512]{2,1,0:T(8,128)(2,1)S(1)} %collective-permute-done.5.refs_6_), channel_id=1, source_target_pairs={{0,24},{1,33},{8,16},{9,41},{16,8},{17,49},{24,0},{25,57},{32,56},... | collective-permute-start | bytes 589832 | tf_op jit(solution)/shard_map/ppermute | solution.py:178
  78.5 0.0 collective-permute-done.3.refs_4_
  78.5 3.9 %collective-permute-start.4 = (bf16[8,24,512]{2,1,0:T(8,128)(2,1)S(1)}, bf16[8,24,512]{2,1,0:T(8,128)(2,1)S(1)}, u32[]{:S(2)}, u32[]{:S(2)}) collective-permute-start(bf16[8,24,512]{2,1,0:T(8,128)(2,1)S(1)} %collective-permute-done.3.refs_4_), channel_id=1, source_target_pairs={{0,32},{1,17},{8,40},{9,25},{16,48},{17,1},{24,56},{25,9},{32,0},{... | collective-permute-start | bytes 589832 | tf_op jit(solution)/shard_map/ppermute | solution.py:178
  82.4 0.0 collective-permute-done.1.refs_2_
  82.5 1.9 %collective-permute-start.2 = (bf16[8,24,512]{2,1,0:T(8,128)(2,1)S(1)}, bf16[8,24,512]{2,1,0:T(8,128)(2,1)S(1)}, u32[]{:S(2)}, u32[]{:S(2)}) collective-permute-start(bf16[8,24,512]{2,1,0:T(8,128)(2,1)S(1)} %collective-permute-done.1.refs_2_), channel_id=1, source_target_pairs={{0,32},{1,33},{8,40},{9,41},{16,48},{17,49},{24,56},{25,57},{32,0}... | collective-permute-start | bytes 589832 | tf_op jit(solution)/shard_map/ppermute | solution.py:178
  84.4 0.0 collective-permute-done.refs_1_
  84.4 0.0 collective-permute-done.6.refs_7_
  84.4 1.8 %collective-permute-done.4.refs_5_ = bf16[8,24,512]{2,1,0:T(8,128)(2,1)S(1)} collective-permute-done((bf16[8,24,512]{2,1,0:T(8,128)(2,1)S(1)}, bf16[8,24,512]{2,1,0:T(8,128)(2,1)S(1)}, u32[]{:S(2)}, u32[]{:S(2)}) %collective-permute-start.4) | collective-permute-done | bytes 196640 | tf_op jit(solution)/shard_map/ppermute | solution.py:178
  86.2 3.8 %collective-permute-done.2.refs_3_ = bf16[8,24,512]{2,1,0:T(8,128)(2,1)S(1)} collective-permute-done((bf16[8,24,512]{2,1,0:T(8,128)(2,1)S(1)}, bf16[8,24,512]{2,1,0:T(8,128)(2,1)S(1)}, u32[]{:S(2)}, u32[]{:S(2)}) %collective-permute-start.2) | collective-permute-done | bytes 196640 | tf_op jit(solution)/shard_map/ppermute | solution.py:178
  90.0 6.1 %shard_map.45 = bf16[8,24,512]{2,1,0:T(8,128)(2,1)} custom-call(bf16[8,24,512]{2,1,0:T(8,128)(2,1)S(1)} %all_to_all.22.refs_0_, bf16[8,24,512]{2,1,0:T(8,128)(2,1)S(1)} %collective-permute-done.refs_1_, bf16[8,24,512]{2,1,0:T(8,128)(2,1)S(1)} %collective-permute-done.1.refs_2_, bf16[8,24,512]{2,1,0:T(8,128)(2,1)S(1)} %collective-permute-done.2.refs_3_, ...), custom_call_target="tpu_custom_call" | custom-call | flops 4529848320 | bytes 1572864 | tf_op jit(solution)/shard_map/pallas_call | solution.py:36
  96.1 3.4 %all-to-all-start.3 = ((bf16[8,24,512]{2,1,0:T(8,128)(2,1)}), bf16[8,24,512]{2,1,0:T(8,128)(2,1)S(1)}, u32[]{:S(2)}, u32[]{:S(2)}) async-start(bf16[8,24,512]{2,1,0:T(8,128)(2,1)} %shard_map.45), calls=%async_computation.3 | async-start | bytes 393216 | tf_op jit(solution)/shard_map/all_to_all | solution.py:169
  99.5 0.9 shard_map.43
  100.4 14.3 %all-to-all-done.3.arrived = bf16[8,24,512]{2,1,0:T(8,128)(2,1)S(1)} async-done(((bf16[8,24,512]{2,1,0:T(8,128)(2,1)}), bf16[8,24,512]{2,1,0:T(8,128)(2,1)S(1)}, u32[]{:S(2)}, u32[]{:S(2)}) %all-to-all-start.3) | async-done | bytes 196640 | tf_op jit(solution)/shard_map/all_to_all | solution.py:169
  114.7 0.8 shard_map.46
  (1 shorter events, 0.0 us)
Async XLA Ops:
  62.1 12.4 %collective-permute-start.5 = (bf16[8,24,512]{2,1,0:T(8,128)(2,1)S(1)}, bf16[8,24,512]{2,1,0:T(8,128)(2,1)S(1)}, u32[]{:S(2)}, u32[]{:S(2)}) collective-permute-start(bf16[8,24,512]{2,1,0:T(8,128)(2,1)S(1)} %all_to_all.22.refs_0_), channel_id=1, source_target_pairs={{0,32},{1,9},{8,40},{9,1},{16,48},{17,25},{24,56},{25,17},{32,0},{... | collective-permute-start | bytes 589832 | tf_op jit(solution)/shard_map/ppermute | solution.py:178
  64.0 14.5 %collective-permute-start.3 = (bf16[8,24,512]{2,1,0:T(8,128)(2,1)S(1)}, bf16[8,24,512]{2,1,0:T(8,128)(2,1)S(1)}, u32[]{:S(2)}, u32[]{:S(2)}) collective-permute-start(bf16[8,24,512]{2,1,0:T(8,128)(2,1)S(1)} %all_to_all.22.refs_0_), channel_id=1, source_target_pairs={{0,8},{1,33},{8,0},{9,41},{16,24},{17,49},{24,16},{25,57},{32,40},... | collective-permute-start | bytes 589832 | tf_op jit(solution)/shard_map/ppermute | solution.py:178
  66.6 15.8 %collective-permute-start.1 = (bf16[8,24,512]{2,1,0:T(8,128)(2,1)S(1)}, bf16[8,24,512]{2,1,0:T(8,128)(2,1)S(1)}, u32[]{:S(2)}, u32[]{:S(2)}) collective-permute-start(bf16[8,24,512]{2,1,0:T(8,128)(2,1)S(1)} %all_to_all.22.refs_0_), channel_id=1, source_target_pairs={{0,16},{1,25},{8,24},{9,17},{16,0},{17,9},{24,8},{25,1},{32,48},{3... | collective-permute-start | bytes 589832 | tf_op jit(solution)/shard_map/ppermute | solution.py:178
  71.4 13.0 %collective-permute-start = (bf16[8,24,512]{2,1,0:T(8,128)(2,1)S(1)}, bf16[8,24,512]{2,1,0:T(8,128)(2,1)S(1)}, u32[]{:S(2)}, u32[]{:S(2)}) collective-permute-start(bf16[8,24,512]{2,1,0:T(8,128)(2,1)S(1)} %all_to_all.22.refs_0_), channel_id=1, source_target_pairs={{0,24},{1,17},{8,16},{9,25},{16,8},{17,1},{24,0},{25,9},{32,56},{3... | collective-permute-start | bytes 589832 | tf_op jit(solution)/shard_map/ppermute | solution.py:178
  74.5 9.9 %collective-permute-start.6 = (bf16[8,24,512]{2,1,0:T(8,128)(2,1)S(1)}, bf16[8,24,512]{2,1,0:T(8,128)(2,1)S(1)}, u32[]{:S(2)}, u32[]{:S(2)}) collective-permute-start(bf16[8,24,512]{2,1,0:T(8,128)(2,1)S(1)} %collective-permute-done.5.refs_6_), channel_id=1, source_target_pairs={{0,24},{1,33},{8,16},{9,41},{16,8},{17,49},{24,0},{25,57},{32,56},... | collective-permute-start | bytes 589832 | tf_op jit(solution)/shard_map/ppermute | solution.py:178
  78.5 7.7 %collective-permute-start.4 = (bf16[8,24,512]{2,1,0:T(8,128)(2,1)S(1)}, bf16[8,24,512]{2,1,0:T(8,128)(2,1)S(1)}, u32[]{:S(2)}, u32[]{:S(2)}) collective-permute-start(bf16[8,24,512]{2,1,0:T(8,128)(2,1)S(1)} %collective-permute-done.3.refs_4_), channel_id=1, source_target_pairs={{0,32},{1,17},{8,40},{9,25},{16,48},{17,1},{24,56},{25,9},{32,0},{... | collective-permute-start | bytes 589832 | tf_op jit(solution)/shard_map/ppermute | solution.py:178
  82.5 7.6 %collective-permute-start.2 = (bf16[8,24,512]{2,1,0:T(8,128)(2,1)S(1)}, bf16[8,24,512]{2,1,0:T(8,128)(2,1)S(1)}, u32[]{:S(2)}, u32[]{:S(2)}) collective-permute-start(bf16[8,24,512]{2,1,0:T(8,128)(2,1)S(1)} %collective-permute-done.1.refs_2_), channel_id=1, source_target_pairs={{0,32},{1,33},{8,40},{9,41},{16,48},{17,49},{24,56},{25,57},{32,0}... | collective-permute-start | bytes 589832 | tf_op jit(solution)/shard_map/ppermute | solution.py:178
  96.1 18.6 %all-to-all-start.3 = ((bf16[8,24,512]{2,1,0:T(8,128)(2,1)}), bf16[8,24,512]{2,1,0:T(8,128)(2,1)S(1)}, u32[]{:S(2)}, u32[]{:S(2)}) async-start(bf16[8,24,512]{2,1,0:T(8,128)(2,1)} %shard_map.45), calls=%async_computation.3 | async-start | bytes 393216 | tf_op jit(solution)/shard_map/all_to_all | solution.py:169

commit v6 on v4

--- a/solution.py
+++ b/solution.py
@@ -103,22 +103,24 @@
 
 
 def orthogonal_kernel(*refs):
-    pieces, (out, whole, gram, poly, second) = refs[:MATS], refs[MATS:]
+    pieces, (out, whole, product, gram, poly, second) = refs[:MATS], refs[MATS:]
     rows = FF // MATS
     tiles = [slice(start, start + TILE) for start in range(0, FF, TILE)]
-    squares = jnp.zeros(pieces[0].shape[1:], jnp.float32)
     for number, piece in enumerate(pieces):
-        value = piece[...].astype(jnp.float32)
-        squares += jnp.sum(value * value, axis=0)
-        left, right = unpacked(value)
+        left, right = unpacked(piece[...].astype(jnp.float32))
         place = slice(number * rows, (number + 1) * rows)
         whole[place, :HALF] = left.astype(jnp.bfloat16)
         whole[place, HALF:] = right.astype(jnp.bfloat16)
-    norm_square = jnp.full((1, 1), jnp.sum(squares), jnp.float32)
-    inverse = 1.0 / (jnp.sqrt(norm_square) + NORM_EPS)
-    for tile in tiles:
-        product = dot_transposed(whole[tile, :], whole[...])
-        gram[tile, :] = (product * (inverse * inverse)).astype(jnp.bfloat16)
+    on_diagonal = lax.broadcasted_iota(jnp.int32, (TILE, TILE), 0) == lax.broadcasted_iota(
+        jnp.int32, (TILE, TILE), 1
+    )
+    norm_square = jnp.float32(0.0)
+    for tile in tiles:
+        product[tile, :] = dot_transposed(whole[tile, :], whole[...])
+        norm_square += jnp.sum(jnp.where(on_diagonal, product[tile, tile], 0.0))
+    inverse = 1.0 / (jnp.sqrt(jnp.full((1, 1), norm_square, jnp.float32)) + NORM_EPS)
+    for tile in tiles:
+        gram[tile, :] = (product[tile, :] * (inverse * inverse)).astype(jnp.bfloat16)
     for tile in tiles:
         squared = dot_f32(gram[tile, :], gram[...])
         poly[tile, :] = (COEF_B * gram[tile, :].astype(jnp.float32) + COEF_C * squared).astype(
@@ -154,6 +156,7 @@
         *pieces,
         scratch=[
             pltpu.VMEM((FF, D), jnp.bfloat16),
+            pltpu.VMEM((FF, FF), jnp.float32),
             pltpu.VMEM((FF, FF), jnp.bfloat16),
             pltpu.VMEM((FF, FF), jnp.bfloat16),
             pltpu.VMEM((FF, D), jnp.bfloat16),
@@ -173,17 +176,17 @@
         size = lax.axis_size(axis)
         return lax.ppermute(value, axis, [(place, place ^ flip) for place in range(size)])
 
-    side, other_side, far = swapped(piece, "x", 1), swapped(piece, "x", 3), swapped(piece, "x", 2)
-    plane = swapped(piece, "z", 1)
+    plane, side, other_side = swapped(piece, "z", 1), swapped(piece, "x", 1), swapped(piece, "x", 3)
+    far = swapped(side, "x", 3)
     return [
         piece,
+        other_side,
+        swapped(other_side, "z", 1),
+        plane,
+        swapped(plane, "x", 1),
         side,
-        other_side,
         far,
         swapped(far, "z", 1),
-        plane,
-        swapped(plane, "x", 3),
-        swapped(plane, "x", 1),
     ]
 
 

time: 115 us -> 117 us (1.017)
  the two profiles are of different devices: /device:TPU:32 before, /device:TPU:6 now
where the time goes in v6:
time: 117 us; the launch traced here: 116 us
  blocking collectives  59.9 us (51%)
  starting transfers between devices  23.3 us (20%)
  waiting for transfers between devices  21.8 us (19%)
  Pallas kernels  9.77 us (8%)
    all_to_all x3, blocking collectives, exchanged(): lax.all_to_all(value, axes, split_axis=0, concat_axis=0, tiled=True, axis...  59.9 us
    ppermute x7, starting transfers between devices, swapped(): lax.ppermute(value, axis, [(place, place ^ flip) for place in range(size)])  19.6 us
    all_to_all x1, waiting for transfers between devices, exchanged(): lax.all_to_all(value, axes, split_axis=0, concat_axis=0, tiled=True, axis...  15.2 us
    pallas_call x6, Pallas kernels, call(): pl.pallas_call(kernel, out_shape=out_shape, in_specs=[pl.BlockSpec(memory...  9.77 us
    ppermute x7, waiting for transfers between devices, swapped(): lax.ppermute(value, axis, [(place, place ^ flip) for place in range(size)])  6.6 us
    all_to_all x1, starting transfers between devices, exchanged(): lax.all_to_all(value, axes, split_axis=0, concat_axis=0, tiled=True, axis...  3.67 us
  transfers between devices with their start and end apart: 8, of which 4 were waited for; matrix products, arithmetic and copies ran while one was open for 0% of the time, Pallas kernels for 1%

profile of v6, /device:TPU:6, one launch (start us, length us, event | category | flops | bytes accessed | tf_op | source)
XLA Modules:
  0.0 115.5 jit_solution(10024097734746764476)
XLA Ops:
  0.6 1.3 %shard_map.41 = (f32[32,1,128]{2,1,0:T(1,128)S(1)}, f32[12,8,1024]{2,1,0:T(8,128)S(1)}, f32[12,8,1024]{2,1,0:T(8,128)S(1)}) custom-call(f32[12,8,1024]{2,1,0:T(8,128)} %bitcast.4, f32[12,8,1024]{2,1,0:T(8,128)} %bitcast.5), custom_call_target="tpu_custom_call" | custom-call | tf_op jit(solution)/shard_map/pallas_call | solution.py:35
  1.9 14.1 %all_to_all.20.parts = f32[32,1,128]{2,1,0:T(1,128)S(1)} all-to-all(f32[32,1,128]{2,1,0:T(1,128)S(1)} %get-tuple-element.5), channel_id=1, replica_groups=mesh['z'=16,'x'=4,'y'=4,'core'=2] {'x','y','core'}, dimensions={0} | all-to-all | bytes 32768 | tf_op jit(solution)/shard_map/all_to_all | solution.py:171
  16.0 26.3 %all_to_all.21.total = f32[16,1,128]{2,1,0:T(1,128)S(1)} all-to-all(f32[16,1,128]{2,1,0:T(1,128)S(1)} %shard_map.42), channel_id=1, replica_groups=mesh['z'=16,'x'=4,'y'=4,'core'=2] {'z'}, dimensions={0} | all-to-all | bytes 16384 | tf_op jit(solution)/shard_map/all_to_all | solution.py:171
  42.3 0.2 shard_map.44
  42.5 19.6 %all_to_all.22.refs_0_ = bf16[8,24,512]{2,1,0:T(8,128)(2,1)S(1)} all-to-all(bf16[8,24,512]{2,1,0:T(8,128)(2,1)S(1)} %shard_map.44), channel_id=1, replica_groups={{0,64,128,192,288,352,416,480},{32,96,160,224,256,320,384,448},{1,65,12..., dimensions={0} | all-to-all | bytes 393216 | tf_op jit(solution)/shard_map/all_to_all | solution.py:171
  62.1 2.6 %collective-permute-start.4 = (bf16[8,24,512]{2,1,0:T(8,128)(2,1)S(1)}, bf16[8,24,512]{2,1,0:T(8,128)(2,1)S(1)}, u32[]{:S(2)}, u32[]{:S(2)}) collective-permute-start(bf16[8,24,512]{2,1,0:T(8,128)(2,1)S(1)} %all_to_all.22.refs_0_), channel_id=1, source_target_pairs={{0,8},{8,0},{16,24},{24,16},{1,9},{9,1},{17,25},{25,17},{2,10},{10... | collective-permute-start | bytes 589832 | tf_op jit(solution)/shard_map/ppermute | solution.py:177
  64.7 1.9 %collective-permute-start.2 = (bf16[8,24,512]{2,1,0:T(8,128)(2,1)S(1)}, bf16[8,24,512]{2,1,0:T(8,128)(2,1)S(1)}, u32[]{:S(2)}, u32[]{:S(2)}) collective-permute-start(bf16[8,24,512]{2,1,0:T(8,128)(2,1)S(1)} %all_to_all.22.refs_0_), channel_id=1, source_target_pairs={{0,32},{32,0},{64,96},{96,64},{128,160},{160,128},{192,224},{224,1... | collective-permute-start | bytes 589832 | tf_op jit(solution)/shard_map/ppermute | solution.py:177
  66.6 4.0 %collective-permute-start = (bf16[8,24,512]{2,1,0:T(8,128)(2,1)S(1)}, bf16[8,24,512]{2,1,0:T(8,128)(2,1)S(1)}, u32[]{:S(2)}, u32[]{:S(2)}) collective-permute-start(bf16[8,24,512]{2,1,0:T(8,128)(2,1)S(1)} %all_to_all.22.refs_0_), channel_id=1, source_target_pairs={{0,24},{8,16},{16,8},{24,0},{1,25},{9,17},{17,9},{25,1},{2,26},{10... | collective-permute-start | bytes 589832 | tf_op jit(solution)/shard_map/ppermute | solution.py:177
  70.6 0.0 collective-permute-done.4.refs_5_
  70.6 3.1 %collective-permute-start.5 = (bf16[8,24,512]{2,1,0:T(8,128)(2,1)S(1)}, bf16[8,24,512]{2,1,0:T(8,128)(2,1)S(1)}, u32[]{:S(2)}, u32[]{:S(2)}) collective-permute-start(bf16[8,24,512]{2,1,0:T(8,128)(2,1)S(1)} %collective-permute-done.4.refs_5_), channel_id=1, source_target_pairs={{0,24},{8,16},{16,8},{24,0},{1,25},{9,17},{17,9},{25,1},{2,26},{10... | collective-permute-start | bytes 589832 | tf_op jit(solution)/shard_map/ppermute | solution.py:177
  73.7 0.0 collective-permute-done.2.refs_3_
  73.7 2.1 %collective-permute-start.3 = (bf16[8,24,512]{2,1,0:T(8,128)(2,1)S(1)}, bf16[8,24,512]{2,1,0:T(8,128)(2,1)S(1)}, u32[]{:S(2)}, u32[]{:S(2)}) collective-permute-start(bf16[8,24,512]{2,1,0:T(8,128)(2,1)S(1)} %collective-permute-done.2.refs_3_), channel_id=1, source_target_pairs={{0,8},{8,0},{16,24},{24,16},{1,9},{9,1},{17,25},{25,17},{2,10},{10... | collective-permute-start | bytes 589832 | tf_op jit(solution)/shard_map/ppermute | solution.py:177
  75.8 1.4 %collective-permute-done.refs_1_ = bf16[8,24,512]{2,1,0:T(8,128)(2,1)S(1)} collective-permute-done((bf16[8,24,512]{2,1,0:T(8,128)(2,1)S(1)}, bf16[8,24,512]{2,1,0:T(8,128)(2,1)S(1)}, u32[]{:S(2)}, u32[]{:S(2)}) %collective-permute-start) | collective-permute-done | bytes 196640 | tf_op jit(solution)/shard_map/ppermute | solution.py:177
  77.2 3.6 %collective-permute-start.1 = (bf16[8,24,512]{2,1,0:T(8,128)(2,1)S(1)}, bf16[8,24,512]{2,1,0:T(8,128)(2,1)S(1)}, u32[]{:S(2)}, u32[]{:S(2)}) collective-permute-start(bf16[8,24,512]{2,1,0:T(8,128)(2,1)S(1)} %collective-permute-done.refs_1_), channel_id=1, source_target_pairs={{0,32},{32,0},{64,96},{96,64},{128,160},{160,128},{192,224},{224,1... | collective-permute-start | bytes 589832 | tf_op jit(solution)/shard_map/ppermute | solution.py:177
  80.9 0.0 collective-permute-done.5.refs_6_
  80.9 2.4 %collective-permute-start.6 = (bf16[8,24,512]{2,1,0:T(8,128)(2,1)S(1)}, bf16[8,24,512]{2,1,0:T(8,128)(2,1)S(1)}, u32[]{:S(2)}, u32[]{:S(2)}) collective-permute-start(bf16[8,24,512]{2,1,0:T(8,128)(2,1)S(1)} %collective-permute-done.5.refs_6_), channel_id=1, source_target_pairs={{0,32},{32,0},{64,96},{96,64},{128,160},{160,128},{192,224},{224,1... | collective-permute-start | bytes 589832 | tf_op jit(solution)/shard_map/ppermute | solution.py:177
  83.3 0.0 collective-permute-done.3.refs_4_
  83.3 2.5 %collective-permute-done.1.refs_2_ = bf16[8,24,512]{2,1,0:T(8,128)(2,1)S(1)} collective-permute-done((bf16[8,24,512]{2,1,0:T(8,128)(2,1)S(1)}, bf16[8,24,512]{2,1,0:T(8,128)(2,1)S(1)}, u32[]{:S(2)}, u32[]{:S(2)}) %collective-permute-start.1) | collective-permute-done | bytes 196640 | tf_op jit(solution)/shard_map/ppermute | solution.py:177
  85.7 2.7 %collective-permute-done.6.refs_7_ = bf16[8,24,512]{2,1,0:T(8,128)(2,1)S(1)} collective-permute-done((bf16[8,24,512]{2,1,0:T(8,128)(2,1)S(1)}, bf16[8,24,512]{2,1,0:T(8,128)(2,1)S(1)}, u32[]{:S(2)}, u32[]{:S(2)}) %collective-permute-start.6) | collective-permute-done | bytes 196640 | tf_op jit(solution)/shard_map/ppermute | solution.py:177
  88.4 6.6 %shard_map.45 = bf16[8,24,512]{2,1,0:T(8,128)(2,1)} custom-call(bf16[8,24,512]{2,1,0:T(8,128)(2,1)S(1)} %all_to_all.22.refs_0_, bf16[8,24,512]{2,1,0:T(8,128)(2,1)S(1)} %collective-permute-done.refs_1_, bf16[8,24,512]{2,1,0:T(8,128)(2,1)S(1)} %collective-permute-done.1.refs_2_, bf16[8,24,512]{2,1,0:T(8,128)(2,1)S(1)} %collective-permute-done.2.refs_3_, ...), custom_call_target="tpu_custom_call" | custom-call | flops 4529848320 | bytes 1572864 | tf_op jit(solution)/shard_map/pallas_call | solution.py:35
  95.0 3.7 %all-to-all-start.3 = ((bf16[8,24,512]{2,1,0:T(8,128)(2,1)}), bf16[8,24,512]{2,1,0:T(8,128)(2,1)S(1)}, u32[]{:S(2)}, u32[]{:S(2)}) async-start(bf16[8,24,512]{2,1,0:T(8,128)(2,1)} %shard_map.45), calls=%async_computation.3 | async-start | bytes 393216 | tf_op jit(solution)/shard_map/all_to_all | solution.py:171
  98.7 0.9 shard_map.43
  99.5 15.2 %all-to-all-done.3.arrived = bf16[8,24,512]{2,1,0:T(8,128)(2,1)S(1)} async-done(((bf16[8,24,512]{2,1,0:T(8,128)(2,1)}), bf16[8,24,512]{2,1,0:T(8,128)(2,1)S(1)}, u32[]{:S(2)}, u32[]{:S(2)}) %all-to-all-start.3) | async-done | bytes 196640 | tf_op jit(solution)/shard_map/all_to_all | solution.py:171
  114.7 0.8 shard_map.46
  (1 shorter events, 0.0 us)
Async XLA Ops:
  62.1 8.4 %collective-permute-start.4 = (bf16[8,24,512]{2,1,0:T(8,128)(2,1)S(1)}, bf16[8,24,512]{2,1,0:T(8,128)(2,1)S(1)}, u32[]{:S(2)}, u32[]{:S(2)}) collective-permute-start(bf16[8,24,512]{2,1,0:T(8,128)(2,1)S(1)} %all_to_all.22.refs_0_), channel_id=1, source_target_pairs={{0,8},{8,0},{16,24},{24,16},{1,9},{9,1},{17,25},{25,17},{2,10},{10... | collective-permute-start | bytes 589832 | tf_op jit(solution)/shard_map/ppermute | solution.py:177
  64.7 9.0 %collective-permute-start.2 = (bf16[8,24,512]{2,1,0:T(8,128)(2,1)S(1)}, bf16[8,24,512]{2,1,0:T(8,128)(2,1)S(1)}, u32[]{:S(2)}, u32[]{:S(2)}) collective-permute-start(bf16[8,24,512]{2,1,0:T(8,128)(2,1)S(1)} %all_to_all.22.refs_0_), channel_id=1, source_target_pairs={{0,32},{32,0},{64,96},{96,64},{128,160},{160,128},{192,224},{224,1... | collective-permute-start | bytes 589832 | tf_op jit(solution)/shard_map/ppermute | solution.py:177
  66.6 10.6 %collective-permute-start = (bf16[8,24,512]{2,1,0:T(8,128)(2,1)S(1)}, bf16[8,24,512]{2,1,0:T(8,128)(2,1)S(1)}, u32[]{:S(2)}, u32[]{:S(2)}) collective-permute-start(bf16[8,24,512]{2,1,0:T(8,128)(2,1)S(1)} %all_to_all.22.refs_0_), channel_id=1, source_target_pairs={{0,24},{8,16},{16,8},{24,0},{1,25},{9,17},{17,9},{25,1},{2,26},{10... | collective-permute-start | bytes 589832 | tf_op jit(solution)/shard_map/ppermute | solution.py:177
  70.6 10.3 %collective-permute-start.5 = (bf16[8,24,512]{2,1,0:T(8,128)(2,1)S(1)}, bf16[8,24,512]{2,1,0:T(8,128)(2,1)S(1)}, u32[]{:S(2)}, u32[]{:S(2)}) collective-permute-start(bf16[8,24,512]{2,1,0:T(8,128)(2,1)S(1)} %collective-permute-done.4.refs_5_), channel_id=1, source_target_pairs={{0,24},{8,16},{16,8},{24,0},{1,25},{9,17},{17,9},{25,1},{2,26},{10... | collective-permute-start | bytes 589832 | tf_op jit(solution)/shard_map/ppermute | solution.py:177
  73.7 9.6 %collective-permute-start.3 = (bf16[8,24,512]{2,1,0:T(8,128)(2,1)S(1)}, bf16[8,24,512]{2,1,0:T(8,128)(2,1)S(1)}, u32[]{:S(2)}, u32[]{:S(2)}) collective-permute-start(bf16[8,24,512]{2,1,0:T(8,128)(2,1)S(1)} %collective-permute-done.2.refs_3_), channel_id=1, source_target_pairs={{0,8},{8,0},{16,24},{24,16},{1,9},{9,1},{17,25},{25,17},{2,10},{10... | collective-permute-start | bytes 589832 | tf_op jit(solution)/shard_map/ppermute | solution.py:177
  77.2 8.5 %collective-permute-start.1 = (bf16[8,24,512]{2,1,0:T(8,128)(2,1)S(1)}, bf16[8,24,512]{2,1,0:T(8,128)(2,1)S(1)}, u32[]{:S(2)}, u32[]{:S(2)}) collective-permute-start(bf16[8,24,512]{2,1,0:T(8,128)(2,1)S(1)} %collective-permute-done.refs_1_), channel_id=1, source_target_pairs={{0,32},{32,0},{64,96},{96,64},{128,160},{160,128},{192,224},{224,1... | collective-permute-start | bytes 589832 | tf_op jit(solution)/shard_map/ppermute | solution.py:177
  80.9 7.6 %collective-permute-start.6 = (bf16[8,24,512]{2,1,0:T(8,128)(2,1)S(1)}, bf16[8,24,512]{2,1,0:T(8,128)(2,1)S(1)}, u32[]{:S(2)}, u32[]{:S(2)}) collective-permute-start(bf16[8,24,512]{2,1,0:T(8,128)(2,1)S(1)} %collective-permute-done.5.refs_6_), channel_id=1, source_target_pairs={{0,32},{32,0},{64,96},{96,64},{128,160},{160,128},{192,224},{224,1... | collective-permute-start | bytes 589832 | tf_op jit(solution)/shard_map/ppermute | solution.py:177
  95.0 19.7 %all-to-all-start.3 = ((bf16[8,24,512]{2,1,0:T(8,128)(2,1)}), bf16[8,24,512]{2,1,0:T(8,128)(2,1)S(1)}, u32[]{:S(2)}, u32[]{:S(2)}) async-start(bf16[8,24,512]{2,1,0:T(8,128)(2,1)} %shard_map.45), calls=%async_computation.3 | async-start | bytes 393216 | tf_op jit(solution)/shard_map/all_to_all | solution.py:171

commit v7 on v4

--- a/solution.py
+++ b/solution.py
@@ -67,8 +67,9 @@
     return factor[None]
 
 
-def follow_kernel(total, gradient, decayed, momentum_next):
+def follow_kernel(total, gradient, decayed, momentum_next, stamp):
     momentum_next[...] = decayed[...] + factor_of(total) * gradient[...]
+    stamp[...] = jnp.sum(total[...], axis=0)
 
 
 def blend_kernel(total, gradient, decayed, outgoing):
@@ -103,7 +104,7 @@
 
 
 def orthogonal_kernel(*refs):
-    pieces, (out, whole, gram, poly, second) = refs[:MATS], refs[MATS:]
+    pieces, (_, out, whole, gram, poly, second) = refs[:MATS], refs[MATS:]
     rows = FF // MATS
     tiles = [slice(start, start + TILE) for start in range(0, FF, TILE)]
     squares = jnp.zeros(pieces[0].shape[1:], jnp.float32)
@@ -147,11 +148,12 @@
     out[:, :, HALF:] = jnp.swapaxes(right, 0, 1).astype(jnp.bfloat16)
 
 
-def orthogonal_rows(pieces):
+def orthogonal_rows(pieces, stamp):
     return call(
         orthogonal_kernel,
         jax.ShapeDtypeStruct(pieces[0].shape, jnp.bfloat16),
         *pieces,
+        stamp,
         scratch=[
             pltpu.VMEM((FF, D), jnp.bfloat16),
             pltpu.VMEM((FF, FF), jnp.bfloat16),
@@ -207,8 +209,10 @@
         blend_kernel, jax.ShapeDtypeStruct((MATS, 24, HALF), jnp.bfloat16), squares, kept, decayed
     )
     piece = exchanged(outgoing, "z", PLANES)
-    returning = orthogonal_rows(gathered(piece))
-    momentum_next = call(follow_kernel, whole, squares, kept, decayed)
+    momentum_next, stamp = call(
+        follow_kernel, (whole, jax.ShapeDtypeStruct((1, 128), jnp.float32)), squares, kept, decayed
+    )
+    returning = orthogonal_rows(gathered(piece), stamp)
     arrived = exchanged(returning, "z", PLANES)
     update = call(spread_kernel, jax.ShapeDtypeStruct(shape, jnp.bfloat16), arrived)
     return (jnp.swapaxes(momentum_next, 0, 1), jnp.swapaxes(update, 0, 1))

time: 115 us -> 114 us (level)
  the two profiles are of different devices: /device:TPU:32 before, /device:TPU:6 now
where the time goes in v7:
time: 114 us; the launch traced here: 113 us
  blocking collectives  78.3 us (69%)
  starting transfers between devices  22.8 us (20%)
  Pallas kernels  8.68 us (8%)
  waiting for transfers between devices  2.76 us (2%)
    all_to_all x4, blocking collectives, exchanged(): lax.all_to_all(value, axes, split_axis=0, concat_axis=0, tiled=True, axis...  78.3 us
    ppermute x7, starting transfers between devices, swapped(): lax.ppermute(value, axis, [(place, place ^ flip) for place in range(size)])  22.8 us
    pallas_call x6, Pallas kernels, call(): pl.pallas_call(kernel, out_shape=out_shape, in_specs=[pl.BlockSpec(memory...  8.68 us
    ppermute x7, waiting for transfers between devices, swapped(): lax.ppermute(value, axis, [(place, place ^ flip) for place in range(size)])  2.76 us
  transfers between devices with their start and end apart: 7, of which 1 were waited for; matrix products, arithmetic and copies ran while one was open for 0% of the time, Pallas kernels for 1%

profile of v7, /device:TPU:6, one launch (start us, length us, event | category | flops | bytes accessed | tf_op | source)
XLA Modules:
  0.0 113.2 jit_solution(983914341096065503)
XLA Ops:
  0.6 1.3 %shard_map.41 = (f32[32,1,128]{2,1,0:T(1,128)S(1)}, f32[12,8,1024]{2,1,0:T(8,128)S(1)}, f32[12,8,1024]{2,1,0:T(8,128)S(1)}) custom-call(f32[12,8,1024]{2,1,0:T(8,128)} %bitcast.4, f32[12,8,1024]{2,1,0:T(8,128)} %bitcast.5), custom_call_target="tpu_custom_call" | custom-call | tf_op jit(solution)/shard_map/pallas_call | solution.py:35
  1.9 14.1 %all_to_all.20.parts = f32[32,1,128]{2,1,0:T(1,128)S(1)} all-to-all(f32[32,1,128]{2,1,0:T(1,128)S(1)} %get-tuple-element.7), channel_id=1, replica_groups=mesh['z'=16,'x'=4,'y'=4,'core'=2] {'x','y','core'}, dimensions={0} | all-to-all | bytes 32768 | tf_op jit(solution)/shard_map/all_to_all | solution.py:170
  16.0 26.3 %all_to_all.21.total = f32[16,1,128]{2,1,0:T(1,128)S(1)} all-to-all(f32[16,1,128]{2,1,0:T(1,128)S(1)} %shard_map.42), channel_id=1, replica_groups=mesh['z'=16,'x'=4,'y'=4,'core'=2] {'z'}, dimensions={0} | all-to-all | bytes 16384 | tf_op jit(solution)/shard_map/all_to_all | solution.py:170
  42.3 0.2 shard_map.44
  42.5 19.6 %all_to_all.22.refs_0_ = bf16[8,24,512]{2,1,0:T(8,128)(2,1)S(1)} all-to-all(bf16[8,24,512]{2,1,0:T(8,128)(2,1)S(1)} %shard_map.44), channel_id=1, replica_groups={{0,64,128,192,288,352,416,480},{32,96,160,224,256,320,384,448},{1,65,12..., dimensions={0} | all-to-all | bytes 393216 | tf_op jit(solution)/shard_map/all_to_all | solution.py:170
  62.1 1.9 %collective-permute-start.4 = (bf16[8,24,512]{2,1,0:T(8,128)(2,1)S(1)}, bf16[8,24,512]{2,1,0:T(8,128)(2,1)S(1)}, u32[]{:S(2)}, u32[]{:S(2)}) collective-permute-start(bf16[8,24,512]{2,1,0:T(8,128)(2,1)S(1)} %all_to_all.22.refs_0_), channel_id=1, source_target_pairs={{0,32},{32,0},{64,96},{96,64},{128,160},{160,128},{192,224},{224,1... | collective-permute-start | bytes 589832 | tf_op jit(solution)/shard_map/ppermute | solution.py:176
  64.0 4.0 %collective-permute-start.2 = (bf16[8,24,512]{2,1,0:T(8,128)(2,1)S(1)}, bf16[8,24,512]{2,1,0:T(8,128)(2,1)S(1)}, u32[]{:S(2)}, u32[]{:S(2)}) collective-permute-start(bf16[8,24,512]{2,1,0:T(8,128)(2,1)S(1)} %all_to_all.22.refs_0_), channel_id=1, source_target_pairs={{0,16},{8,24},{16,0},{24,8},{1,17},{9,25},{17,1},{25,9},{2,18},{10... | collective-permute-start | bytes 589832 | tf_op jit(solution)/shard_map/ppermute | solution.py:176
  68.1 3.1 %collective-permute-start.1 = (bf16[8,24,512]{2,1,0:T(8,128)(2,1)S(1)}, bf16[8,24,512]{2,1,0:T(8,128)(2,1)S(1)}, u32[]{:S(2)}, u32[]{:S(2)}) collective-permute-start(bf16[8,24,512]{2,1,0:T(8,128)(2,1)S(1)} %all_to_all.22.refs_0_), channel_id=1, source_target_pairs={{0,24},{8,16},{16,8},{24,0},{1,25},{9,17},{17,9},{25,1},{2,26},{10... | collective-permute-start | bytes 589832 | tf_op jit(solution)/shard_map/ppermute | solution.py:176
  71.2 2.1 %collective-permute-start = (bf16[8,24,512]{2,1,0:T(8,128)(2,1)S(1)}, bf16[8,24,512]{2,1,0:T(8,128)(2,1)S(1)}, u32[]{:S(2)}, u32[]{:S(2)}) collective-permute-start(bf16[8,24,512]{2,1,0:T(8,128)(2,1)S(1)} %all_to_all.22.refs_0_), channel_id=1, source_target_pairs={{0,8},{8,0},{16,24},{24,16},{1,9},{9,1},{17,25},{25,17},{2,10},{10... | collective-permute-start | bytes 589832 | tf_op jit(solution)/shard_map/ppermute | solution.py:176
  73.3 0.0 collective-permute-done.4.refs_5_
  73.3 3.8 %collective-permute-start.6 = (bf16[8,24,512]{2,1,0:T(8,128)(2,1)S(1)}, bf16[8,24,512]{2,1,0:T(8,128)(2,1)S(1)}, u32[]{:S(2)}, u32[]{:S(2)}) collective-permute-start(bf16[8,24,512]{2,1,0:T(8,128)(2,1)S(1)} %collective-permute-done.4.refs_5_), channel_id=1, source_target_pairs={{0,8},{8,0},{16,24},{24,16},{1,9},{9,1},{17,25},{25,17},{2,10},{10... | collective-permute-start | bytes 589832 | tf_op jit(solution)/shard_map/ppermute | solution.py:176
  77.1 4.0 %collective-permute-start.5 = (bf16[8,24,512]{2,1,0:T(8,128)(2,1)S(1)}, bf16[8,24,512]{2,1,0:T(8,128)(2,1)S(1)}, u32[]{:S(2)}, u32[]{:S(2)}) collective-permute-start(bf16[8,24,512]{2,1,0:T(8,128)(2,1)S(1)} %collective-permute-done.4.refs_5_), channel_id=1, source_target_pairs={{0,24},{8,16},{16,8},{24,0},{1,25},{9,17},{17,9},{25,1},{2,26},{10... | collective-permute-start | bytes 589832 | tf_op jit(solution)/shard_map/ppermute | solution.py:176
  81.0 0.0 collective-permute-done.2.refs_3_
  81.0 3.9 %collective-permute-start.3 = (bf16[8,24,512]{2,1,0:T(8,128)(2,1)S(1)}, bf16[8,24,512]{2,1,0:T(8,128)(2,1)S(1)}, u32[]{:S(2)}, u32[]{:S(2)}) collective-permute-start(bf16[8,24,512]{2,1,0:T(8,128)(2,1)S(1)} %collective-permute-done.2.refs_3_), channel_id=1, source_target_pairs={{0,32},{32,0},{64,96},{96,64},{128,160},{160,128},{192,224},{224,1... | collective-permute-start | bytes 589832 | tf_op jit(solution)/shard_map/ppermute | solution.py:176
  85.0 0.9 shard_map.43
  85.8 0.0 collective-permute-done.1.refs_2_
  85.8 0.0 collective-permute-done.refs_1_
  85.8 0.0 collective-permute-done.6.refs_7_
  85.9 0.0 collective-permute-done.5.refs_6_
  85.9 2.7 %collective-permute-done.3.refs_4_ = bf16[8,24,512]{2,1,0:T(8,128)(2,1)S(1)} collective-permute-done((bf16[8,24,512]{2,1,0:T(8,128)(2,1)S(1)}, bf16[8,24,512]{2,1,0:T(8,128)(2,1)S(1)}, u32[]{:S(2)}, u32[]{:S(2)}) %collective-permute-start.3) | collective-permute-done | bytes 196640 | tf_op jit(solution)/shard_map/ppermute | solution.py:176
  88.6 5.5 %shard_map.45 = bf16[8,24,512]{2,1,0:T(8,128)(2,1)S(1)} custom-call(bf16[8,24,512]{2,1,0:T(8,128)(2,1)S(1)} %all_to_all.22.refs_0_, bf16[8,24,512]{2,1,0:T(8,128)(2,1)S(1)} %collective-permute-done.refs_1_, bf16[8,24,512]{2,1,0:T(8,128)(2,1)S(1)} %collective-permute-done.1.refs_2_, bf16[8,24,512]{2,1,0:T(8,128)(2,1)S(1)} %collective-permute-done.2.refs_3_, ...), custom_call_target="tpu_custom_call" | custom-call | flops 4529848320 | bytes 1572864 | tf_op jit(solution)/shard_map/pallas_call | solution.py:35
  94.1 18.4 %all_to_all.23.arrived = bf16[8,24,512]{2,1,0:T(8,128)(2,1)S(1)} all-to-all(bf16[8,24,512]{2,1,0:T(8,128)(2,1)S(1)} %shard_map.45), channel_id=1, replica_groups={{0,64,128,192,288,352,416,480},{32,96,160,224,256,320,384,448},{1,65,12..., dimensions={0} | all-to-all | bytes 393216 | tf_op jit(solution)/shard_map/all_to_all | solution.py:170
  112.5 0.8 shard_map.46
  (1 shorter events, 0.0 us)
Async XLA Ops:
  62.1 11.2 %collective-permute-start.4 = (bf16[8,24,512]{2,1,0:T(8,128)(2,1)S(1)}, bf16[8,24,512]{2,1,0:T(8,128)(2,1)S(1)}, u32[]{:S(2)}, u32[]{:S(2)}) collective-permute-start(bf16[8,24,512]{2,1,0:T(8,128)(2,1)S(1)} %all_to_all.22.refs_0_), channel_id=1, source_target_pairs={{0,32},{32,0},{64,96},{96,64},{128,160},{160,128},{192,224},{224,1... | collective-permute-start | bytes 589832 | tf_op jit(solution)/shard_map/ppermute | solution.py:176
  64.0 17.0 %collective-permute-start.2 = (bf16[8,24,512]{2,1,0:T(8,128)(2,1)S(1)}, bf16[8,24,512]{2,1,0:T(8,128)(2,1)S(1)}, u32[]{:S(2)}, u32[]{:S(2)}) collective-permute-start(bf16[8,24,512]{2,1,0:T(8,128)(2,1)S(1)} %all_to_all.22.refs_0_), channel_id=1, source_target_pairs={{0,16},{8,24},{16,0},{24,8},{1,17},{9,25},{17,1},{25,9},{2,18},{10... | collective-permute-start | bytes 589832 | tf_op jit(solution)/shard_map/ppermute | solution.py:176
  68.1 17.7 %collective-permute-start.1 = (bf16[8,24,512]{2,1,0:T(8,128)(2,1)S(1)}, bf16[8,24,512]{2,1,0:T(8,128)(2,1)S(1)}, u32[]{:S(2)}, u32[]{:S(2)}) collective-permute-start(bf16[8,24,512]{2,1,0:T(8,128)(2,1)S(1)} %all_to_all.22.refs_0_), channel_id=1, source_target_pairs={{0,24},{8,16},{16,8},{24,0},{1,25},{9,17},{17,9},{25,1},{2,26},{10... | collective-permute-start | bytes 589832 | tf_op jit(solution)/shard_map/ppermute | solution.py:176
  71.2 14.6 %collective-permute-start = (bf16[8,24,512]{2,1,0:T(8,128)(2,1)S(1)}, bf16[8,24,512]{2,1,0:T(8,128)(2,1)S(1)}, u32[]{:S(2)}, u32[]{:S(2)}) collective-permute-start(bf16[8,24,512]{2,1,0:T(8,128)(2,1)S(1)} %all_to_all.22.refs_0_), channel_id=1, source_target_pairs={{0,8},{8,0},{16,24},{24,16},{1,9},{9,1},{17,25},{25,17},{2,10},{10... | collective-permute-start | bytes 589832 | tf_op jit(solution)/shard_map/ppermute | solution.py:176
  73.3 12.6 %collective-permute-start.6 = (bf16[8,24,512]{2,1,0:T(8,128)(2,1)S(1)}, bf16[8,24,512]{2,1,0:T(8,128)(2,1)S(1)}, u32[]{:S(2)}, u32[]{:S(2)}) collective-permute-start(bf16[8,24,512]{2,1,0:T(8,128)(2,1)S(1)} %collective-permute-done.4.refs_5_), channel_id=1, source_target_pairs={{0,8},{8,0},{16,24},{24,16},{1,9},{9,1},{17,25},{25,17},{2,10},{10... | collective-permute-start | bytes 589832 | tf_op jit(solution)/shard_map/ppermute | solution.py:176
  77.1 8.8 %collective-permute-start.5 = (bf16[8,24,512]{2,1,0:T(8,128)(2,1)S(1)}, bf16[8,24,512]{2,1,0:T(8,128)(2,1)S(1)}, u32[]{:S(2)}, u32[]{:S(2)}) collective-permute-start(bf16[8,24,512]{2,1,0:T(8,128)(2,1)S(1)} %collective-permute-done.4.refs_5_), channel_id=1, source_target_pairs={{0,24},{8,16},{16,8},{24,0},{1,25},{9,17},{17,9},{25,1},{2,26},{10... | collective-permute-start | bytes 589832 | tf_op jit(solution)/shard_map/ppermute | solution.py:176
  81.0 7.6 %collective-permute-start.3 = (bf16[8,24,512]{2,1,0:T(8,128)(2,1)S(1)}, bf16[8,24,512]{2,1,0:T(8,128)(2,1)S(1)}, u32[]{:S(2)}, u32[]{:S(2)}) collective-permute-start(bf16[8,24,512]{2,1,0:T(8,128)(2,1)S(1)} %collective-permute-done.2.refs_3_), channel_id=1, source_target_pairs={{0,32},{32,0},{64,96},{96,64},{128,160},{160,128},{192,224},{224,1... | collective-permute-start | bytes 589832 | tf_op jit(solution)/shard_map/ppermute | solution.py:176

commit v8 on v7

--- a/solution.py
+++ b/solution.py
@@ -12,6 +12,7 @@
 MATS = 8
 HALF = D // 2
 TILE = 256
+BLOCKS = tuple(tuple(range(start, start + 8)) for start in range(0, 64, 8))
 PLANES = ((0, 2, 4, 6, 9, 11, 13, 15), (1, 3, 5, 7, 8, 10, 12, 14))
 
 
@@ -104,12 +105,12 @@
 
 
 def orthogonal_kernel(*refs):
-    pieces, (_, out, whole, gram, poly, second) = refs[:MATS], refs[MATS:]
+    pieces, _, out, whole, gram, poly, second = refs
     rows = FF // MATS
     tiles = [slice(start, start + TILE) for start in range(0, FF, TILE)]
-    squares = jnp.zeros(pieces[0].shape[1:], jnp.float32)
-    for number, piece in enumerate(pieces):
-        value = piece[...].astype(jnp.float32)
+    squares = jnp.zeros(pieces.shape[2:], jnp.float32)
+    for number in range(MATS):
+        value = pieces[number].astype(jnp.float32)
         squares += jnp.sum(value * value, axis=0)
         left, right = unpacked(value)
         place = slice(number * rows, (number + 1) * rows)
@@ -130,11 +131,13 @@
         second[tile, :] = (inverse * combined).astype(jnp.bfloat16)
     for tile in tiles:
         gram[tile, :] = dot_transposed(second[tile, :], second[...]).astype(jnp.bfloat16)
-    own = gram[:rows, :]
+    member = lax.rem(lax.axis_index("z"), 2) * 4 + lax.axis_index("x")
+    place = pl.ds(pl.multiple_of(member * rows, 32), rows)
+    own = gram[place, :]
     own_poly = (COEF_B * own.astype(jnp.float32) + COEF_C * dot_f32(own, gram[...])).astype(
         jnp.bfloat16
     )
-    combined = COEF_A * second[:rows, :].astype(jnp.float32) + dot_f32(own_poly, second[...])
+    combined = COEF_A * second[place, :].astype(jnp.float32) + dot_f32(own_poly, second[...])
     scaled = 0.2 * math.sqrt(max(FF, D)) * combined
     for number, block in enumerate(packed_blocks(scaled[:, :HALF], scaled[:, HALF:])):
         out[number] = block.astype(jnp.bfloat16)
@@ -151,8 +154,8 @@
 def orthogonal_rows(pieces, stamp):
     return call(
         orthogonal_kernel,
-        jax.ShapeDtypeStruct(pieces[0].shape, jnp.bfloat16),
-        *pieces,
+        jax.ShapeDtypeStruct(pieces.shape[1:], jnp.bfloat16),
+        pieces,
         stamp,
         scratch=[
             pltpu.VMEM((FF, D), jnp.bfloat16),
@@ -171,22 +174,7 @@
 
 
 def gathered(piece):
-    def swapped(value, axis, flip):
-        size = lax.axis_size(axis)
-        return lax.ppermute(value, axis, [(place, place ^ flip) for place in range(size)])
-
-    side, other_side, far = swapped(piece, "x", 1), swapped(piece, "x", 3), swapped(piece, "x", 2)
-    plane = swapped(piece, "z", 1)
-    return [
-        piece,
-        side,
-        other_side,
-        far,
-        swapped(far, "z", 1),
-        plane,
-        swapped(plane, "x", 3),
-        swapped(plane, "x", 1),
-    ]
+    return exchanged(jnp.broadcast_to(piece[None], (MATS, *piece.shape)), ("z", "x"), BLOCKS)
 
 
 def local(gradient, momentum):

time: 114 us -> 114 us (level)
  the two profiles are of different devices: /device:TPU:6 before, /device:TPU:32 now
where the time goes in v8:
time: 114 us
  blocking collectives  80.3 us (70%)
  waiting for transfers between devices  16.7 us (15%)
  Pallas kernels  8.95 us (8%)
  starting transfers between devices  6.1 us (5%)
  local copies, waits for them, and re-layouts  1.3 us (1%)
    all_to_all x4, blocking collectives, exchanged(): lax.all_to_all(value, axes, split_axis=0, concat_axis=0, tiled=True, axis...  80.3 us
    all_to_all x1, waiting for transfers between devices, exchanged(): lax.all_to_all(value, axes, split_axis=0, concat_axis=0, tiled=True, axis...  16.7 us
    pallas_call x6, Pallas kernels, call(): pl.pallas_call(kernel, out_shape=out_shape, in_specs=[pl.BlockSpec(memory...  8.95 us
    all_to_all x1, starting transfers between devices, exchanged(): lax.all_to_all(value, axes, split_axis=0, concat_axis=0, tiled=True, axis...  6.1 us
  transfers between devices with their start and end apart: 1, of which 1 were waited for; matrix products, arithmetic and copies ran while one was open for 0% of the time, Pallas kernels for 1%

profile of v8, /device:TPU:32, one launch (start us, length us, event | category | flops | bytes accessed | tf_op | source)
XLA Modules:
  0.0 114.1 jit_solution(13505209574227653538)
XLA Ops:
  0.6 1.3 %shard_map.41 = (f32[32,1,128]{2,1,0:T(1,128)S(1)}, f32[12,8,1024]{2,1,0:T(8,128)S(1)}, f32[12,8,1024]{2,1,0:T(8,128)S(1)}) custom-call(f32[12,8,1024]{2,1,0:T(8,128)} %bitcast.4, f32[12,8,1024]{2,1,0:T(8,128)} %bitcast.5), custom_call_target="tpu_custom_call" | custom-call | tf_op jit(solution)/shard_map/pallas_call | solution.py:36
  1.9 14.5 %all_to_all.25.parts = f32[32,1,128]{2,1,0:T(1,128)S(1)} all-to-all(f32[32,1,128]{2,1,0:T(1,128)S(1)} %get-tuple-element.7), channel_id=1, replica_groups=mesh['z'=16,'x'=4,'y'=4,'core'=2] {'x','y','core'}, dimensions={0} | all-to-all | bytes 32768 | tf_op jit(solution)/shard_map/all_to_all | solution.py:173
  16.4 26.1 %all_to_all.26.total = f32[16,1,128]{2,1,0:T(1,128)S(1)} all-to-all(f32[16,1,128]{2,1,0:T(1,128)S(1)} %shard_map.42), channel_id=1, replica_groups=mesh['z'=16,'x'=4,'y'=4,'core'=2] {'z'}, dimensions={0} | all-to-all | bytes 16384 | tf_op jit(solution)/shard_map/all_to_all | solution.py:173
  42.6 0.2 shard_map.44
  42.8 18.4 %all_to_all.27 = bf16[8,24,512]{2,1,0:T(8,128)(2,1)S(1)} all-to-all(bf16[8,24,512]{2,1,0:T(8,128)(2,1)S(1)} %shard_map.44), channel_id=1, replica_groups={{0,64,128,192,288,352,416,480},{32,96,160,224,256,320,384,448},{1,65,12..., dimensions={0} | all-to-all | bytes 393216 | tf_op jit(solution)/shard_map/all_to_all | solution.py:173
  61.2 1.3 %broadcast_in_dim.2 = bf16[8,8,24,512]{3,2,1,0:T(8,128)(2,1)} broadcast(bf16[8,24,512]{2,1,0:T(8,128)(2,1)S(1)} %all_to_all.27), dimensions={1,2,3} | broadcast | bytes 1769472 | tf_op jit(solution)/shard_map/broadcast_in_dim | solution.py:177
  62.5 6.1 %all-to-all-start.3 = ((bf16[8,8,24,512]{3,2,1,0:T(8,128)(2,1)}), bf16[8,8,24,512]{3,2,1,0:T(8,128)(2,1)S(1)}, u32[]{:S(2)}, u32[]{:S(2)}) async-start(bf16[8,8,24,512]{3,2,1,0:T(8,128)(2,1)} %broadcast_in_dim.2), calls=%async_computation.3 | async-start | bytes 3145728 | tf_op jit(solution)/shard_map/all_to_all | solution.py:173
  68.7 0.9 shard_map.43
  69.5 16.7 %all-to-all-done.3.refs_0_ = bf16[8,8,24,512]{3,2,1,0:T(8,128)(2,1)S(1)} async-done(((bf16[8,8,24,512]{3,2,1,0:T(8,128)(2,1)}), bf16[8,8,24,512]{3,2,1,0:T(8,128)(2,1)S(1)}, u32[]{:S(2)}, u32[]{:S(2)}) %all-to-all-start.3) | async-done | bytes 1572896 | tf_op jit(solution)/shard_map/all_to_all | solution.py:173
  86.3 5.7 %shard_map.45 = bf16[8,24,512]{2,1,0:T(8,128)(2,1)S(1)} custom-call(bf16[8,8,24,512]{3,2,1,0:T(8,128)(2,1)S(1)} %all-to-all-done.3.refs_0_, f32[1,128]{1,0:T(1,128)S(1)} %get-tuple-element.11.refs_1_), custom_call_target="tpu_custom_call" | custom-call | flops 4529848320 | bytes 1572864 | tf_op jit(solution)/shard_map/pallas_call | solution.py:36
  92.0 21.3 %all_to_all.28.arrived = bf16[8,24,512]{2,1,0:T(8,128)(2,1)S(1)} all-to-all(bf16[8,24,512]{2,1,0:T(8,128)(2,1)S(1)} %shard_map.45), channel_id=1, replica_groups={{0,64,128,192,288,352,416,480},{32,96,160,224,256,320,384,448},{1,65,12..., dimensions={0} | all-to-all | bytes 393216 | tf_op jit(solution)/shard_map/all_to_all | solution.py:173
  113.3 0.8 shard_map.46
  (1 shorter events, 0.0 us)
Async XLA Ops:
  62.5 23.7 %all-to-all-start.3 = ((bf16[8,8,24,512]{3,2,1,0:T(8,128)(2,1)}), bf16[8,8,24,512]{3,2,1,0:T(8,128)(2,1)S(1)}, u32[]{:S(2)}, u32[]{:S(2)}) async-start(bf16[8,8,24,512]{3,2,1,0:T(8,128)(2,1)} %broadcast_in_dim.2), calls=%async_computation.3 | async-start | bytes 3145728 | tf_op jit(solution)/shard_map/all_to_all | solution.py:173

commit v9 on v8

--- a/solution.py
+++ b/solution.py
@@ -81,6 +81,10 @@
     outgoing[...] = packed.astype(jnp.bfloat16)
 
 
+def copy_kernel(piece, out):
+    out[...] = jnp.broadcast_to(piece[...][None], out.shape)
+
+
 def unpacked(value):
     left, right = [], []
     for number in range(0, MATS, 2):
@@ -109,13 +113,19 @@
     rows = FF // MATS
     tiles = [slice(start, start + TILE) for start in range(0, FF, TILE)]
     squares = jnp.zeros(pieces.shape[2:], jnp.float32)
-    for number in range(MATS):
-        value = pieces[number].astype(jnp.float32)
-        squares += jnp.sum(value * value, axis=0)
+    member = lax.rem(lax.axis_index("z"), 2) * 4 + lax.axis_index("x")
+
+    def place(source, start):
+        value = pieces[source].astype(jnp.float32)
         left, right = unpacked(value)
-        place = slice(number * rows, (number + 1) * rows)
-        whole[place, :HALF] = left.astype(jnp.bfloat16)
-        whole[place, HALF:] = right.astype(jnp.bfloat16)
+        whole[pl.ds(start, rows), :HALF] = left.astype(jnp.bfloat16)
+        whole[pl.ds(start, rows), HALF:] = right.astype(jnp.bfloat16)
+        return jnp.sum(value * value, axis=0)
+
+    for number in range(1, MATS):
+        squares += place(number, number * rows)
+    squares += place(0, pl.multiple_of(member * rows, 32))
+    place(member, 0)
     norm_square = jnp.full((1, 1), jnp.sum(squares), jnp.float32)
     inverse = 1.0 / (jnp.sqrt(norm_square) + NORM_EPS)
     for tile in tiles:
@@ -131,13 +141,11 @@
         second[tile, :] = (inverse * combined).astype(jnp.bfloat16)
     for tile in tiles:
         gram[tile, :] = dot_transposed(second[tile, :], second[...]).astype(jnp.bfloat16)
-    member = lax.rem(lax.axis_index("z"), 2) * 4 + lax.axis_index("x")
-    place = pl.ds(pl.multiple_of(member * rows, 32), rows)
-    own = gram[place, :]
+    own = gram[:rows, :]
     own_poly = (COEF_B * own.astype(jnp.float32) + COEF_C * dot_f32(own, gram[...])).astype(
         jnp.bfloat16
     )
-    combined = COEF_A * second[place, :].astype(jnp.float32) + dot_f32(own_poly, second[...])
+    combined = COEF_A * second[:rows, :].astype(jnp.float32) + dot_f32(own_poly, second[...])
     scaled = 0.2 * math.sqrt(max(FF, D)) * combined
     for number, block in enumerate(packed_blocks(scaled[:, :HALF], scaled[:, HALF:])):
         out[number] = block.astype(jnp.bfloat16)
@@ -174,7 +182,8 @@
 
 
 def gathered(piece):
-    return exchanged(jnp.broadcast_to(piece[None], (MATS, *piece.shape)), ("z", "x"), BLOCKS)
+    copies = call(copy_kernel, jax.ShapeDtypeStruct((MATS, *piece.shape), piece.dtype), piece)
+    return exchanged(copies, ("z", "x"), BLOCKS)
 
 
 def local(gradient, momentum):

time: 114 us -> 114 us (level)
  local copies, waits for them, and re-layouts: 1.3 us -> 0 us
  Pallas kernels: 8.95 us -> 10.1 us
    broadcast_in_dim x1 -> x0, local copies, waits for them, and re-layouts: 1.3 us -> none  [gathered(): jnp.broadcast_to(piece[None], (MATS, *piece.shape))]
    pallas_call x6 -> x7, Pallas kernels: 8.95 us -> 10.1 us  [call(): pl.pallas_call(kernel, out_shape=out_shape, in_specs=[pl.BlockSpec(memory...]
where the time goes in v9:
time: 114 us
  blocking collectives  80.3 us (70%)
  waiting for transfers between devices  16.7 us (15%)
  Pallas kernels  10.1 us (9%)
  starting transfers between devices  6.1 us (5%)
    all_to_all x4, blocking collectives, exchanged(): lax.all_to_all(value, axes, split_axis=0, concat_axis=0, tiled=True, axis...  80.3 us
    all_to_all x1, waiting for transfers between devices, exchanged(): lax.all_to_all(value, axes, split_axis=0, concat_axis=0, tiled=True, axis...  16.7 us
    pallas_call x7, Pallas kernels, call(): pl.pallas_call(kernel, out_shape=out_shape, in_specs=[pl.BlockSpec(memory...  10.1 us
    all_to_all x1, starting transfers between devices, exchanged(): lax.all_to_all(value, axes, split_axis=0, concat_axis=0, tiled=True, axis...  6.1 us
  transfers between devices with their start and end apart: 1, of which 1 were waited for; matrix products, arithmetic and copies ran while one was open for 0% of the time, Pallas kernels for 1%

profile of v9, /device:TPU:32, one launch (start us, length us, event | category | flops | bytes accessed | tf_op | source)
XLA Modules:
  0.0 113.9 jit_solution(11350251212534663076)
XLA Ops:
  0.6 1.3 %shard_map.41 = (f32[32,1,128]{2,1,0:T(1,128)S(1)}, f32[12,8,1024]{2,1,0:T(8,128)S(1)}, f32[12,8,1024]{2,1,0:T(8,128)S(1)}) custom-call(f32[12,8,1024]{2,1,0:T(8,128)} %bitcast.4, f32[12,8,1024]{2,1,0:T(8,128)} %bitcast.5), custom_call_target="tpu_custom_call" | custom-call | tf_op jit(solution)/shard_map/pallas_call | solution.py:36
  1.9 14.5 %all_to_all.25.parts = f32[32,1,128]{2,1,0:T(1,128)S(1)} all-to-all(f32[32,1,128]{2,1,0:T(1,128)S(1)} %get-tuple-element.7), channel_id=1, replica_groups=mesh['z'=16,'x'=4,'y'=4,'core'=2] {'x','y','core'}, dimensions={0} | all-to-all | bytes 32768 | tf_op jit(solution)/shard_map/all_to_all | solution.py:181
  16.4 26.1 %all_to_all.26.total = f32[16,1,128]{2,1,0:T(1,128)S(1)} all-to-all(f32[16,1,128]{2,1,0:T(1,128)S(1)} %shard_map.42), channel_id=1, replica_groups=mesh['z'=16,'x'=4,'y'=4,'core'=2] {'z'}, dimensions={0} | all-to-all | bytes 16384 | tf_op jit(solution)/shard_map/all_to_all | solution.py:181
  42.6 0.2 shard_map.44
  42.8 18.4 %all_to_all.27.piece = bf16[8,24,512]{2,1,0:T(8,128)(2,1)S(1)} all-to-all(bf16[8,24,512]{2,1,0:T(8,128)(2,1)S(1)} %shard_map.44), channel_id=1, replica_groups={{0,64,128,192,288,352,416,480},{32,96,160,224,256,320,384,448},{1,65,12..., dimensions={0} | all-to-all | bytes 393216 | tf_op jit(solution)/shard_map/all_to_all | solution.py:181
  61.2 1.3 %shard_map.45 = bf16[8,8,24,512]{3,2,1,0:T(8,128)(2,1)} custom-call(bf16[8,24,512]{2,1,0:T(8,128)(2,1)S(1)} %all_to_all.27.piece), custom_call_target="tpu_custom_call" | custom-call | tf_op jit(solution)/shard_map/pallas_call | solution.py:36
  62.5 6.1 %all-to-all-start.3 = ((bf16[8,8,24,512]{3,2,1,0:T(8,128)(2,1)}), bf16[8,8,24,512]{3,2,1,0:T(8,128)(2,1)S(1)}, u32[]{:S(2)}, u32[]{:S(2)}) async-start(bf16[8,8,24,512]{3,2,1,0:T(8,128)(2,1)} %shard_map.45), calls=%async_computation.3 | async-start | bytes 3145728 | tf_op jit(solution)/shard_map/all_to_all | solution.py:181
  68.6 0.9 shard_map.43
  69.5 16.7 %all-to-all-done.3.refs_0_ = bf16[8,8,24,512]{3,2,1,0:T(8,128)(2,1)S(1)} async-done(((bf16[8,8,24,512]{3,2,1,0:T(8,128)(2,1)}), bf16[8,8,24,512]{3,2,1,0:T(8,128)(2,1)S(1)}, u32[]{:S(2)}, u32[]{:S(2)}) %all-to-all-start.3) | async-done | bytes 1572896 | tf_op jit(solution)/shard_map/all_to_all | solution.py:181
  86.2 5.6 %shard_map.46 = bf16[8,24,512]{2,1,0:T(8,128)(2,1)S(1)} custom-call(bf16[8,8,24,512]{3,2,1,0:T(8,128)(2,1)S(1)} %all-to-all-done.3.refs_0_, f32[1,128]{1,0:T(1,128)S(1)} %get-tuple-element.11.refs_1_), custom_call_target="tpu_custom_call" | custom-call | flops 4529848320 | bytes 1572864 | tf_op jit(solution)/shard_map/pallas_call | solution.py:36
  91.8 21.3 %all_to_all.28.arrived = bf16[8,24,512]{2,1,0:T(8,128)(2,1)S(1)} all-to-all(bf16[8,24,512]{2,1,0:T(8,128)(2,1)S(1)} %shard_map.46), channel_id=1, replica_groups={{0,64,128,192,288,352,416,480},{32,96,160,224,256,320,384,448},{1,65,12..., dimensions={0} | all-to-all | bytes 393216 | tf_op jit(solution)/shard_map/all_to_all | solution.py:181
  113.1 0.8 shard_map.47
  (1 shorter events, 0.0 us)
Async XLA Ops:
  62.5 23.7 %all-to-all-start.3 = ((bf16[8,8,24,512]{3,2,1,0:T(8,128)(2,1)}), bf16[8,8,24,512]{3,2,1,0:T(8,128)(2,1)S(1)}, u32[]{:S(2)}, u32[]{:S(2)}) async-start(bf16[8,8,24,512]{3,2,1,0:T(8,128)(2,1)} %shard_map.45), calls=%async_computation.3 | async-start | bytes 3145728 | tf_op jit(solution)/shard_map/all_to_all | solution.py:181

commit v10 on v9

--- a/solution.py
+++ b/solution.py
@@ -68,11 +68,6 @@
     return factor[None]
 
 
-def follow_kernel(total, gradient, decayed, momentum_next, stamp):
-    momentum_next[...] = decayed[...] + factor_of(total) * gradient[...]
-    stamp[...] = jnp.sum(total[...], axis=0)
-
-
 def blend_kernel(total, gradient, decayed, outgoing):
     scaled = factor_of(total) * gradient[...]
     blended = jnp.swapaxes(scaled + MOMENTUM_RATE * (decayed[...] + scaled), 0, 1)
@@ -109,7 +104,7 @@
 
 
 def orthogonal_kernel(*refs):
-    pieces, _, out, whole, gram, poly, second = refs
+    pieces, out, whole, gram, poly, second = refs
     rows = FF // MATS
     tiles = [slice(start, start + TILE) for start in range(0, FF, TILE)]
     squares = jnp.zeros(pieces.shape[2:], jnp.float32)
@@ -151,7 +146,8 @@
         out[number] = block.astype(jnp.bfloat16)
 
 
-def spread_kernel(arrived, out):
+def finish_kernel(total, gradient, decayed, arrived, momentum_next, out):
+    momentum_next[...] = decayed[...] + factor_of(total) * gradient[...]
     value = arrived[...].astype(jnp.float32)
     left = jnp.concatenate([value[:, :8], value[:, 16:20]], axis=1)
     right = jnp.concatenate([value[:, 8:16], value[:, 20:]], axis=1)
@@ -159,12 +155,11 @@
     out[:, :, HALF:] = jnp.swapaxes(right, 0, 1).astype(jnp.bfloat16)
 
 
-def orthogonal_rows(pieces, stamp):
+def orthogonal_rows(pieces):
     return call(
         orthogonal_kernel,
         jax.ShapeDtypeStruct(pieces.shape[1:], jnp.bfloat16),
         pieces,
-        stamp,
         scratch=[
             pltpu.VMEM((FF, D), jnp.bfloat16),
             pltpu.VMEM((FF, FF), jnp.bfloat16),
@@ -206,12 +201,16 @@
         blend_kernel, jax.ShapeDtypeStruct((MATS, 24, HALF), jnp.bfloat16), squares, kept, decayed
     )
     piece = exchanged(outgoing, "z", PLANES)
-    momentum_next, stamp = call(
-        follow_kernel, (whole, jax.ShapeDtypeStruct((1, 128), jnp.float32)), squares, kept, decayed
-    )
-    returning = orthogonal_rows(gathered(piece), stamp)
+    returning = orthogonal_rows(gathered(piece))
     arrived = exchanged(returning, "z", PLANES)
-    update = call(spread_kernel, jax.ShapeDtypeStruct(shape, jnp.bfloat16), arrived)
+    momentum_next, update = call(
+        finish_kernel,
+        (whole, jax.ShapeDtypeStruct(shape, jnp.bfloat16)),
+        squares,
+        kept,
+        decayed,
+        arrived,
+    )
     return (jnp.swapaxes(momentum_next, 0, 1), jnp.swapaxes(update, 0, 1))
 
 

time: 114 us -> 111 us (0.974)
  the two profiles are of different devices: /device:TPU:32 before, /device:TPU:6 now
where the time goes in v10:
time: 111 us; the launch traced here: 110 us
  blocking collectives  101 us (91%)
  Pallas kernels  8.23 us (7%)
    all_to_all x5, blocking collectives, exchanged(): lax.all_to_all(value, axes, split_axis=0, concat_axis=0, tiled=True, axis...  101 us
    pallas_call x6, Pallas kernels, call(): pl.pallas_call(kernel, out_shape=out_shape, in_specs=[pl.BlockSpec(memory...  8.23 us

profile of v10, /device:TPU:6, one launch (start us, length us, event | category | flops | bytes accessed | tf_op | source)
XLA Modules:
  0.0 109.9 jit_solution(2937311637270986165)
XLA Ops:
  0.6 1.3 %shard_map.41 = (f32[32,1,128]{2,1,0:T(1,128)S(1)}, f32[12,8,1024]{2,1,0:T(8,128)S(1)}, f32[12,8,1024]{2,1,0:T(8,128)S(1)}) custom-call(f32[12,8,1024]{2,1,0:T(8,128)} %bitcast.4, f32[12,8,1024]{2,1,0:T(8,128)} %bitcast.5), custom_call_target="tpu_custom_call" | custom-call | tf_op jit(solution)/shard_map/pallas_call | solution.py:36
  1.9 14.1 %all_to_all.25.parts = f32[32,1,128]{2,1,0:T(1,128)S(1)} all-to-all(f32[32,1,128]{2,1,0:T(1,128)S(1)} %get-tuple-element.7), channel_id=1, replica_groups=mesh['z'=16,'x'=4,'y'=4,'core'=2] {'x','y','core'}, dimensions={0} | all-to-all | bytes 32768 | tf_op jit(solution)/shard_map/all_to_all | solution.py:176
  16.0 26.3 %all_to_all.26.total = f32[16,1,128]{2,1,0:T(1,128)S(1)} all-to-all(f32[16,1,128]{2,1,0:T(1,128)S(1)} %shard_map.42), channel_id=1, replica_groups=mesh['z'=16,'x'=4,'y'=4,'core'=2] {'z'}, dimensions={0} | all-to-all | bytes 16384 | tf_op jit(solution)/shard_map/all_to_all | solution.py:176
  42.3 0.2 shard_map.43
  42.5 19.6 %all_to_all.27.piece = bf16[8,24,512]{2,1,0:T(8,128)(2,1)S(1)} all-to-all(bf16[8,24,512]{2,1,0:T(8,128)(2,1)S(1)} %shard_map.43), channel_id=1, replica_groups={{0,64,128,192,288,352,416,480},{32,96,160,224,256,320,384,448},{1,65,12..., dimensions={0} | all-to-all | bytes 393216 | tf_op jit(solution)/shard_map/all_to_all | solution.py:176
  62.1 0.1 shard_map.44
  62.2 21.1 %all_to_all.28.refs_0_ = bf16[8,8,24,512]{3,2,1,0:T(8,128)(2,1)S(1)} all-to-all(bf16[8,8,24,512]{3,2,1,0:T(8,128)(2,1)S(1)} %shard_map.44), channel_id=1, replica_groups={{0,8,16,24,32,40,48,56},{64,72,80,88,96,104,112,120},{128,136,144,152,1..., dimensions={0} | all-to-all | bytes 3145728 | tf_op jit(solution)/shard_map/all_to_all | solution.py:176
  83.3 5.6 %shard_map.45 = bf16[8,24,512]{2,1,0:T(8,128)(2,1)S(1)} custom-call(bf16[8,8,24,512]{3,2,1,0:T(8,128)(2,1)S(1)} %all_to_all.28.refs_0_), custom_call_target="tpu_custom_call" | custom-call | flops 4529848320 | bytes 1572864 | tf_op jit(solution)/shard_map/pallas_call | solution.py:36
  88.9 20.0 %all_to_all.29.arrived = bf16[8,24,512]{2,1,0:T(8,128)(2,1)S(1)} all-to-all(bf16[8,24,512]{2,1,0:T(8,128)(2,1)S(1)} %shard_map.45), channel_id=1, replica_groups={{0,64,128,192,288,352,416,480},{32,96,160,224,256,320,384,448},{1,65,12..., dimensions={0} | all-to-all | bytes 393216 | tf_op jit(solution)/shard_map/all_to_all | solution.py:176
  109.0 0.9 shard_map.46
  (1 shorter events, 0.0 us)

commit v11 on v10

--- a/solution.py
+++ b/solution.py
@@ -77,16 +77,16 @@
 
 
 def copy_kernel(piece, out):
-    out[...] = jnp.broadcast_to(piece[...][None], out.shape)
-
-
-def unpacked(value):
+    value = piece[...].astype(jnp.float32)
     left, right = [], []
     for number in range(0, MATS, 2):
         first, second = value[number], value[number + 1]
         left += [first[:8], second[:8], first[16:20], second[16:20]]
         right += [first[8:16], second[8:16], first[20:], second[20:]]
-    return jnp.concatenate(left, axis=0), jnp.concatenate(right, axis=0)
+    for start, parts in ((0, left), (HALF, right)):
+        half = jnp.concatenate(parts, axis=0).astype(jnp.bfloat16)
+        for number in range(MATS):
+            out[number, :, start : start + HALF] = half
 
 
 def packed_blocks(left, right):
@@ -103,44 +103,36 @@
     return blocks
 
 
-def orthogonal_kernel(*refs):
-    pieces, out, whole, gram, poly, second = refs
+def orthogonal_kernel(whole, out, gram, poly, second):
     rows = FF // MATS
     tiles = [slice(start, start + TILE) for start in range(0, FF, TILE)]
-    squares = jnp.zeros(pieces.shape[2:], jnp.float32)
-    member = lax.rem(lax.axis_index("z"), 2) * 4 + lax.axis_index("x")
-
-    def place(source, start):
-        value = pieces[source].astype(jnp.float32)
-        left, right = unpacked(value)
-        whole[pl.ds(start, rows), :HALF] = left.astype(jnp.bfloat16)
-        whole[pl.ds(start, rows), HALF:] = right.astype(jnp.bfloat16)
-        return jnp.sum(value * value, axis=0)
-
-    for number in range(1, MATS):
-        squares += place(number, number * rows)
-    squares += place(0, pl.multiple_of(member * rows, 32))
-    place(member, 0)
-    norm_square = jnp.full((1, 1), jnp.sum(squares), jnp.float32)
-    inverse = 1.0 / (jnp.sqrt(norm_square) + NORM_EPS)
+    on_diagonal = lax.broadcasted_iota(jnp.int32, (TILE, TILE), 0) == lax.broadcasted_iota(
+        jnp.int32, (TILE, TILE), 1
+    )
+    norm_square = jnp.float32(0.0)
     for tile in tiles:
         product = dot_transposed(whole[tile, :], whole[...])
-        gram[tile, :] = (product * (inverse * inverse)).astype(jnp.bfloat16)
-    for tile in tiles:
-        squared = dot_f32(gram[tile, :], gram[...])
-        poly[tile, :] = (COEF_B * gram[tile, :].astype(jnp.float32) + COEF_C * squared).astype(
-            jnp.bfloat16
-        )
+        norm_square += jnp.sum(jnp.where(on_diagonal, product[:, tile], 0.0))
+        gram[tile, :] = product.astype(jnp.bfloat16)
+    inverse = 1.0 / (jnp.sqrt(jnp.full((1, 1), norm_square, jnp.float32)) + NORM_EPS)
+    scale = inverse * inverse
+    for tile in tiles:
+        squared = scale * dot_f32(gram[tile, :], gram[...])
+        poly[tile, :] = (
+            scale * (COEF_B * gram[tile, :].astype(jnp.float32) + COEF_C * squared)
+        ).astype(jnp.bfloat16)
     for tile in tiles:
         combined = COEF_A * whole[tile, :].astype(jnp.float32) + dot_f32(poly[tile, :], whole[...])
         second[tile, :] = (inverse * combined).astype(jnp.bfloat16)
     for tile in tiles:
         gram[tile, :] = dot_transposed(second[tile, :], second[...]).astype(jnp.bfloat16)
-    own = gram[:rows, :]
+    member = lax.rem(lax.axis_index("z"), 2) * 4 + lax.axis_index("x")
+    place = pl.ds(pl.multiple_of(member * rows, 32), rows)
+    own = gram[place, :]
     own_poly = (COEF_B * own.astype(jnp.float32) + COEF_C * dot_f32(own, gram[...])).astype(
         jnp.bfloat16
     )
-    combined = COEF_A * second[:rows, :].astype(jnp.float32) + dot_f32(own_poly, second[...])
+    combined = COEF_A * second[place, :].astype(jnp.float32) + dot_f32(own_poly, second[...])
     scaled = 0.2 * math.sqrt(max(FF, D)) * combined
     for number, block in enumerate(packed_blocks(scaled[:, :HALF], scaled[:, HALF:])):
         out[number] = block.astype(jnp.bfloat16)
@@ -155,13 +147,12 @@
     out[:, :, HALF:] = jnp.swapaxes(right, 0, 1).astype(jnp.bfloat16)
 
 
-def orthogonal_rows(pieces):
+def orthogonal_rows(whole):
     return call(
         orthogonal_kernel,
-        jax.ShapeDtypeStruct(pieces.shape[1:], jnp.bfloat16),
-        pieces,
+        jax.ShapeDtypeStruct((MATS, 24, HALF), jnp.bfloat16),
+        whole,
         scratch=[
-            pltpu.VMEM((FF, D), jnp.bfloat16),
             pltpu.VMEM((FF, FF), jnp.bfloat16),
             pltpu.VMEM((FF, FF), jnp.bfloat16),
             pltpu.VMEM((FF, D), jnp.bfloat16),
@@ -177,8 +168,9 @@
 
 
 def gathered(piece):
-    copies = call(copy_kernel, jax.ShapeDtypeStruct((MATS, *piece.shape), piece.dtype), piece)
-    return exchanged(copies, ("z", "x"), BLOCKS)
+    rows = FF // MATS
+    copies = call(copy_kernel, jax.ShapeDtypeStruct((MATS, rows, D), piece.dtype), piece)
+    return exchanged(copies, ("z", "x"), BLOCKS).reshape(FF, D)
 
 
 def local(gradient, momentum):

time: 111 us -> 112 us (level)
  no operation moved by 1% of the time
where the time goes in v11:
time: 112 us; the launch traced here: 110 us
  blocking collectives  101 us (90%)
  Pallas kernels  8.36 us (7%)
    all_to_all x5, blocking collectives, exchanged(): lax.all_to_all(value, axes, split_axis=0, concat_axis=0, tiled=True, axis...  101 us
    pallas_call x6, Pallas kernels, call(): pl.pallas_call(kernel, out_shape=out_shape, in_specs=[pl.BlockSpec(memory...  8.36 us

profile of v11, /device:TPU:6, one launch (start us, length us, event | category | flops | bytes accessed | tf_op | source)
XLA Modules:
  0.0 110.0 jit_solution(18378269773415893921)
XLA Ops:
  0.6 1.3 %shard_map.41 = (f32[32,1,128]{2,1,0:T(1,128)S(1)}, f32[12,8,1024]{2,1,0:T(8,128)S(1)}, f32[12,8,1024]{2,1,0:T(8,128)S(1)}) custom-call(f32[12,8,1024]{2,1,0:T(8,128)} %bitcast.6, f32[12,8,1024]{2,1,0:T(8,128)} %bitcast.7), custom_call_target="tpu_custom_call" | custom-call | tf_op jit(solution)/shard_map/pallas_call | solution.py:36
  1.9 14.1 %all_to_all.25.parts = f32[32,1,128]{2,1,0:T(1,128)S(1)} all-to-all(f32[32,1,128]{2,1,0:T(1,128)S(1)} %get-tuple-element.7), channel_id=1, replica_groups=mesh['z'=16,'x'=4,'y'=4,'core'=2] {'x','y','core'}, dimensions={0} | all-to-all | bytes 32768 | tf_op jit(solution)/shard_map/all_to_all | solution.py:167
  16.0 26.3 %all_to_all.26.total = f32[16,1,128]{2,1,0:T(1,128)S(1)} all-to-all(f32[16,1,128]{2,1,0:T(1,128)S(1)} %shard_map.42), channel_id=1, replica_groups=mesh['z'=16,'x'=4,'y'=4,'core'=2] {'z'}, dimensions={0} | all-to-all | bytes 16384 | tf_op jit(solution)/shard_map/all_to_all | solution.py:167
  42.3 0.2 shard_map.43
  42.5 19.6 %all_to_all.27.piece = bf16[8,24,512]{2,1,0:T(8,128)(2,1)S(1)} all-to-all(bf16[8,24,512]{2,1,0:T(8,128)(2,1)S(1)} %shard_map.43), channel_id=1, replica_groups={{0,64,128,192,288,352,416,480},{32,96,160,224,256,320,384,448},{1,65,12..., dimensions={0} | all-to-all | bytes 393216 | tf_op jit(solution)/shard_map/all_to_all | solution.py:167
  62.1 0.1 shard_map.44
  62.3 21.1 %all_to_all.28 = bf16[8,96,1024]{2,1,0:T(8,128)(2,1)S(1)} all-to-all(bf16[8,96,1024]{2,1,0:T(8,128)(2,1)S(1)} %shard_map.44), channel_id=1, replica_groups={{0,8,16,24,32,40,48,56},{64,72,80,88,96,104,112,120},{128,136,144,152,1..., dimensions={0} | all-to-all | bytes 3145728 | tf_op jit(solution)/shard_map/all_to_all | solution.py:167
  83.3 5.7 %shard_map.45 = bf16[8,24,512]{2,1,0:T(8,128)(2,1)S(1)} custom-call(bf16[768,1024]{1,0:T(8,128)(2,1)S(1)} %bitcast.5), custom_call_target="tpu_custom_call" | custom-call | flops 4529848320 | bytes 1572864 | tf_op jit(solution)/shard_map/pallas_call | solution.py:36
  89.1 20.0 %all_to_all.29.arrived = bf16[8,24,512]{2,1,0:T(8,128)(2,1)S(1)} all-to-all(bf16[8,24,512]{2,1,0:T(8,128)(2,1)S(1)} %shard_map.45), channel_id=1, replica_groups={{0,64,128,192,288,352,416,480},{32,96,160,224,256,320,384,448},{1,65,12..., dimensions={0} | all-to-all | bytes 393216 | tf_op jit(solution)/shard_map/all_to_all | solution.py:167
  109.1 0.9 shard_map.46
  (1 shorter events, 0.0 us)

commit v12 on v11

--- a/solution.py
+++ b/solution.py
@@ -105,14 +105,16 @@
 
 def orthogonal_kernel(whole, out, gram, poly, second):
     rows = FF // MATS
-    tiles = [slice(start, start + TILE) for start in range(0, FF, TILE)]
+    tiles = [slice(0, FF)]
     on_diagonal = lax.broadcasted_iota(jnp.int32, (TILE, TILE), 0) == lax.broadcasted_iota(
         jnp.int32, (TILE, TILE), 1
     )
     norm_square = jnp.float32(0.0)
     for tile in tiles:
         product = dot_transposed(whole[tile, :], whole[...])
-        norm_square += jnp.sum(jnp.where(on_diagonal, product[:, tile], 0.0))
+        for start in range(0, FF, TILE):
+            corner = product[start : start + TILE, start : start + TILE]
+            norm_square += jnp.sum(jnp.where(on_diagonal, corner, 0.0))
         gram[tile, :] = product.astype(jnp.bfloat16)
     inverse = 1.0 / (jnp.sqrt(jnp.full((1, 1), norm_square, jnp.float32)) + NORM_EPS)
     scale = inverse * inverse

time: 112 us -> 112 us (level)
  no operation moved by 1% of the time
where the time goes in v12:
time: 112 us; the launch traced here: 111 us
  blocking collectives  101 us (90%)
  Pallas kernels  9.01 us (8%)
    all_to_all x5, blocking collectives, exchanged(): lax.all_to_all(value, axes, split_axis=0, concat_axis=0, tiled=True, axis...  101 us
    pallas_call x6, Pallas kernels, call(): pl.pallas_call(kernel, out_shape=out_shape, in_specs=[pl.BlockSpec(memory...  9.01 us

profile of v12, /device:TPU:6, one launch (start us, length us, event | category | flops | bytes accessed | tf_op | source)
XLA Modules:
  0.0 110.7 jit_solution(11816213684733550057)
XLA Ops:
  0.6 1.3 %shard_map.41 = (f32[32,1,128]{2,1,0:T(1,128)S(1)}, f32[12,8,1024]{2,1,0:T(8,128)S(1)}, f32[12,8,1024]{2,1,0:T(8,128)S(1)}) custom-call(f32[12,8,1024]{2,1,0:T(8,128)} %bitcast.6, f32[12,8,1024]{2,1,0:T(8,128)} %bitcast.7), custom_call_target="tpu_custom_call" | custom-call | tf_op jit(solution)/shard_map/pallas_call | solution.py:36
  1.9 14.1 %all_to_all.25.parts = f32[32,1,128]{2,1,0:T(1,128)S(1)} all-to-all(f32[32,1,128]{2,1,0:T(1,128)S(1)} %get-tuple-element.7), channel_id=1, replica_groups=mesh['z'=16,'x'=4,'y'=4,'core'=2] {'x','y','core'}, dimensions={0} | all-to-all | bytes 32768 | tf_op jit(solution)/shard_map/all_to_all | solution.py:169
  16.0 26.3 %all_to_all.26.total = f32[16,1,128]{2,1,0:T(1,128)S(1)} all-to-all(f32[16,1,128]{2,1,0:T(1,128)S(1)} %shard_map.42), channel_id=1, replica_groups=mesh['z'=16,'x'=4,'y'=4,'core'=2] {'z'}, dimensions={0} | all-to-all | bytes 16384 | tf_op jit(solution)/shard_map/all_to_all | solution.py:169
  42.3 0.2 shard_map.43
  42.5 19.6 %all_to_all.27.piece = bf16[8,24,512]{2,1,0:T(8,128)(2,1)S(1)} all-to-all(bf16[8,24,512]{2,1,0:T(8,128)(2,1)S(1)} %shard_map.43), channel_id=1, replica_groups={{0,64,128,192,288,352,416,480},{32,96,160,224,256,320,384,448},{1,65,12..., dimensions={0} | all-to-all | bytes 393216 | tf_op jit(solution)/shard_map/all_to_all | solution.py:169
  62.1 0.1 shard_map.44
  62.3 21.1 %all_to_all.28 = bf16[8,96,1024]{2,1,0:T(8,128)(2,1)S(1)} all-to-all(bf16[8,96,1024]{2,1,0:T(8,128)(2,1)S(1)} %shard_map.44), channel_id=1, replica_groups={{0,8,16,24,32,40,48,56},{64,72,80,88,96,104,112,120},{128,136,144,152,1..., dimensions={0} | all-to-all | bytes 3145728 | tf_op jit(solution)/shard_map/all_to_all | solution.py:169
  83.3 6.4 %shard_map.45 = bf16[8,24,512]{2,1,0:T(8,128)(2,1)S(1)} custom-call(bf16[768,1024]{1,0:T(8,128)(2,1)S(1)} %bitcast.5), custom_call_target="tpu_custom_call" | custom-call | flops 4529848320 | bytes 1572864 | tf_op jit(solution)/shard_map/pallas_call | solution.py:36
  89.7 20.0 %all_to_all.29.arrived = bf16[8,24,512]{2,1,0:T(8,128)(2,1)S(1)} all-to-all(bf16[8,24,512]{2,1,0:T(8,128)(2,1)S(1)} %shard_map.45), channel_id=1, replica_groups={{0,64,128,192,288,352,416,480},{32,96,160,224,256,320,384,448},{1,65,12..., dimensions={0} | all-to-all | bytes 393216 | tf_op jit(solution)/shard_map/all_to_all | solution.py:169
  109.8 0.9 shard_map.46
  (1 shorter events, 0.0 us)

commit v13 on v11

--- a/solution.py
+++ b/solution.py
@@ -111,21 +111,22 @@
     )
     norm_square = jnp.float32(0.0)
     for tile in tiles:
-        product = dot_transposed(whole[tile, :], whole[...])
-        norm_square += jnp.sum(jnp.where(on_diagonal, product[:, tile], 0.0))
-        gram[tile, :] = product.astype(jnp.bfloat16)
+        product = dot_transposed(whole[...], whole[tile, :])
+        norm_square += jnp.sum(jnp.where(on_diagonal, product[tile, :], 0.0))
+        gram[:, tile] = product.astype(jnp.bfloat16)
     inverse = 1.0 / (jnp.sqrt(jnp.full((1, 1), norm_square, jnp.float32)) + NORM_EPS)
     scale = inverse * inverse
     for tile in tiles:
-        squared = scale * dot_f32(gram[tile, :], gram[...])
-        poly[tile, :] = (
-            scale * (COEF_B * gram[tile, :].astype(jnp.float32) + COEF_C * squared)
+        squared = scale * dot_f32(gram[...], gram[:, tile])
+        poly[:, tile] = (
+            scale * (COEF_B * gram[:, tile].astype(jnp.float32) + COEF_C * squared)
         ).astype(jnp.bfloat16)
+    for start in range(0, D, TILE):
+        tile = slice(start, start + TILE)
+        combined = COEF_A * whole[:, tile].astype(jnp.float32) + dot_f32(poly[...], whole[:, tile])
+        second[:, tile] = (inverse * combined).astype(jnp.bfloat16)
     for tile in tiles:
-        combined = COEF_A * whole[tile, :].astype(jnp.float32) + dot_f32(poly[tile, :], whole[...])
-        second[tile, :] = (inverse * combined).astype(jnp.bfloat16)
-    for tile in tiles:
-        gram[tile, :] = dot_transposed(second[tile, :], second[...]).astype(jnp.bfloat16)
+        gram[:, tile] = dot_transposed(second[...], second[tile, :]).astype(jnp.bfloat16)
     member = lax.rem(lax.axis_index("z"), 2) * 4 + lax.axis_index("x")
     place = pl.ds(pl.multiple_of(member * rows, 32), rows)
     own = gram[place, :]

time: 112 us -> 112 us (level)
  no operation moved by 1% of the time
where the time goes in v13:
time: 112 us; the launch traced here: 111 us
  blocking collectives  101 us (90%)
  Pallas kernels  8.98 us (8%)
    all_to_all x5, blocking collectives, exchanged(): lax.all_to_all(value, axes, split_axis=0, concat_axis=0, tiled=True, axis...  101 us
    pallas_call x6, Pallas kernels, call(): pl.pallas_call(kernel, out_shape=out_shape, in_specs=[pl.BlockSpec(memory...  8.98 us

profile of v13, /device:TPU:6, one launch (start us, length us, event | category | flops | bytes accessed | tf_op | source)
XLA Modules:
  0.0 110.7 jit_solution(8762795757588595009)
XLA Ops:
  0.6 1.3 %shard_map.41 = (f32[32,1,128]{2,1,0:T(1,128)S(1)}, f32[12,8,1024]{2,1,0:T(8,128)S(1)}, f32[12,8,1024]{2,1,0:T(8,128)S(1)}) custom-call(f32[12,8,1024]{2,1,0:T(8,128)} %bitcast.6, f32[12,8,1024]{2,1,0:T(8,128)} %bitcast.7), custom_call_target="tpu_custom_call" | custom-call | tf_op jit(solution)/shard_map/pallas_call | solution.py:36
  1.9 14.1 %all_to_all.25.parts = f32[32,1,128]{2,1,0:T(1,128)S(1)} all-to-all(f32[32,1,128]{2,1,0:T(1,128)S(1)} %get-tuple-element.7), channel_id=1, replica_groups=mesh['z'=16,'x'=4,'y'=4,'core'=2] {'x','y','core'}, dimensions={0} | all-to-all | bytes 32768 | tf_op jit(solution)/shard_map/all_to_all | solution.py:168
  16.0 26.3 %all_to_all.26.total = f32[16,1,128]{2,1,0:T(1,128)S(1)} all-to-all(f32[16,1,128]{2,1,0:T(1,128)S(1)} %shard_map.42), channel_id=1, replica_groups=mesh['z'=16,'x'=4,'y'=4,'core'=2] {'z'}, dimensions={0} | all-to-all | bytes 16384 | tf_op jit(solution)/shard_map/all_to_all | solution.py:168
  42.3 0.2 shard_map.43
  42.5 19.6 %all_to_all.27.piece = bf16[8,24,512]{2,1,0:T(8,128)(2,1)S(1)} all-to-all(bf16[8,24,512]{2,1,0:T(8,128)(2,1)S(1)} %shard_map.43), channel_id=1, replica_groups={{0,64,128,192,288,352,416,480},{32,96,160,224,256,320,384,448},{1,65,12..., dimensions={0} | all-to-all | bytes 393216 | tf_op jit(solution)/shard_map/all_to_all | solution.py:168
  62.1 0.1 shard_map.44
  62.3 21.1 %all_to_all.28 = bf16[8,96,1024]{2,1,0:T(8,128)(2,1)S(1)} all-to-all(bf16[8,96,1024]{2,1,0:T(8,128)(2,1)S(1)} %shard_map.44), channel_id=1, replica_groups={{0,8,16,24,32,40,48,56},{64,72,80,88,96,104,112,120},{128,136,144,152,1..., dimensions={0} | all-to-all | bytes 3145728 | tf_op jit(solution)/shard_map/all_to_all | solution.py:168
  83.3 6.3 %shard_map.45 = bf16[8,24,512]{2,1,0:T(8,128)(2,1)S(1)} custom-call(bf16[768,1024]{1,0:T(8,128)(2,1)S(1)} %bitcast.5), custom_call_target="tpu_custom_call" | custom-call | flops 4529848320 | bytes 1572864 | tf_op jit(solution)/shard_map/pallas_call | solution.py:36
  89.7 20.0 %all_to_all.29.arrived = bf16[8,24,512]{2,1,0:T(8,128)(2,1)S(1)} all-to-all(bf16[8,24,512]{2,1,0:T(8,128)(2,1)S(1)} %shard_map.45), channel_id=1, replica_groups={{0,64,128,192,288,352,416,480},{32,96,160,224,256,320,384,448},{1,65,12..., dimensions={0} | all-to-all | bytes 393216 | tf_op jit(solution)/shard_map/all_to_all | solution.py:168
  109.7 0.9 shard_map.46
  (1 shorter events, 0.0 us)

commit v14 on v11

--- a/solution.py
+++ b/solution.py
@@ -11,7 +11,7 @@
 FF = 768
 MATS = 8
 HALF = D // 2
-TILE = 256
+TILE = 128
 BLOCKS = tuple(tuple(range(start, start + 8)) for start in range(0, 64, 8))
 PLANES = ((0, 2, 4, 6, 9, 11, 13, 15), (1, 3, 5, 7, 8, 10, 12, 14))
 

time: 112 us -> 115 us (1.027)
  Pallas kernels: 8.36 us -> 11.4 us
    pallas_call x6, Pallas kernels: 8.36 us -> 11.4 us  [call(): pl.pallas_call(kernel, out_shape=out_shape, in_specs=[pl.BlockSpec(memory...]
where the time goes in v14:
time: 115 us; the launch traced here: 113 us
  blocking collectives  101 us (88%)
  Pallas kernels  11.4 us (10%)
    all_to_all x5, blocking collectives, exchanged(): lax.all_to_all(value, axes, split_axis=0, concat_axis=0, tiled=True, axis...  101 us
    pallas_call x6, Pallas kernels, call(): pl.pallas_call(kernel, out_shape=out_shape, in_specs=[pl.BlockSpec(memory...  11.4 us

profile of v14, /device:TPU:6, one launch (start us, length us, event | category | flops | bytes accessed | tf_op | source)
XLA Modules:
  0.0 113.1 jit_solution(7524923169520824100)
XLA Ops:
  0.6 1.3 %shard_map.41 = (f32[32,1,128]{2,1,0:T(1,128)S(1)}, f32[12,8,1024]{2,1,0:T(8,128)S(1)}, f32[12,8,1024]{2,1,0:T(8,128)S(1)}) custom-call(f32[12,8,1024]{2,1,0:T(8,128)} %bitcast.6, f32[12,8,1024]{2,1,0:T(8,128)} %bitcast.7), custom_call_target="tpu_custom_call" | custom-call | tf_op jit(solution)/shard_map/pallas_call | solution.py:36
  1.9 14.1 %all_to_all.25.parts = f32[32,1,128]{2,1,0:T(1,128)S(1)} all-to-all(f32[32,1,128]{2,1,0:T(1,128)S(1)} %get-tuple-element.7), channel_id=1, replica_groups=mesh['z'=16,'x'=4,'y'=4,'core'=2] {'x','y','core'}, dimensions={0} | all-to-all | bytes 32768 | tf_op jit(solution)/shard_map/all_to_all | solution.py:167
  16.0 26.3 %all_to_all.26.total = f32[16,1,128]{2,1,0:T(1,128)S(1)} all-to-all(f32[16,1,128]{2,1,0:T(1,128)S(1)} %shard_map.42), channel_id=1, replica_groups=mesh['z'=16,'x'=4,'y'=4,'core'=2] {'z'}, dimensions={0} | all-to-all | bytes 16384 | tf_op jit(solution)/shard_map/all_to_all | solution.py:167
  42.3 0.2 shard_map.43
  42.5 19.6 %all_to_all.27.piece = bf16[8,24,512]{2,1,0:T(8,128)(2,1)S(1)} all-to-all(bf16[8,24,512]{2,1,0:T(8,128)(2,1)S(1)} %shard_map.43), channel_id=1, replica_groups={{0,64,128,192,288,352,416,480},{32,96,160,224,256,320,384,448},{1,65,12..., dimensions={0} | all-to-all | bytes 393216 | tf_op jit(solution)/shard_map/all_to_all | solution.py:167
  62.1 0.1 shard_map.44
  62.3 21.1 %all_to_all.28 = bf16[8,96,1024]{2,1,0:T(8,128)(2,1)S(1)} all-to-all(bf16[8,96,1024]{2,1,0:T(8,128)(2,1)S(1)} %shard_map.44), channel_id=1, replica_groups={{0,8,16,24,32,40,48,56},{64,72,80,88,96,104,112,120},{128,136,144,152,1..., dimensions={0} | all-to-all | bytes 3145728 | tf_op jit(solution)/shard_map/all_to_all | solution.py:167
  83.3 8.8 %shard_map.45 = bf16[8,24,512]{2,1,0:T(8,128)(2,1)S(1)} custom-call(bf16[768,1024]{1,0:T(8,128)(2,1)S(1)} %bitcast.5), custom_call_target="tpu_custom_call" | custom-call | flops 4529848320 | bytes 1572864 | tf_op jit(solution)/shard_map/pallas_call | solution.py:36
  92.2 20.0 %all_to_all.29.arrived = bf16[8,24,512]{2,1,0:T(8,128)(2,1)S(1)} all-to-all(bf16[8,24,512]{2,1,0:T(8,128)(2,1)S(1)} %shard_map.45), channel_id=1, replica_groups={{0,64,128,192,288,352,416,480},{32,96,160,224,256,320,384,448},{1,65,12..., dimensions={0} | all-to-all | bytes 393216 | tf_op jit(solution)/shard_map/all_to_all | solution.py:167
  112.2 0.9 shard_map.46
  (1 shorter events, 0.0 us)

commit v15 on v11

--- a/solution.py
+++ b/solution.py
@@ -179,16 +179,16 @@
     whole = jax.ShapeDtypeStruct(shape, jnp.float32)
     squares, kept, decayed = call(
         start_kernel,
-        (jax.ShapeDtypeStruct((32, 1, 128), jnp.float32), whole, whole),
+        (jax.ShapeDtypeStruct((16, 1, 128), jnp.float32), whole, whole),
         gradient,
         momentum,
         scratch=[pltpu.SemaphoreType.DMA((2,))],
         space=pl.ANY,
         limit=54272,
     )
-    squares = exchanged(squares, ("x", "y", "core"))
-    squares = call(add_kernel, jax.ShapeDtypeStruct((16, 1, 128), jnp.float32), squares)
-    squares = exchanged(squares, "z")
+    squares = exchanged(squares, ("x", "y"))
+    squares = call(add_kernel, jax.ShapeDtypeStruct((32, 1, 128), jnp.float32), squares)
+    squares = exchanged(squares, ("z", "core"))
     outgoing = call(
         blend_kernel, jax.ShapeDtypeStruct((MATS, 24, HALF), jnp.bfloat16), squares, kept, decayed
     )

time: 112 us -> 115 us (1.027)
  blocking collectives: 101 us -> 104 us
    all_to_all x5, blocking collectives: 101 us -> 104 us  [exchanged(): lax.all_to_all(value, axes, split_axis=0, concat_axis=0, tiled=True, axis...]
where the time goes in v15:
time: 115 us; the launch traced here: 113 us
  blocking collectives  104 us (90%)
  Pallas kernels  8.39 us (7%)
    all_to_all x5, blocking collectives, exchanged(): lax.all_to_all(value, axes, split_axis=0, concat_axis=0, tiled=True, axis...  104 us
    pallas_call x6, Pallas kernels, call(): pl.pallas_call(kernel, out_shape=out_shape, in_specs=[pl.BlockSpec(memory...  8.39 us

profile of v15, /device:TPU:6, one launch (start us, length us, event | category | flops | bytes accessed | tf_op | source)
XLA Modules:
  0.0 113.1 jit_solution(11009575847319275518)
XLA Ops:
  0.6 1.3 %shard_map.41 = (f32[16,1,128]{2,1,0:T(1,128)S(1)}, f32[12,8,1024]{2,1,0:T(8,128)S(1)}, f32[12,8,1024]{2,1,0:T(8,128)S(1)}) custom-call(f32[12,8,1024]{2,1,0:T(8,128)} %bitcast.6, f32[12,8,1024]{2,1,0:T(8,128)} %bitcast.7), custom_call_target="tpu_custom_call" | custom-call | tf_op jit(solution)/shard_map/pallas_call | solution.py:36
  1.9 13.9 %all_to_all.25.parts = f32[16,1,128]{2,1,0:T(1,128)S(1)} all-to-all(f32[16,1,128]{2,1,0:T(1,128)S(1)} %get-tuple-element.7), channel_id=1, replica_groups=mesh['z'=16,'x'=4,'y'=4,'core'=2] {'x','y'}, dimensions={0} | all-to-all | bytes 16384 | tf_op jit(solution)/shard_map/all_to_all | solution.py:167
  15.8 26.7 %all_to_all.26.total = f32[32,1,128]{2,1,0:T(1,128)S(1)} all-to-all(f32[32,1,128]{2,1,0:T(1,128)S(1)} %shard_map.42), channel_id=1, replica_groups=mesh['z'=16,'x'=4,'y'=4,'core'=2] {'z','core'}, dimensions={0} | all-to-all | bytes 32768 | tf_op jit(solution)/shard_map/all_to_all | solution.py:167
  42.5 0.3 shard_map.43
  42.8 20.6 %all_to_all.27.piece = bf16[8,24,512]{2,1,0:T(8,128)(2,1)S(1)} all-to-all(bf16[8,24,512]{2,1,0:T(8,128)(2,1)S(1)} %shard_map.43), channel_id=1, replica_groups={{0,64,128,192,288,352,416,480},{32,96,160,224,256,320,384,448},{1,65,12..., dimensions={0} | all-to-all | bytes 393216 | tf_op jit(solution)/shard_map/all_to_all | solution.py:167
  63.3 0.1 shard_map.44
  63.5 23.0 %all_to_all.28 = bf16[8,96,1024]{2,1,0:T(8,128)(2,1)S(1)} all-to-all(bf16[8,96,1024]{2,1,0:T(8,128)(2,1)S(1)} %shard_map.44), channel_id=1, replica_groups={{0,8,16,24,32,40,48,56},{64,72,80,88,96,104,112,120},{128,136,144,152,1..., dimensions={0} | all-to-all | bytes 3145728 | tf_op jit(solution)/shard_map/all_to_all | solution.py:167
  86.4 5.7 %shard_map.45 = bf16[8,24,512]{2,1,0:T(8,128)(2,1)S(1)} custom-call(bf16[768,1024]{1,0:T(8,128)(2,1)S(1)} %bitcast.5), custom_call_target="tpu_custom_call" | custom-call | flops 4529848320 | bytes 1572864 | tf_op jit(solution)/shard_map/pallas_call | solution.py:36
  92.2 20.0 %all_to_all.29.arrived = bf16[8,24,512]{2,1,0:T(8,128)(2,1)S(1)} all-to-all(bf16[8,24,512]{2,1,0:T(8,128)(2,1)S(1)} %shard_map.45), channel_id=1, replica_groups={{0,64,128,192,288,352,416,480},{32,96,160,224,256,320,384,448},{1,65,12..., dimensions={0} | all-to-all | bytes 393216 | tf_op jit(solution)/shard_map/all_to_all | solution.py:167
  112.2 1.0 shard_map.46
  (1 shorter events, 0.0 us)

commit v16 on v14

--- a/solution.py
+++ b/solution.py
@@ -11,7 +11,7 @@
 FF = 768
 MATS = 8
 HALF = D // 2
-TILE = 128
+TILE = 384
 BLOCKS = tuple(tuple(range(start, start + 8)) for start in range(0, 64, 8))
 PLANES = ((0, 2, 4, 6, 9, 11, 13, 15), (1, 3, 5, 7, 8, 10, 12, 14))
 

time: 115 us -> 111 us (0.965)
  Pallas kernels: 11.4 us -> 8.1 us
    pallas_call x6, Pallas kernels: 11.4 us -> 8.1 us  [call(): pl.pallas_call(kernel, out_shape=out_shape, in_specs=[pl.BlockSpec(memory...]
where the time goes in v16:
time: 111 us; the launch traced here: 110 us
  blocking collectives  101 us (91%)
  Pallas kernels  8.1 us (7%)
    all_to_all x5, blocking collectives, exchanged(): lax.all_to_all(value, axes, split_axis=0, concat_axis=0, tiled=True, axis...  101 us
    pallas_call x6, Pallas kernels, call(): pl.pallas_call(kernel, out_shape=out_shape, in_specs=[pl.BlockSpec(memory...  8.1 us

profile of v16, /device:TPU:6, one launch (start us, length us, event | category | flops | bytes accessed | tf_op | source)
XLA Modules:
  0.0 109.8 jit_solution(14787806880766274769)
XLA Ops:
  0.6 1.3 %shard_map.41 = (f32[32,1,128]{2,1,0:T(1,128)S(1)}, f32[12,8,1024]{2,1,0:T(8,128)S(1)}, f32[12,8,1024]{2,1,0:T(8,128)S(1)}) custom-call(f32[12,8,1024]{2,1,0:T(8,128)} %bitcast.6, f32[12,8,1024]{2,1,0:T(8,128)} %bitcast.7), custom_call_target="tpu_custom_call" | custom-call | tf_op jit(solution)/shard_map/pallas_call | solution.py:36
  1.9 14.1 %all_to_all.25.parts = f32[32,1,128]{2,1,0:T(1,128)S(1)} all-to-all(f32[32,1,128]{2,1,0:T(1,128)S(1)} %get-tuple-element.7), channel_id=1, replica_groups=mesh['z'=16,'x'=4,'y'=4,'core'=2] {'x','y','core'}, dimensions={0} | all-to-all | bytes 32768 | tf_op jit(solution)/shard_map/all_to_all | solution.py:167
  16.0 26.3 %all_to_all.26.total = f32[16,1,128]{2,1,0:T(1,128)S(1)} all-to-all(f32[16,1,128]{2,1,0:T(1,128)S(1)} %shard_map.42), channel_id=1, replica_groups=mesh['z'=16,'x'=4,'y'=4,'core'=2] {'z'}, dimensions={0} | all-to-all | bytes 16384 | tf_op jit(solution)/shard_map/all_to_all | solution.py:167
  42.3 0.2 shard_map.43
  42.5 19.6 %all_to_all.27.piece = bf16[8,24,512]{2,1,0:T(8,128)(2,1)S(1)} all-to-all(bf16[8,24,512]{2,1,0:T(8,128)(2,1)S(1)} %shard_map.43), channel_id=1, replica_groups={{0,64,128,192,288,352,416,480},{32,96,160,224,256,320,384,448},{1,65,12..., dimensions={0} | all-to-all | bytes 393216 | tf_op jit(solution)/shard_map/all_to_all | solution.py:167
  62.1 0.1 shard_map.44
  62.3 21.1 %all_to_all.28 = bf16[8,96,1024]{2,1,0:T(8,128)(2,1)S(1)} all-to-all(bf16[8,96,1024]{2,1,0:T(8,128)(2,1)S(1)} %shard_map.44), channel_id=1, replica_groups={{0,8,16,24,32,40,48,56},{64,72,80,88,96,104,112,120},{128,136,144,152,1..., dimensions={0} | all-to-all | bytes 3145728 | tf_op jit(solution)/shard_map/all_to_all | solution.py:167
  83.3 5.5 %shard_map.45 = bf16[8,24,512]{2,1,0:T(8,128)(2,1)S(1)} custom-call(bf16[768,1024]{1,0:T(8,128)(2,1)S(1)} %bitcast.5), custom_call_target="tpu_custom_call" | custom-call | flops 4529848320 | bytes 1572864 | tf_op jit(solution)/shard_map/pallas_call | solution.py:36
  88.8 20.0 %all_to_all.29.arrived = bf16[8,24,512]{2,1,0:T(8,128)(2,1)S(1)} all-to-all(bf16[8,24,512]{2,1,0:T(8,128)(2,1)S(1)} %shard_map.45), channel_id=1, replica_groups={{0,64,128,192,288,352,416,480},{32,96,160,224,256,320,384,448},{1,65,12..., dimensions={0} | all-to-all | bytes 393216 | tf_op jit(solution)/shard_map/all_to_all | solution.py:167
  108.8 0.9 shard_map.46
  (1 shorter events, 0.0 us)
